TPU v7x, 128 devices: a whole 4x4x4 slice. The times are simulated.
128 devices in a mesh: fsdp: 8 (over z, core), tp: 16 (over y, x).
Axes of the slice: x: 4, y: 4, z: 4, core: 2. Of those that a mesh axis runs over, the one named last changes fastest.
Arguments:
- momentum: float32 [8192, 16384], P('fsdp', 'tp'), may hold values from -60 to 60
- gradient: bfloat16 [8192, 16384], P('fsdp', 'tp'), may hold values from -60 to 60
- basis_prev: float32 [16384, 256], P('tp'), may hold values from -0.046875 to 0.046875
Outputs:
- update: bfloat16 [8192, 16384], P('fsdp', 'tp')
- new_momentum: float32 [8192, 16384], P('fsdp', 'tp')
- new_basis: float32 [16384, 256], P('tp')
All inputs are finite; a program needn't handle non-finite values.
Results may differ from a plain program's by a relative error of at most 0.0018.
Values sent between devices are 32-bit elements; how exact they have to be, the bound alone decides.
No kernel may reach another device: no remote copies, remote signals or barrier semaphores. Data moves between devices by JAX's collectives and lax.ppermute only.
A program may use at most 64 MiB of HBM per device.

v0:
```python
import math

import jax
import jax.numpy as jnp
from jax import lax
from jax.sharding import PartitionSpec as P

M = 8192
N = 16384
R = 256


momentum_keep = 0.95
epsilon_norm = 1e-06
highest = lax.Precision.HIGHEST


def matmul(left, right):
    return jnp.dot(left, right, precision=highest, preferred_element_type=jnp.float32)


def left_contract(left, right):
    return lax.dot_general(
        left, right, (((0,), (0,)), ((), ())), precision=highest, preferred_element_type=jnp.float32
    )


def orthonormal(products, gram_matrix):
    lower_factor = jnp.linalg.cholesky(gram_matrix)
    return lax.linalg.triangular_solve(
        lower_factor, products, left_side=False, lower=True, transpose_a=True
    )


def local(momentum, gradient, basis_prev):
    buffer = momentum + gradient.astype(jnp.float32)
    products = lax.psum(matmul(buffer, basis_prev), "tp")
    gram_matrix = lax.psum(matmul(products.T, products), "fsdp")
    basis = orthonormal(products, gram_matrix)
    reduced = lax.psum(left_contract(buffer, basis), "fsdp")
    squares = lax.psum(jnp.sum(reduced * reduced, axis=0), "tp")
    new_momentum = buffer - (1.0 - momentum_keep) * matmul(basis, reduced.T)
    column_norm = jnp.sqrt(squares)
    new_basis = reduced / (column_norm + epsilon_norm)
    update = (math.sqrt(M * N / R) * matmul(basis, new_basis.T)).astype(jnp.bfloat16)
    return (update, new_momentum, new_basis)


def solution(mesh):
    in_specs = (P("fsdp", "tp"), P("fsdp", "tp"), P("tp", None))
    out_specs = (P("fsdp", "tp"), P("fsdp", "tp"), P("tp", None))
    return jax.shard_map(local, mesh=mesh, in_specs=in_specs, out_specs=out_specs, check_vma=False)
```

profile of v0, /device:TPU:0, one launch (start us, length us, event | category | flops | bytes accessed | tf_op | source)
XLA Modules:
  0.0 380.9 jit_solution(3010959136852868497)
XLA Ops:
  7.2 1.2 copy-done
  8.4 6.5 %fusion.1 = f32[1024,256]{1,0:T(8,128)} fusion(f32[1024,256]{1,0:T(8,128)S(1)} %copy-done, f32[1024,1024]{1,0:T(8,128)} %param.3, bf16[1024,1024]{1,0:T(8,128)(2,1)} %param.4), kind=kOutput, calls=%fused_computation.6 | convolution fusion | flops 3223322624 | bytes 8388608 | tf_op jit(solution)/shard_map/dot_general | solution.py:19
  14.9 89.4 %all-reduce.5.cloned.1.call-done = f32[1024,256]{1,0:T(8,128)} async-done(((f32[1024,256]{1,0:T(8,128)}), f32[1024,256]{1,0:T(8,128)}) %all-reduce.5.cloned.1.call-update) | async-done | bytes 1048592 | tf_op jit(solution)/shard_map/psum | solution.py:37
  104.3 4.1 %fusion.14 = f32[256,256]{0,1:T(8,128)} fusion(f32[1024,256]{1,0:T(8,128)} %all-reduce.5.cloned.1.call-done), kind=kOutput, calls=%fused_computation.40 | convolution fusion | flops 805306368 | bytes 1310720 | tf_op jit(solution)/shard_map/dot_general | solution.py:19
  108.7 59.2 %all-reduce.7.cloned.1.call-done = f32[256,256]{0,1:T(8,128)} async-done(((f32[256,256]{0,1:T(8,128)}), f32[256,256]{0,1:T(8,128)}) %all-reduce.7.cloned.1.call-update) | async-done | bytes 262160 | tf_op jit(solution)/shard_map/psum | solution.py:38
  167.9 1.1 copy.7
  170.6 11.7 %cholesky.50 = f32[128,128]{1,0:T(8,128)S(1)} custom-call(f32[128,128]{1,0:T(8,128)S(1)} %cholesky.118), custom_call_target="Cholesky" | custom-call | tf_op jit(solution)/shard_map/jit(cholesky)/cholesky | solution.py:29
  182.4 9.8 %custom-call.14 = f32[1,128,128]{1,2,0:T(8,128)S(1)} custom-call(f32[1,128,128]{2,1,0:T(8,128)S(1)} %get-tuple-element.24), custom_call_target="InvertDiagBlocksLowerTriangular" | custom-call | tf_op jit(solution)/shard_map/jit(cholesky)/cholesky | solution.py:29
  192.2 1.0 constant_dynamic-update-slice_fusion.1
  193.3 1.1 convolution_subtract_fusion.1
  194.4 11.7 %cholesky.105 = f32[128,128]{1,0:T(8,128)S(1)} custom-call(f32[128,128]{1,0:T(8,128)S(1)} %convolution_subtract_fusion.1), custom_call_target="Cholesky" | custom-call | tf_op jit(solution)/shard_map/jit(cholesky)/cholesky | solution.py:29
  209.2 5.5 %while.1 = (s32[]{:T(128)}, f32[256,256]{1,0:T(8,128)S(1)}, s32[2,2]{1,0:T(2,128)S(1)}, f32[2,128,128]{2,1,0:T(8,128)}, s32[]{:T(128)}) while((s32[]{:T(128)}, f32[256,256]{1,0:T(8,128)S(1)}, s32[2,2]{1,0:T(2,128)S(1)}, f32[2,128,128]{2,1,0:T(8,128)}, s32[]{:T(128)}) %tuple.27), condition=%wide.while_cond, body=%wide.while_body.sunk | while | flops 2 | bytes 132705 | solution.py:30
  210.0 2.1 bitcast_dynamic-update-slice_fusion.2
  212.6 2.1 bitcast_dynamic-update-slice_fusion.2
  214.7 20.5 %custom-call.15 = f32[2,128,128]{1,2,0:T(8,128)S(1)} custom-call(f32[2,128,128]{2,1,0:T(8,128)} %get-tuple-element.10), custom_call_target="InvertDiagBlocksLowerTriangular" | custom-call | tf_op jit(solution)/shard_map/triangular_solve | solution.py:30
  235.2 1.7 fusion.2
  236.9 2.2 convolution_subtract_fusion
  240.5 9.8 %fusion = f32[1024,256]{1,0:T(8,128)} fusion(f32[1024,1024]{1,0:T(8,128)} %param.3, bf16[1024,1024]{1,0:T(8,128)(2,1)S(1)} %copy-done.2, f32[1024,128]{0,1:T(8,128)S(1)} %fusion.5, f32[1024,128]{0,1:T(8,128)S(1)} %fusion.2), kind=kOutput, calls=%fused_computation.5 | convolution fusion | flops 3223584768 | bytes 8388608 | tf_op jit(solution)/shard_map/dot_general | solution.py:23
  250.4 61.8 %all-reduce.9.cloned.1.call-done = f32[1024,256]{1,0:T(8,128)} async-done(((f32[1024,256]{1,0:T(8,128)}), f32[1024,256]{1,0:T(8,128)}) %all-reduce.9.cloned.1.call-update) | async-done | bytes 1048592 | tf_op jit(solution)/shard_map/psum | solution.py:40
  312.2 1.4 multiply_reduce_fusion
  313.6 40.3 %psum.31 = f32[256]{0:T(256)S(1)} all-reduce(f32[256]{0:T(256)S(1)} %multiply_reduce_fusion), channel_id=1, replica_groups=mesh['fsdp'=8,'tp'=16] {'tp'}, use_global_device_ids=true, to_apply=%region_8.9 | all-reduce | flops 256 | bytes 2048 | tf_op jit(solution)/shard_map/psum | solution.py:41
  353.9 1.5 broadcast_divide_fusion
  355.4 10.1 %multiply_convert_fusion = bf16[1024,1024]{1,0:T(8,128)(2,1)} fusion(f32[1024,256]{1,0:T(8,128)S(1)} %broadcast_divide_fusion, f32[1024,128]{0,1:T(8,128)} %copy-done.6, f32[1024,128]{0,1:T(8,128)} %copy-done.3), kind=kOutput, calls=%fused_computation.3 | convolution fusion | flops 3223584768 | bytes 4194304 | tf_op jit(solution)/shard_map/dot_general | solution.py:19
  365.6 8.8 %multiply_subtract_fusion = f32[1024,1024]{1,0:T(8,128)} fusion(f32[1024,256]{1,0:T(8,128)S(1)} %copy-done.5, f32[1024,1024]{1,0:T(8,128)S(1)} %copy-done.1, bf16[1024,1024]{1,0:T(8,128)(2,1)S(1)} %copy-done.2, f32[1024,128]{0,1:T(8,128)S(1)} %copy-done.7, f32[1024,128]{0,1:T(8,128)S(1)} %copy-done.4), kind=kOutput, calls=%fused_computation.2 | convolution fusion | flops 3225681920 | bytes 12582912 | tf_op jit(solution)/shard_map/dot_general | solution.py:19
  (43 shorter events, 6.6 us)
Async XLA Ops:
  7.2 1.2 copy-start
  7.2 97.2 %all-reduce.5.cloned.1.call-start = ((), (), s32[]{:S(2)}) async-start(), calls=%async_computation | async-start | bytes 2097152 | tf_op jit(solution)/shard_map/psum | solution.py:37
  14.9 153.0 %all-reduce.7.cloned.1.call-start = ((), (), s32[]{:S(2)}) async-start(), calls=%async_computation.1 | async-start | bytes 524288 | tf_op jit(solution)/shard_map/psum | solution.py:38
  108.4 132.1 %copy-start.2 = (bf16[1024,1024]{1,0:T(8,128)(2,1)S(1)}, bf16[1024,1024]{1,0:T(8,128)(2,1)}, u32[]{:S(2)}) copy-start(bf16[1024,1024]{1,0:T(8,128)(2,1)} %param.4) | copy-start | bytes 6291460
  108.4 203.8 %all-reduce.9.cloned.1.call-start = ((), (), s32[]{:S(2)}) async-start(), calls=%async_computation.2 | async-start | bytes 2097152 | tf_op jit(solution)/shard_map/psum | solution.py:40
  169.9 0.7 copy-start.10
  206.1 2.0 copy-start.9
  236.8 2.9 copy-start.3
  239.7 0.8 copy-start.6
  353.9 11.6 %copy-start.1 = (f32[1024,1024]{1,0:T(8,128)S(1)}, f32[1024,1024]{1,0:T(8,128)}, u32[]{:S(2)}) copy-start(f32[1024,1024]{1,0:T(8,128)} %param.3) | copy-start | bytes 12582916
  353.9 11.6 %copy-start.4 = (f32[1024,128]{0,1:T(8,128)S(1)}, f32[1024,128]{0,1:T(8,128)}, u32[]{:S(2)}) copy-start(f32[1024,128]{0,1:T(8,128)} %copy-done.3) | copy-start | bytes 1572868
  353.9 11.6 %copy-start.5 = (f32[1024,256]{1,0:T(8,128)S(1)}, f32[1024,256]{1,0:T(8,128)}, u32[]{:S(2)}) copy-start(f32[1024,256]{1,0:T(8,128)} %all-reduce.9.cloned.1.call-done) | copy-start | bytes 3145732
  353.9 11.6 %copy-start.7 = (f32[1024,128]{0,1:T(8,128)S(1)}, f32[1024,128]{0,1:T(8,128)}, u32[]{:S(2)}) copy-start(f32[1024,128]{0,1:T(8,128)} %copy-done.6) | copy-start | bytes 1572868
  355.4 19.0 %copy-start.8 = (f32[1024,256]{1,0:T(8,128)}, f32[1024,256]{1,0:T(8,128)S(1)}, u32[]{:S(2)}) copy-start(f32[1024,256]{1,0:T(8,128)S(1)} %broadcast_divide_fusion) | copy-start | bytes 3145732
Sparse Core Ops, SparseCore 0:
  15.0 89.3 all-reduce.4
  108.6 59.2 all-reduce.6
  250.5 61.6 all-reduce.8
where the time goes:
time: 382 us; the launch traced here: 381 us
  waiting for transfers between devices  210 us (55%)
  other arithmetic  59.3 us (16%)
  matrix products  46 us (12%)
  blocking collectives  40.3 us (11%)
  between operations  15.2 us (4%)
  local copies, waits for them, and re-layouts  9.19 us (2%)
    psum x1, waiting for transfers between devices, local(): products = lax.psum(matmul(buffer, basis_prev), 'tp')  89.4 us
    psum x1, waiting for transfers between devices, local(): reduced = lax.psum(left_contract(buffer, basis), 'fsdp')  61.8 us
    psum x1, waiting for transfers between devices, local(): gram_matrix = lax.psum(matmul(products.T, products), 'fsdp')  59.2 us
    psum x1, blocking collectives, local(): squares = lax.psum(jnp.sum(reduced * reduced, axis=0), 'tp')  40.3 us
    another operation x6, other arithmetic, orthonormal(): lower_factor = jnp.linalg.cholesky(gram_matrix)  34 us
    dot_general x4, matrix products, matmul(): jnp.dot(left, right, precision=highest, preferred_element_type=jnp.float32)  29.5 us
    another operation x3, other arithmetic, orthonormal(): lax.linalg.triangular_solve(lower_factor, products, left_side=False, lowe...  21.5 us
    dot_general x1, matrix products, left_contract(): lax.dot_general(left, right, (((0,), (0,)), ((), ())), precision=highest,...  9.85 us
  transfers between devices with their start and end apart: 3, of which 3 were waited for; matrix products, arithmetic and copies ran while one was open for 0% of the time, Pallas kernels for 0%

commit v1 on v0

v1 whole, which is shorter than its diff:
```python
import math

import jax
import jax.numpy as jnp
from jax import lax
from jax.sharding import PartitionSpec as P

M = 8192
N = 16384
R = 256


momentum_keep = 0.95
epsilon_norm = 1e-06
highest = lax.Precision.HIGHEST
both = ("fsdp", "tp")


def dot(left, right, dims, precision=highest):
    return lax.dot_general(
        left, right, (dims, ((), ())), precision=precision, preferred_element_type=jnp.float32
    )


def pairs(target):
    out = []
    for z in range(4):
        for core in range(2):
            for y in range(4):
                for x in range(4):
                    tz, tcore, ty, tx = target(z, core, y, x)
                    here = (z * 2 + core) * 16 + y * 4 + x
                    there = (tz * 2 + tcore) * 16 + ty * 4 + tx
                    out.append((here, there))
    return out


def first_axis(k):
    def target(z, core, y, x):
        return (z, core, y, (x + k) % 4) if core == 0 else (z, core, (y + k) % 4, x)

    return pairs(target)


def second_axis(k):
    def target(z, core, y, x):
        return (z, core, (y + k) % 4, x) if core == 0 else (z, core, y, (x + k) % 4)

    return pairs(target)


def along_z(k):
    return pairs(lambda z, core, y, x: ((z + k) % 4, core, y, x))


other_core = pairs(lambda z, core, y, x: (z, 1 - core, y, x))


def send(value, where):
    return lax.ppermute(value, both, where)


def chunk(value, count, index):
    rows = value.shape[0] // count
    return lax.dynamic_slice_in_dim(value, index * rows, rows, 0)


def scatter_sum(value, me, where):
    one, two, three = [send(chunk(value, 4, (me + k) % 4), where(k)) for k in (1, 2, 3)]
    return (chunk(value, 4, me) + two) + (one + three)


def exchange_sum(value, where):
    one, two, three = [send(value, where(k)) for k in (1, 2, 3)]
    return (value + two) + (one + three)


def gather(value, me, where):
    parts = [value] + [send(value, where(k)) for k in (1, 2, 3)]
    rows = value.shape[0]
    out = jnp.zeros((4 * rows,) + value.shape[1:], value.dtype)
    for k in range(4):
        out = lax.dynamic_update_slice_in_dim(out, parts[k], ((me - k) % 4) * rows, 0)
    return out


def join_cores(value, core):
    other = send(value, other_core)
    return jnp.where(
        core == 0, jnp.concatenate([value, other], 0), jnp.concatenate([other, value], 0)
    )


def local(momentum, gradient, basis_prev):
    fsdp, tp = lax.axis_index("fsdp"), lax.axis_index("tp")
    z, core, y, x = fsdp // 2, fsdp % 2, tp // 4, tp % 4
    me = jnp.where(core == 0, x, y)

    buffer = momentum + gradient.astype(jnp.float32)
    partial = dot(buffer, basis_prev, ((1,), (0,)))
    products = scatter_sum(partial, me, first_axis)
    products = exchange_sum(products, second_axis)
    products = gather(products, me, first_axis)

    gram = dot(products, products, ((0,), (0,)))
    half = chunk(gram, 2, core) + send(chunk(gram, 2, 1 - core), other_core)
    half = exchange_sum(half, along_z)
    gram_matrix = join_cores(half, core)

    crossed = dot(buffer, products, ((0,), (0,)))
    part = chunk(crossed, 2, core) + send(chunk(crossed, 2, 1 - core), other_core)
    part = scatter_sum(part, z, along_z)
    part = gather(part, z, along_z)
    crossed = join_cores(part, core)

    lower_factor = jnp.linalg.cholesky(gram_matrix)
    inverse = lax.linalg.triangular_solve(
        lower_factor, jnp.eye(R, dtype=jnp.float32), left_side=True, lower=True
    )
    basis = dot(products, inverse, ((1,), (1,)))
    reduced = dot(crossed, inverse, ((1,), (1,)))
    squares = jnp.sum(reduced * reduced, axis=0)
    everywhere = lax.all_to_all(jnp.broadcast_to(squares[None, None], (16, 1, R)), "tp", 0, 0)
    squares = jnp.sum(everywhere, axis=(0, 1))
    new_momentum = buffer - (1.0 - momentum_keep) * dot(basis, reduced, ((1,), (1,)))
    column_norm = jnp.sqrt(squares)
    new_basis = reduced / (column_norm + epsilon_norm)
    update = (math.sqrt(M * N / R) * dot(basis, new_basis, ((1,), (1,)))).astype(jnp.bfloat16)
    return (update, new_momentum, new_basis)


def solution(mesh):
    in_specs = (P("fsdp", "tp"), P("fsdp", "tp"), P("tp", None))
    out_specs = (P("fsdp", "tp"), P("fsdp", "tp"), P("tp", None))
    return jax.shard_map(local, mesh=mesh, in_specs=in_specs, out_specs=out_specs, check_vma=False)
```

time: 382 us -> 178 us (0.47)
  waiting for transfers between devices: 210 us -> 27.8 us
  starting transfers between devices: 0.3 us -> 40.6 us
  blocking collectives: 40.3 us -> 0 us
  between operations: 15.2 us -> 2.37 us
  matrix products: 46 us -> 33.9 us
    psum x3 -> x0, waiting for transfers between devices: 210 us -> none  [the longest x1 89.4 us: local(): products = lax.psum(matmul(buffer, basis_prev), 'tp')]
    psum x1 -> x0, blocking collectives: 40.3 us -> none  [local(): squares = lax.psum(jnp.sum(reduced * reduced, axis=0), 'tp')]
    ppermute x0 -> x22, starting transfers between devices: none -> 34.6 us  [send(): return lax.ppermute(value, both, where)]
    ppermute x0 -> x22, waiting for transfers between devices: none -> 27.4 us  [send(): return lax.ppermute(value, both, where)]
    dot_general x5 -> x7, matrix products: 39.3 us -> 30.2 us  [dot(): lax.dot_general(left, right, (dims, ((), ())), precision=precision, prefe...]
    all_to_all x0 -> x1, starting transfers between devices: none -> 5.98 us  [local(): lax.all_to_all(jnp.broadcast_to(squares[None, None], (16, 1, R)), 'tp', 0...]
  transfers between devices with their start and end apart: 3 -> 23, of which waited for: 3 -> 16; matrix products, arithmetic and copies ran while one was open for 0% -> 49% of each run, Pallas kernels for 0% -> 0%
where the time goes in v1:
time: 178 us; the launch traced here: 177 us
  other arithmetic  62.1 us (35%)
  starting transfers between devices  40.6 us (23%)
  matrix products  33.9 us (19%)
  waiting for transfers between devices  27.8 us (16%)
  local copies, waits for them, and re-layouts  10.5 us (6%)
  between operations  2.37 us (1%)
    another operation x6, other arithmetic, local(): lower_factor = jnp.linalg.cholesky(gram_matrix)  36.3 us
    ppermute x22, starting transfers between devices, send(): return lax.ppermute(value, both, where)  34.6 us
    dot_general x7, matrix products, dot(): lax.dot_general(left, right, (dims, ((), ())), precision=precision, prefe...  30.2 us
    ppermute x22, waiting for transfers between devices, send(): return lax.ppermute(value, both, where)  27.4 us
    another operation x3, other arithmetic, local(): lax.linalg.triangular_solve(lower_factor, jnp.eye(R, dtype=jnp.float32),...  21.5 us
    all_to_all x1, starting transfers between devices, local(): lax.all_to_all(jnp.broadcast_to(squares[None, None], (16, 1, R)), 'tp', 0...  5.98 us
    another operation x6, local copies, waits for them, and re-layouts  5.18 us
  transfers between devices with their start and end apart: 23, of which 16 were waited for; matrix products, arithmetic and copies ran while one was open for 49% of the time, Pallas kernels for 0%

profile of v1, /device:TPU:0, one launch (start us, length us, event | category | flops | bytes accessed | tf_op | source)
XLA Modules:
  0.0 177.2 jit_solution(13083056388023580013)
XLA Ops:
  1.9 5.6 %fusion.1 = f32[1024,256]{1,0:T(8,128)S(1)} fusion(f32[1024,256]{1,0:T(8,128)S(1)} %copy-done, f32[1024,1024]{1,0:T(8,128)} %param.3, bf16[1024,1024]{1,0:T(8,128)(2,1)} %param.4), kind=kOutput, calls=%fused_computation.6 | convolution fusion | flops 3223322624 | bytes 8388608 | tf_op jit(solution)/shard_map/dot_general | solution.py:20
  7.6 3.2 %collective-permute-start = (f32[256,256]{1,0:T(8,128)S(1)}, f32[256,256]{1,0:T(8,128)S(1)}, u32[]{:S(2)}, u32[]{:S(2)}) collective-permute-start(f32[256,256]{1,0:T(8,128)S(1)} %get-tuple-element.25), channel_id=1, source_target_pairs={{0,2},{1,3},{2,0},{3,1},{4,6},{5,7},{6,4},{7,5},{8,10},{9,11},{10,... | collective-permute-start | bytes 786440 | tf_op jit(solution)/shard_map/ppermute | solution.py:60
  11.3 2.6 %collective-permute-start.2 = (f32[256,256]{1,0:T(8,128)S(1)}, f32[256,256]{1,0:T(8,128)}, u32[]{:S(2)}, u32[]{:S(2)}) collective-permute-start(f32[256,256]{1,0:T(8,128)S(1)} %get-tuple-element.26), channel_id=1, source_target_pairs={{0,3},{1,0},{2,1},{3,2},{4,7},{5,4},{6,5},{7,6},{8,11},{9,8},{10,9... | collective-permute-start | bytes 786440 | tf_op jit(solution)/shard_map/ppermute | solution.py:60
  15.5 2.8 %collective-permute-done.1 = f32[256,256]{1,0:T(8,128)S(1)} collective-permute-done((f32[256,256]{1,0:T(8,128)S(1)}, f32[256,256]{1,0:T(8,128)S(1)}, u32[]{:S(2)}, u32[]{:S(2)}) %collective-permute-start.1) | collective-permute-done | bytes 262176 | tf_op jit(solution)/shard_map/ppermute | solution.py:60
  19.6 3.3 %collective-permute-start.3 = (f32[256,256]{1,0:T(8,128)S(1)}, f32[256,256]{1,0:T(8,128)S(1)}, u32[]{:S(2)}, u32[]{:S(2)}) collective-permute-start(f32[256,256]{1,0:T(8,128)S(1)} %add_add_fusion.1), channel_id=1, source_target_pairs={{0,8},{1,9},{2,10},{3,11},{4,12},{5,13},{6,14},{7,15},{8,0},{9,1},... | collective-permute-start | bytes 786440 | tf_op jit(solution)/shard_map/ppermute | solution.py:60
  23.6 2.6 %collective-permute-start.5 = (f32[256,256]{1,0:T(8,128)S(1)}, f32[256,256]{1,0:T(8,128)S(1)}, u32[]{:S(2)}, u32[]{:S(2)}) collective-permute-start(f32[256,256]{1,0:T(8,128)S(1)} %add_add_fusion.1), channel_id=1, source_target_pairs={{0,12},{1,13},{2,14},{3,15},{4,0},{5,1},{6,2},{7,3},{8,4},{9,5},{1... | collective-permute-start | bytes 786440 | tf_op jit(solution)/shard_map/ppermute | solution.py:60
  27.6 2.9 %collective-permute-done.4 = f32[256,256]{1,0:T(8,128)S(1)} collective-permute-done((f32[256,256]{1,0:T(8,128)S(1)}, f32[256,256]{1,0:T(8,128)S(1)}, u32[]{:S(2)}, u32[]{:S(2)}) %collective-permute-start.4) | collective-permute-done | bytes 262176 | tf_op jit(solution)/shard_map/ppermute | solution.py:60
  32.4 3.1 %collective-permute-start.7 = (f32[256,256]{1,0:T(8,128)S(1)}, f32[256,256]{1,0:T(8,128)S(1)}, u32[]{:S(2)}, u32[]{:S(2)}) collective-permute-start(f32[256,256]{1,0:T(8,128)S(1)} %get-tuple-element.22), channel_id=1, source_target_pairs={{0,2},{1,3},{2,0},{3,1},{4,6},{5,7},{6,4},{7,5},{8,10},{9,11},{10,... | collective-permute-start | bytes 786440 | tf_op jit(solution)/shard_map/ppermute | solution.py:60
  35.6 2.9 %collective-permute-done.6 = f32[256,256]{1,0:T(8,128)S(1)} collective-permute-done((f32[256,256]{1,0:T(8,128)S(1)}, f32[256,256]{1,0:T(8,128)S(1)}, u32[]{:S(2)}, u32[]{:S(2)}) %collective-permute-start.6) | collective-permute-done | bytes 262176 | tf_op jit(solution)/shard_map/ppermute | solution.py:60
  38.6 4.1 %collective-permute-done.7 = f32[256,256]{1,0:T(8,128)S(1)} collective-permute-done((f32[256,256]{1,0:T(8,128)S(1)}, f32[256,256]{1,0:T(8,128)S(1)}, u32[]{:S(2)}, u32[]{:S(2)}) %collective-permute-start.7) | collective-permute-done | bytes 262176 | tf_op jit(solution)/shard_map/ppermute | solution.py:60
  46.0 4.0 %collective-permute-start.10 = (f32[128,256]{0,1:T(8,128)S(1)}, f32[128,256]{0,1:T(8,128)S(1)}, u32[]{:S(2)}, u32[]{:S(2)}) collective-permute-start(f32[128,256]{0,1:T(8,128)S(1)} %dynamic-slice_add_fusion.1), channel_id=1, source_target_pairs={{0,64},{1,65},{2,66},{3,67},{4,68},{5,69},{6,70},{7,71},{8,72},{9,... | collective-permute-start | bytes 393224 | tf_op jit(solution)/shard_map/ppermute | solution.py:60
  51.0 2.2 %collective-permute-start.12 = (f32[128,256]{0,1:T(8,128)S(1)}, f32[128,256]{0,1:T(8,128)S(1)}, u32[]{:S(2)}, u32[]{:S(2)}) collective-permute-start(f32[128,256]{0,1:T(8,128)S(1)} %dynamic-slice_add_fusion.1), channel_id=1, source_target_pairs={{0,96},{1,97},{2,98},{3,99},{4,100},{5,101},{6,102},{7,103},{8,104... | collective-permute-start | bytes 393224 | tf_op jit(solution)/shard_map/ppermute | solution.py:60
  54.3 2.5 %collective-permute-done.11 = f32[128,256]{0,1:T(8,128)S(1)} collective-permute-done((f32[128,256]{0,1:T(8,128)S(1)}, f32[128,256]{0,1:T(8,128)S(1)}, u32[]{:S(2)}, u32[]{:S(2)}) %collective-permute-start.11) | collective-permute-done | bytes 131104 | tf_op jit(solution)/shard_map/ppermute | solution.py:60
  57.6 8.8 %fusion = f32[1024,256]{1,0:T(8,128)S(1)} fusion(f32[1024,256]{1,0:T(8,128)S(1)} %constant_dynamic-update-slice_fusion.5, f32[1024,1024]{1,0:T(8,128)} %param.3, bf16[1024,1024]{1,0:T(8,128)(2,1)} %param.4), kind=kOutput, calls=%fused_computation.5 | convolution fusion | flops 3223322624 | bytes 8388608 | tf_op jit(solution)/shard_map/dot_general | solution.py:20
  70.3 11.7 %cholesky.50 = f32[128,128]{1,0:T(8,128)S(1)} custom-call(f32[128,128]{1,0:T(8,128)S(1)} %cholesky.118), custom_call_target="Cholesky" | custom-call | tf_op jit(solution)/shard_map/jit(cholesky)/cholesky | solution.py:116
  82.7 10.6 %custom-call.14 = f32[1,128,128]{1,2,0:T(8,128)S(1)} custom-call(f32[1,128,128]{2,1,0:T(8,128)} %get-tuple-element.34), custom_call_target="InvertDiagBlocksLowerTriangular" | custom-call | tf_op jit(solution)/shard_map/jit(cholesky)/cholesky | solution.py:116
  96.1 12.5 %cholesky.105 = f32[128,128]{1,0:T(8,128)S(1)} custom-call(f32[128,128]{1,0:T(8,128)} %convolution_subtract_fusion.1), custom_call_target="Cholesky" | custom-call | tf_op jit(solution)/shard_map/jit(cholesky)/cholesky | solution.py:116
  113.7 2.2 %collective-permute-start.15 = (f32[128,256]{1,0:T(8,128)S(1)}, f32[128,256]{1,0:T(8,128)S(1)}, u32[]{:S(2)}, u32[]{:S(2)}) collective-permute-start(f32[128,256]{1,0:T(8,128)S(1)} %get-tuple-element.28), channel_id=1, source_target_pairs={{0,64},{1,65},{2,66},{3,67},{4,68},{5,69},{6,70},{7,71},{8,72},{9,... | collective-permute-start | bytes 393224 | tf_op jit(solution)/shard_map/ppermute | solution.py:60
  119.1 5.2 %while.1 = (s32[]{:T(128)}, f32[256,256]{1,0:T(8,128)S(1)}, s32[2,2]{1,0:T(2,128)S(1)}, f32[2,128,128]{2,1,0:T(8,128)}, s32[]{:T(128)}) while((s32[]{:T(128)}, f32[256,256]{1,0:T(8,128)S(1)}, s32[2,2]{1,0:T(2,128)S(1)}, f32[2,128,128]{2,1,0:T(8,128)}, s32[]{:T(128)}) %tuple.34), condition=%wide.while_cond, body=%wide.while_body.sunk | while | flops 2 | bytes 132705 | solution.py:117
  124.3 20.5 %custom-call.15 = f32[2,128,128]{1,2,0:T(8,128)S(1)} custom-call(f32[2,128,128]{2,1,0:T(8,128)} %get-tuple-element.10), custom_call_target="InvertDiagBlocksLowerTriangular" | custom-call | tf_op jit(solution)/shard_map/triangular_solve | solution.py:117
  149.5 5.0 %collective-permute-done.18 = f32[128,256]{1,0:T(8,128)S(1)} collective-permute-done((f32[128,256]{1,0:T(8,128)S(1)}, f32[128,256]{1,0:T(8,128)S(1)}, u32[]{:S(2)}, u32[]{:S(2)}) %collective-permute-start.18) | collective-permute-done | bytes 131104 | tf_op jit(solution)/shard_map/ppermute | solution.py:60
  158.7 6.0 %all-to-all-start = ((f32[16,1,256]{2,1,0:T(1,128)}), f32[16,1,256]{2,1,0:T(1,128)S(1)}, u32[]{:S(2)}, u32[]{:S(2)}) async-start(f32[16,1,256]{2,1,0:T(1,128)} %broadcast_in_dim.17), calls=%async_computation | async-start | bytes 32768 | tf_op jit(solution)/shard_map/all_to_all | solution.py:123
  164.7 7.2 %multiply_subtract_fusion = f32[1024,1024]{1,0:T(8,128)} fusion(f32[1024,256]{1,0:T(8,128)S(1)} %fusion.10, f32[1024,256]{1,0:T(8,128)S(1)} %get-tuple-element.38, f32[1024,1024]{1,0:T(8,128)} %param.3, bf16[1024,1024]{1,0:T(8,128)(2,1)} %param.4), kind=kOutput, calls=%fused_computation.2 | convolution fusion | flops 3225419776 | bytes 12582912 | tf_op jit(solution)/shard_map/dot_general | solution.py:20
  172.5 4.7 %multiply_convert_fusion = bf16[1024,1024]{1,0:T(8,128)(2,1)} fusion(f32[1024,256]{1,0:T(8,128)S(1)} %fusion.10, f32[1024,256]{1,0:T(8,128)S(1)} %broadcast_divide_fusion), kind=kOutput, calls=%fused_computation.3 | convolution fusion | flops 3223322624 | bytes 4194304 | tf_op jit(solution)/shard_map/dot_general | solution.py:20
  (90 shorter events, 43.7 us)
Async XLA Ops:
  7.6 8.0 %collective-permute-start = (f32[256,256]{1,0:T(8,128)S(1)}, f32[256,256]{1,0:T(8,128)S(1)}, u32[]{:S(2)}, u32[]{:S(2)}) collective-permute-start(f32[256,256]{1,0:T(8,128)S(1)} %get-tuple-element.25), channel_id=1, source_target_pairs={{0,2},{1,3},{2,0},{3,1},{4,6},{5,7},{6,4},{7,5},{8,10},{9,11},{10,... | collective-permute-start | bytes 786440 | tf_op jit(solution)/shard_map/ppermute | solution.py:60
  10.8 7.6 %collective-permute-start.1 = (f32[256,256]{1,0:T(8,128)S(1)}, f32[256,256]{1,0:T(8,128)S(1)}, u32[]{:S(2)}, u32[]{:S(2)}) collective-permute-start(f32[256,256]{1,0:T(8,128)S(1)} %get-tuple-element.27), channel_id=1, source_target_pairs={{0,1},{1,2},{2,3},{3,0},{4,5},{5,6},{6,7},{7,4},{8,9},{9,10},{10,1... | collective-permute-start | bytes 786440 | tf_op jit(solution)/shard_map/ppermute | solution.py:60
  11.3 7.3 %collective-permute-start.2 = (f32[256,256]{1,0:T(8,128)S(1)}, f32[256,256]{1,0:T(8,128)}, u32[]{:S(2)}, u32[]{:S(2)}) collective-permute-start(f32[256,256]{1,0:T(8,128)S(1)} %get-tuple-element.26), channel_id=1, source_target_pairs={{0,3},{1,0},{2,1},{3,2},{4,7},{5,4},{6,5},{7,6},{8,11},{9,8},{10,9... | collective-permute-start | bytes 786440 | tf_op jit(solution)/shard_map/ppermute | solution.py:60
  19.6 8.0 %collective-permute-start.3 = (f32[256,256]{1,0:T(8,128)S(1)}, f32[256,256]{1,0:T(8,128)S(1)}, u32[]{:S(2)}, u32[]{:S(2)}) collective-permute-start(f32[256,256]{1,0:T(8,128)S(1)} %add_add_fusion.1), channel_id=1, source_target_pairs={{0,8},{1,9},{2,10},{3,11},{4,12},{5,13},{6,14},{7,15},{8,0},{9,1},... | collective-permute-start | bytes 786440 | tf_op jit(solution)/shard_map/ppermute | solution.py:60
  22.9 7.6 %collective-permute-start.4 = (f32[256,256]{1,0:T(8,128)S(1)}, f32[256,256]{1,0:T(8,128)S(1)}, u32[]{:S(2)}, u32[]{:S(2)}) collective-permute-start(f32[256,256]{1,0:T(8,128)S(1)} %add_add_fusion.1), channel_id=1, source_target_pairs={{0,4},{1,5},{2,6},{3,7},{4,8},{5,9},{6,10},{7,11},{8,12},{9,13},{1... | collective-permute-start | bytes 786440 | tf_op jit(solution)/shard_map/ppermute | solution.py:60
  23.6 7.2 %collective-permute-start.5 = (f32[256,256]{1,0:T(8,128)S(1)}, f32[256,256]{1,0:T(8,128)S(1)}, u32[]{:S(2)}, u32[]{:S(2)}) collective-permute-start(f32[256,256]{1,0:T(8,128)S(1)} %add_add_fusion.1), channel_id=1, source_target_pairs={{0,12},{1,13},{2,14},{3,15},{4,0},{5,1},{6,2},{7,3},{8,4},{9,5},{1... | collective-permute-start | bytes 786440 | tf_op jit(solution)/shard_map/ppermute | solution.py:60
  30.9 7.7 %collective-permute-start.6 = (f32[256,256]{1,0:T(8,128)S(1)}, f32[256,256]{1,0:T(8,128)S(1)}, u32[]{:S(2)}, u32[]{:S(2)}) collective-permute-start(f32[256,256]{1,0:T(8,128)S(1)} %get-tuple-element.22), channel_id=1, source_target_pairs={{0,1},{1,2},{2,3},{3,0},{4,5},{5,6},{6,7},{7,4},{8,9},{9,10},{10,1... | collective-permute-start | bytes 786440 | tf_op jit(solution)/shard_map/ppermute | solution.py:60
  32.4 10.3 %collective-permute-start.7 = (f32[256,256]{1,0:T(8,128)S(1)}, f32[256,256]{1,0:T(8,128)S(1)}, u32[]{:S(2)}, u32[]{:S(2)}) collective-permute-start(f32[256,256]{1,0:T(8,128)S(1)} %get-tuple-element.22), channel_id=1, source_target_pairs={{0,2},{1,3},{2,0},{3,1},{4,6},{5,7},{6,4},{7,5},{8,10},{9,11},{10,... | collective-permute-start | bytes 786440 | tf_op jit(solution)/shard_map/ppermute | solution.py:60
  35.5 7.2 %collective-permute-start.8 = (f32[256,256]{1,0:T(8,128)S(1)}, f32[256,256]{1,0:T(8,128)S(1)}, u32[]{:S(2)}, u32[]{:S(2)}) collective-permute-start(f32[256,256]{1,0:T(8,128)S(1)} %get-tuple-element.22), channel_id=1, source_target_pairs={{0,3},{1,0},{2,1},{3,2},{4,7},{5,4},{6,5},{7,6},{8,11},{9,8},{10,9... | collective-permute-start | bytes 786440 | tf_op jit(solution)/shard_map/ppermute | solution.py:60
  44.6 1.4 collective-permute-start.9
  46.0 8.2 %collective-permute-start.10 = (f32[128,256]{0,1:T(8,128)S(1)}, f32[128,256]{0,1:T(8,128)S(1)}, u32[]{:S(2)}, u32[]{:S(2)}) collective-permute-start(f32[128,256]{0,1:T(8,128)S(1)} %dynamic-slice_add_fusion.1), channel_id=1, source_target_pairs={{0,64},{1,65},{2,66},{3,67},{4,68},{5,69},{6,70},{7,71},{8,72},{9,... | collective-permute-start | bytes 393224 | tf_op jit(solution)/shard_map/ppermute | solution.py:60
  50.0 6.8 %collective-permute-start.11 = (f32[128,256]{0,1:T(8,128)S(1)}, f32[128,256]{0,1:T(8,128)S(1)}, u32[]{:S(2)}, u32[]{:S(2)}) collective-permute-start(f32[128,256]{0,1:T(8,128)S(1)} %dynamic-slice_add_fusion.1), channel_id=1, source_target_pairs={{0,32},{1,33},{2,34},{3,35},{4,36},{5,37},{6,38},{7,39},{8,40},{9,... | collective-permute-start | bytes 393224 | tf_op jit(solution)/shard_map/ppermute | solution.py:60
  51.0 6.3 %collective-permute-start.12 = (f32[128,256]{0,1:T(8,128)S(1)}, f32[128,256]{0,1:T(8,128)S(1)}, u32[]{:S(2)}, u32[]{:S(2)}) collective-permute-start(f32[128,256]{0,1:T(8,128)S(1)} %dynamic-slice_add_fusion.1), channel_id=1, source_target_pairs={{0,96},{1,97},{2,98},{3,99},{4,100},{5,101},{6,102},{7,103},{8,104... | collective-permute-start | bytes 393224 | tf_op jit(solution)/shard_map/ppermute | solution.py:60
  57.4 10.4 %collective-permute-start.13 = (f32[128,256]{0,1:T(8,128)S(1)}, f32[128,256]{0,1:T(8,128)S(1)}, u32[]{:S(2)}, u32[]{:S(2)}) collective-permute-start(f32[128,256]{0,1:T(8,128)S(1)} %add_add_fusion.3), channel_id=1, source_target_pairs={{0,16},{1,17},{2,18},{3,19},{4,20},{5,21},{6,22},{7,23},{8,24},{9,... | collective-permute-start | bytes 393224 | tf_op jit(solution)/shard_map/ppermute | solution.py:60
  67.3 44.4 %collective-permute-start.14 = (f32[512,256]{1,0:T(8,128)}, f32[512,256]{1,0:T(8,128)}, u32[]{:S(2)}, u32[]{:S(2)}) collective-permute-start(f32[512,256]{1,0:T(8,128)} %constant_dynamic-slice_fusion.4), channel_id=1, source_target_pairs={{0,16},{1,17},{2,18},{3,19},{4,20},{5,21},{6,22},{7,23},{8,24},{9,... | collective-permute-start | bytes 1572872 | tf_op jit(solution)/shard_map/ppermute | solution.py:60
  113.7 31.1 %collective-permute-start.15 = (f32[128,256]{1,0:T(8,128)S(1)}, f32[128,256]{1,0:T(8,128)S(1)}, u32[]{:S(2)}, u32[]{:S(2)}) collective-permute-start(f32[128,256]{1,0:T(8,128)S(1)} %get-tuple-element.28), channel_id=1, source_target_pairs={{0,64},{1,65},{2,66},{3,67},{4,68},{5,69},{6,70},{7,71},{8,72},{9,... | collective-permute-start | bytes 393224 | tf_op jit(solution)/shard_map/ppermute | solution.py:60
  115.8 29.0 %collective-permute-start.16 = (f32[128,256]{1,0:T(8,128)S(1)}, f32[128,256]{1,0:T(8,128)S(1)}, u32[]{:S(2)}, u32[]{:S(2)}) collective-permute-start(f32[128,256]{1,0:T(8,128)S(1)} %get-tuple-element.30), channel_id=1, source_target_pairs={{0,32},{1,33},{2,34},{3,35},{4,36},{5,37},{6,38},{7,39},{8,40},{9,... | collective-permute-start | bytes 393224 | tf_op jit(solution)/shard_map/ppermute | solution.py:60
  117.4 27.5 %collective-permute-start.17 = (f32[128,256]{1,0:T(8,128)S(1)}, f32[128,256]{1,0:T(8,128)S(1)}, u32[]{:S(2)}, u32[]{:S(2)}) collective-permute-start(f32[128,256]{1,0:T(8,128)S(1)} %get-tuple-element.29), channel_id=1, source_target_pairs={{0,96},{1,97},{2,98},{3,99},{4,100},{5,101},{6,102},{7,103},{8,104... | collective-permute-start | bytes 393224 | tf_op jit(solution)/shard_map/ppermute | solution.py:60
  145.8 8.7 %collective-permute-start.18 = (f32[128,256]{1,0:T(8,128)S(1)}, f32[128,256]{1,0:T(8,128)S(1)}, u32[]{:S(2)}, u32[]{:S(2)}) collective-permute-start(f32[128,256]{1,0:T(8,128)S(1)} %get-tuple-element.20), channel_id=1, source_target_pairs={{0,32},{1,33},{2,34},{3,35},{4,36},{5,37},{6,38},{7,39},{8,40},{9,... | collective-permute-start | bytes 393224 | tf_op jit(solution)/shard_map/ppermute | solution.py:60
  146.2 8.3 %collective-permute-start.19 = (f32[128,256]{1,0:T(8,128)S(1)}, f32[128,256]{1,0:T(8,128)S(1)}, u32[]{:S(2)}, u32[]{:S(2)}) collective-permute-start(f32[128,256]{1,0:T(8,128)S(1)} %get-tuple-element.20), channel_id=1, source_target_pairs={{0,64},{1,65},{2,66},{3,67},{4,68},{5,69},{6,70},{7,71},{8,72},{9,... | collective-permute-start | bytes 393224 | tf_op jit(solution)/shard_map/ppermute | solution.py:60
  148.1 7.0 %collective-permute-start.20 = (f32[128,256]{1,0:T(8,128)S(1)}, f32[128,256]{1,0:T(8,128)S(1)}, u32[]{:S(2)}, u32[]{:S(2)}) collective-permute-start(f32[128,256]{1,0:T(8,128)S(1)} %get-tuple-element.20), channel_id=1, source_target_pairs={{0,96},{1,97},{2,98},{3,99},{4,100},{5,101},{6,102},{7,103},{8,104... | collective-permute-start | bytes 393224 | tf_op jit(solution)/shard_map/ppermute | solution.py:60
  155.1 2.0 %collective-permute-start.21 = (f32[512,256]{1,0:T(8,128)S(1)}, f32[512,256]{1,0:T(8,128)S(1)}, u32[]{:S(2)}, u32[]{:S(2)}) collective-permute-start(f32[512,256]{1,0:T(8,128)S(1)} %constant_dynamic-update-slice_fusion), channel_id=1, source_target_pairs={{0,16},{1,17},{2,18},{3,19},{4,20},{5,21},{6,22},{7,23},{8,24},{9,... | collective-permute-start | bytes 1572872 | tf_op jit(solution)/shard_map/ppermute | solution.py:60
  158.7 13.6 %all-to-all-start = ((f32[16,1,256]{2,1,0:T(1,128)}), f32[16,1,256]{2,1,0:T(1,128)S(1)}, u32[]{:S(2)}, u32[]{:S(2)}) async-start(f32[16,1,256]{2,1,0:T(1,128)} %broadcast_in_dim.17), calls=%async_computation | async-start | bytes 32768 | tf_op jit(solution)/shard_map/all_to_all | solution.py:123
  172.5 4.7 %copy-start.1 = (f32[1024,256]{1,0:T(8,128)}, f32[1024,256]{1,0:T(8,128)S(1)}, u32[]{:S(2)}) copy-start(f32[1024,256]{1,0:T(8,128)S(1)} %broadcast_divide_fusion) | copy-start | bytes 3145732
  (4 other events, 4.7 us)

commit v2 on v1

v2 whole, which is shorter than its diff:
```python
import math

import jax
import jax.numpy as jnp
from jax import lax
from jax.experimental import pallas as pl
from jax.experimental.pallas import tpu as pltpu
from jax.sharding import PartitionSpec as P

M = 8192
N = 16384
R = 256
BLOCK = 1024
TILE = 128


momentum_keep = 0.95
epsilon_norm = 1e-06
highest = lax.Precision.HIGHEST
both = ("fsdp", "tp")
f32, bf16 = jnp.float32, jnp.bfloat16


def pairs(target):
    out = []
    for z in range(4):
        for core in range(2):
            for y in range(4):
                for x in range(4):
                    tz, tcore, ty, tx = target(z, core, y, x)
                    here = (z * 2 + core) * 16 + y * 4 + x
                    there = (tz * 2 + tcore) * 16 + ty * 4 + tx
                    out.append((here, there))
    return out


def first_axis(k):
    def target(z, core, y, x):
        return (z, core, y, (x + k) % 4) if core == 0 else (z, core, (y + k) % 4, x)

    return pairs(target)


def second_axis(k):
    def target(z, core, y, x):
        return (z, core, (y + k) % 4, x) if core == 0 else (z, core, y, (x + k) % 4)

    return pairs(target)


def along_z(k):
    return pairs(lambda z, core, y, x: ((z + k) % 4, core, y, x))


other_core = pairs(lambda z, core, y, x: (z, 1 - core, y, x))


def send(value, where):
    return lax.ppermute(value, both, where)


def chunk(value, count, index):
    rows = value.shape[0] // count
    return lax.dynamic_slice_in_dim(value, index * rows, rows, 0)


def scatter_sum(value, me, where):
    two, one, three = [send(chunk(value, 4, (me + k) % 4), where(k)) for k in (2, 1, 3)]
    return (chunk(value, 4, me) + two) + (one + three)


def exchange_sum(value, where):
    two, one, three = [send(value, where(k)) for k in (2, 1, 3)]
    return (value + two) + (one + three)


def gather_parts(value, where):
    two, one, three = [send(value, where(k)) for k in (2, 1, 3)]
    return [value, one, two, three]


def assemble(parts, me):
    rows = parts[0].shape[0]
    out = jnp.zeros((4 * rows,) + parts[0].shape[1:], parts[0].dtype)
    for k in range(4):
        out = lax.dynamic_update_slice_in_dim(out, parts[k], ((me - k) % 4) * rows, 0)
    return out


def join_cores(value, core):
    other = send(value, other_core)
    return jnp.where(
        core == 0, jnp.concatenate([value, other], 0), jnp.concatenate([other, value], 0)
    )


def pieces(value, count):
    out = []
    for n in range(count):
        part = value.astype(bf16)
        out.append(part)
        if n < count - 1:
            value = value - part.astype(f32)
    return out


def dot(left, right, dims=((1,), (0,)), precision=None):
    return lax.dot_general(
        left, right, (dims, ((), ())), precision=precision, preferred_element_type=f32
    )


def piece_dot(left, right, dims=((1,), (0,))):
    count = len(left)
    total = None
    for rank in range(count - 1, -1, -1):
        for n in range(rank + 1):
            term = dot(left[n], right[rank - n], dims)
            total = term if total is None else total + term
    return total


def params():
    return pltpu.CompilerParams(vmem_limit_bytes=40 * 2**20)


def vmem():
    return pl.BlockSpec(memory_space=pltpu.VMEM)


PASSES = 3


def products_kernel(momentum, gradient, basis, out, held):
    @pl.when(pl.program_id(0) == 0)
    def _():
        for n, part in enumerate(pieces(basis[...], PASSES)):
            held[n] = part

    buffer = momentum[...] + gradient[...].astype(f32)
    out[...] = piece_dot(pieces(buffer, PASSES), [held[n] for n in range(PASSES)])


def partial_products(momentum, gradient, basis):
    rows = lambda i: (i, 0)
    return pl.pallas_call(
        products_kernel,
        grid=(BLOCK // TILE,),
        in_specs=[
            pl.BlockSpec((TILE, BLOCK), rows),
            pl.BlockSpec((TILE, BLOCK), rows),
            pl.BlockSpec((BLOCK, R), lambda i: (0, 0)),
        ],
        out_specs=pl.BlockSpec((TILE, R), rows),
        out_shape=jax.ShapeDtypeStruct((BLOCK, R), f32),
        scratch_shapes=[pltpu.VMEM((PASSES, BLOCK, R), bf16)],
        compiler_params=params(),
        cost_estimate=pl.CostEstimate(flops=2 * BLOCK * BLOCK * R * 6, bytes_accessed=8 * 2**20, transcendentals=0),
        name="products",
    )(momentum, gradient, basis)


def crossed_kernel(first, index, momentum, gradient, part, *refs):
    if first:
        cross, gram, held = refs
    else:
        cross_in, gram_in, cross, gram, held = refs

    @pl.when(pl.program_id(0) == 0)
    def _():
        turned = pieces(part[...].T, 3)
        for n in range(3):
            held[n] = turned[n]
        own = piece_dot(turned, pieces(part[...], 3))
        gram[...] = own if first else gram_in[...] + own

    buffer = momentum[...] + gradient[...].astype(f32)
    share = piece_dot([held[n] for n in range(PASSES)], pieces(buffer, PASSES))
    cross[...] = share if first else cross_in[...] + share


def crossed_share(index, momentum, gradient, part, before=None):
    rows = part.shape[0]
    width = 512
    first = before is None
    spot = lambda j, s: (s[0], j)
    whole = lambda j, s: (0, 0)
    column = lambda j, s: (0, j)
    sums = [pl.BlockSpec((R, width), column), pl.BlockSpec((R, R), whole)]
    return pl.pallas_call(
        lambda *refs: crossed_kernel(first, *refs),
        grid_spec=pltpu.PrefetchScalarGridSpec(
            num_scalar_prefetch=1,
            grid=(BLOCK // width,),
            in_specs=[
                pl.BlockSpec((rows, width), spot),
                pl.BlockSpec((rows, width), spot),
                pl.BlockSpec((rows, R), whole),
            ]
            + ([] if first else sums),
            out_specs=sums,
            scratch_shapes=[pltpu.VMEM((3, R, rows), bf16)],
        ),
        out_shape=[jax.ShapeDtypeStruct((R, BLOCK), f32), jax.ShapeDtypeStruct((R, R), f32)],
        input_output_aliases={} if first else {4: 0, 5: 1},
        compiler_params=params(),
        cost_estimate=pl.CostEstimate(flops=2 * rows * (BLOCK + R) * R * 6, bytes_accessed=4 * 2**20, transcendentals=0),
        name="crossed",
    )(index, momentum, gradient, part, *([] if first else before))


B = 64
GROUP = 8


def block_inverse(block):
    tiles, width = B // 8, 2 * B
    lane = lax.broadcasted_iota(jnp.int32, (8, width), 1)
    sub = lax.broadcasted_iota(jnp.int32, (8, width), 0)
    wide = jnp.concatenate([block, jnp.zeros_like(block)], axis=1)
    a = [wide[8 * t : 8 * t + 8] + (lane == sub + 8 * t + B).astype(f32) for t in range(tiles)]
    for start in range(0, B, GROUP):
        top = start // 8
        left = tiles - top
        columns = [
            [
                jnp.broadcast_to(a[t][:, start + c : start + c + 1], (8, width))
                for t in range(top, tiles)
            ]
            for c in range(GROUP)
        ]
        for c in range(GROUP):
            r = c
            pivot = jnp.broadcast_to(columns[c][0][r : r + 1, :], (8, width))
            scale = 1.0 / pivot
            factor = [columns[c][t] * scale for t in range(left)]
            factor[0] = jnp.where(sub > r, factor[0], 0.0)
            for later in range(c + 1, GROUP):
                value = jnp.broadcast_to(columns[later][0][r : r + 1, :], (8, width))
                for t in range(left):
                    columns[later][t] = columns[later][t] - factor[t] * value
            row = jnp.broadcast_to(a[top][r : r + 1, :], (8, width))
            for t in range(left):
                a[top + t] = a[top + t] - factor[t] * row
    out = []
    for t in range(tiles):
        pivots = jnp.sum(jnp.where(lane == sub + 8 * t, a[t], 0.0), axis=1, keepdims=True)
        out.append(a[t][:, B:] * lax.rsqrt(pivots))
    return jnp.concatenate(out, 0)


def inverse_kernel(gram, after, out, work):
    row = lax.broadcasted_iota(jnp.int32, (R, R), 0)
    column = lax.broadcasted_iota(jnp.int32, (R, R), 1)
    work[:, :R] = gram[...]
    work[:, R:] = (row == column).astype(f32)
    for n in range(R // B):
        low, high = n * B, n * B + B
        inverse = block_inverse(work[low:high, low:high])
        rows = dot(inverse, work[low:high, :], precision=highest)
        out[low:high, :] = rows[:, R:]
        if high < R:
            work[high:, :] = work[high:, :] - dot(
                rows[:, high:R], rows, ((0,), (0,)), precision=highest
            )


def inverse_factor(gram, after):
    return pl.pallas_call(
        inverse_kernel,
        in_specs=[vmem(), pl.BlockSpec(memory_space=pl.ANY)],
        out_specs=vmem(),
        out_shape=jax.ShapeDtypeStruct((R, R), f32),
        scratch_shapes=[pltpu.VMEM((R, 2 * R), f32)],
        compiler_params=params(),
        cost_estimate=pl.CostEstimate(flops=10 * 10**9, bytes_accessed=2**20, transcendentals=0),
        name="inverse",
    )(gram, after)


def basis_kernel(products, inverse, basis):
    basis[...] = dot(products[...], inverse[...], ((1,), (1,)), precision=highest)


def reduced_kernel(crossed, inverse, reduced, high, low, squares):
    value = dot(inverse[...], crossed[...], precision=highest)
    reduced[...] = value
    high[...], low[...] = pieces(value, 2)
    squares[...] = dot(jnp.ones((8, BLOCK), f32), value * value, ((1,), (1,)), precision=highest)


def form_basis(products, inverse):
    return pl.pallas_call(
        basis_kernel,
        in_specs=[vmem()] * 2,
        out_specs=vmem(),
        out_shape=jax.ShapeDtypeStruct((BLOCK, R), f32),
        compiler_params=params(),
        cost_estimate=pl.CostEstimate(flops=2 * BLOCK * R * R * 6, bytes_accessed=3 * 2**20, transcendentals=0),
        name="basis",
    )(products, inverse)


def form_reduced(crossed, inverse):
    return pl.pallas_call(
        reduced_kernel,
        in_specs=[vmem()] * 2,
        out_specs=[vmem()] * 4,
        out_shape=[
            jax.ShapeDtypeStruct((R, BLOCK), f32),
            jax.ShapeDtypeStruct((R, BLOCK), bf16),
            jax.ShapeDtypeStruct((R, BLOCK), bf16),
            jax.ShapeDtypeStruct((8, R), f32),
        ],
        compiler_params=params(),
        cost_estimate=pl.CostEstimate(flops=2 * BLOCK * R * R * 6, bytes_accessed=3 * 2**20, transcendentals=0),
        name="reduced",
    )(crossed, inverse)


def momentum_kernel(momentum, gradient, basis, high, low, out):
    buffer = momentum[...] + gradient[...].astype(f32)
    product = piece_dot(pieces(basis[...], 2), [high[...], low[...]])
    out[...] = buffer - (1.0 - momentum_keep) * product


def form_momentum(momentum, gradient, basis, high, low):
    rows = lambda i: (i, 0)
    whole = lambda i: (0, 0)
    return pl.pallas_call(
        momentum_kernel,
        grid=(BLOCK // TILE,),
        in_specs=[
            pl.BlockSpec((TILE, BLOCK), rows),
            pl.BlockSpec((TILE, BLOCK), rows),
            pl.BlockSpec((TILE, R), rows),
            pl.BlockSpec((R, BLOCK), whole),
            pl.BlockSpec((R, BLOCK), whole),
        ],
        out_specs=pl.BlockSpec((TILE, BLOCK), rows),
        out_shape=jax.ShapeDtypeStruct((BLOCK, BLOCK), f32),
        compiler_params=params(),
        cost_estimate=pl.CostEstimate(flops=2 * BLOCK * BLOCK * R * 6, bytes_accessed=12 * 2**20, transcendentals=0),
        name="momentum",
    )(momentum, gradient, basis, high, low)


def update_kernel(squares, basis, reduced, high, low, update, new_basis):
    norm = jnp.sqrt(jnp.sum(squares[...], axis=0, keepdims=True)) + epsilon_norm
    new_basis[...] = reduced[...].T / norm
    scaled = basis[...] * (math.sqrt(M * N / R) / norm)
    update[...] = piece_dot(pieces(scaled, 2), [high[...], low[...]]).astype(bf16)


def form_update(squares, basis, reduced, high, low):
    rows = lambda i: (i, 0)
    whole = lambda i: (0, 0)
    return pl.pallas_call(
        update_kernel,
        grid=(BLOCK // TILE,),
        in_specs=[
            pl.BlockSpec((16, R), whole),
            pl.BlockSpec((TILE, R), rows),
            pl.BlockSpec((R, TILE), lambda i: (0, i)),
            pl.BlockSpec((R, BLOCK), whole),
            pl.BlockSpec((R, BLOCK), whole),
        ],
        out_specs=[pl.BlockSpec((TILE, BLOCK), rows), pl.BlockSpec((TILE, R), rows)],
        out_shape=[
            jax.ShapeDtypeStruct((BLOCK, BLOCK), bf16),
            jax.ShapeDtypeStruct((BLOCK, R), f32),
        ],
        compiler_params=params(),
        cost_estimate=pl.CostEstimate(flops=2 * BLOCK * BLOCK * R * 6, bytes_accessed=6 * 2**20, transcendentals=0),
        name="update",
    )(squares, basis, reduced, high, low)


def local(momentum, gradient, basis_prev):
    fsdp, tp = lax.axis_index("fsdp"), lax.axis_index("tp")
    z, core, y, x = fsdp // 2, fsdp % 2, tp // 4, tp % 4
    me = jnp.where(core == 0, x, y)

    partial = partial_products(momentum, gradient, basis_prev)
    quarter = scatter_sum(partial, me, first_axis)
    quarter = exchange_sum(quarter, second_axis)
    parts = gather_parts(quarter, first_axis)

    sums = None
    for k in (0, 1, 3, 2):
        index = ((me - k) % 4).astype(jnp.int32).reshape(1)
        sums = crossed_share(index, momentum, gradient, parts[k], sums)
    crossed, gram = sums
    products = assemble(parts, me)

    half = chunk(gram, 2, core) + send(chunk(gram, 2, 1 - core), other_core)
    half = exchange_sum(half, along_z)
    gram = join_cores(half, core)

    part = chunk(crossed, 2, core) + send(chunk(crossed, 2, 1 - core), other_core)
    part = scatter_sum(part, z, along_z)
    inverse = inverse_factor(gram, part)
    part = assemble(gather_parts(part, along_z), z)
    crossed = join_cores(part, core)

    basis = form_basis(products, inverse)
    reduced, high, low, squares = form_reduced(crossed, inverse)
    spread = jnp.broadcast_to(squares[None, :1], (16, 1, R))
    squares = lax.all_to_all(spread, "tp", 0, 0).reshape(16, R)
    new_momentum = form_momentum(momentum, gradient, basis, high, low)
    update, new_basis = form_update(squares, basis, reduced, high, low)
    return (update, new_momentum, new_basis)


def solution(mesh):
    in_specs = (P("fsdp", "tp"), P("fsdp", "tp"), P("tp", None))
    out_specs = (P("fsdp", "tp"), P("fsdp", "tp"), P("tp", None))
    return jax.shard_map(local, mesh=mesh, in_specs=in_specs, out_specs=out_specs, check_vma=False)
```

time: 178 us -> 126 us (0.71)
  other arithmetic: 62.1 us -> 1.52 us
  Pallas kernels: 0 us -> 36.2 us
  matrix products: 33.9 us -> 0 us
  local copies, waits for them, and re-layouts: 10.5 us -> 20.1 us
  starting transfers between devices: 40.6 us -> 34.8 us
  waiting for transfers between devices: 27.8 us -> 30.2 us
    another operation x9 -> x0, other arithmetic: 57.7 us -> none  [the longest x6 36.3 us: local(): lower_factor = jnp.linalg.cholesky(gram_matrix)]
    pallas_call x0 -> x10, Pallas kernels: none -> 36.2 us  [the longest x1 9.87 us: inverse_factor(): pl.pallas_call(inverse_kernel, in_specs=[vmem(), pl.BlockSpec(memory_spac...]
    dot_general x7 -> x0, matrix products: 30.2 us -> none  [dot(): lax.dot_general(left, right, (dims, ((), ())), precision=precision, prefe...]
    unnamed x10 -> x33, local copies, waits for them, and re-layouts: 2.62 us -> 18.3 us
    another operation x9 -> x0, local copies, waits for them, and re-layouts: 5.28 us -> none
    ppermute x22, starting transfers between devices: 34.6 us -> 30 us  [send(): return lax.ppermute(value, both, where)]
    another operation x5 -> x0, matrix products: 3.61 us -> none  [the longest x2 2.78 us: local(): lower_factor = jnp.linalg.cholesky(gram_matrix)]
    ppermute x22, waiting for transfers between devices: 27.4 us -> 30.2 us  [send(): return lax.ppermute(value, both, where)]
  transfers between devices with their start and end apart: 23 -> 23, of which waited for: 16 -> 10; matrix products, arithmetic and copies ran while one was open for 49% -> 0% of each run, Pallas kernels for 0% -> 18%
where the time goes in v2:
time: 126 us; the launch traced here: 124 us
  Pallas kernels  36.2 us (29%)
  starting transfers between devices  34.8 us (28%)
  waiting for transfers between devices  30.2 us (24%)
  local copies, waits for them, and re-layouts  20.1 us (16%)
  other arithmetic  1.52 us (1%)
    ppermute x22, waiting for transfers between devices, send(): return lax.ppermute(value, both, where)  30.2 us
    ppermute x22, starting transfers between devices, send(): return lax.ppermute(value, both, where)  30 us
    unnamed x33, local copies, waits for them, and re-layouts  18.3 us
    pallas_call x1, Pallas kernels, inverse_factor(): pl.pallas_call(inverse_kernel, in_specs=[vmem(), pl.BlockSpec(memory_spac...  9.87 us
    pallas_call x4, Pallas kernels, crossed_share(): pl.pallas_call(lambda *refs: crossed_kernel(first, *refs), grid_spec=pltp...  8.02 us
    pallas_call x1, Pallas kernels, form_momentum(): pl.pallas_call(momentum_kernel, grid=(BLOCK // TILE,), in_specs=[pl.Block...  5.11 us
    pallas_call x1, Pallas kernels, partial_products(): pl.pallas_call(products_kernel, grid=(BLOCK // TILE,), in_specs=[pl.Block...  5.03 us
    pallas_call x1, Pallas kernels, form_update(): pl.pallas_call(update_kernel, grid=(BLOCK // TILE,), in_specs=[pl.BlockSp...  4.87 us
  transfers between devices with their start and end apart: 23, of which 10 were waited for; matrix products, arithmetic and copies ran while one was open for 0% of the time, Pallas kernels for 18%

profile of v2, /device:TPU:0, one launch (start us, length us, event | category | flops | bytes accessed | tf_op | source)
XLA Modules:
  0.0 123.9 jit_solution(11421059609570152109)
XLA Ops:
  0.7 2.2 %copy-done = f32[1024,1024]{1,0:T(8,128)S(1)} copy-done((f32[1024,1024]{1,0:T(8,128)S(1)}, f32[1024,1024]{1,0:T(8,128)}, u32[]{:S(2)}) %copy-start) | copy-done | bytes 4194328
  5.7 5.0 %products.1 = f32[1024,256]{1,0:T(8,128)S(1)} custom-call(f32[1024,1024]{1,0:T(8,128)S(1)} %copy-done, bf16[1024,1024]{1,0:T(8,128)(2,1)S(1)} %copy-done.3, f32[1024,256]{1,0:T(8,128)S(1)} %copy-done.13), custom_call_target="tpu_custom_call" | custom-call | flops 3221225472 | bytes 8388608 | tf_op jit(solution)/shard_map/products/pallas_call | solution.py:146
  11.7 3.1 %collective-permute-start = (f32[256,256]{1,0:T(8,128)}, f32[256,256]{1,0:T(8,128)}, u32[]{:S(2)}, u32[]{:S(2)}) collective-permute-start(f32[256,256]{1,0:T(8,128)} %get-tuple-element.35), channel_id=1, source_target_pairs={{0,2},{1,3},{2,0},{3,1},{4,6},{5,7},{6,4},{7,5},{8,10},{9,11},{10,... | collective-permute-start | bytes 786440 | tf_op jit(solution)/shard_map/ppermute | solution.py:59
  16.8 3.1 %collective-permute-done = f32[256,256]{1,0:T(8,128)} collective-permute-done((f32[256,256]{1,0:T(8,128)}, f32[256,256]{1,0:T(8,128)}, u32[]{:S(2)}, u32[]{:S(2)}) %collective-permute-start) | collective-permute-done | bytes 262176 | tf_op jit(solution)/shard_map/ppermute | solution.py:59
  19.8 3.0 %collective-permute-done.2 = f32[256,256]{1,0:T(8,128)} collective-permute-done((f32[256,256]{1,0:T(8,128)}, f32[256,256]{1,0:T(8,128)}, u32[]{:S(2)}, u32[]{:S(2)}) %collective-permute-start.2) | collective-permute-done | bytes 262176 | tf_op jit(solution)/shard_map/ppermute | solution.py:59
  24.8 3.1 %collective-permute-start.5 = (f32[256,256]{1,0:T(8,128)S(1)}, f32[256,256]{1,0:T(8,128)S(1)}, u32[]{:S(2)}, u32[]{:S(2)}) collective-permute-start(f32[256,256]{1,0:T(8,128)S(1)} %add_add_fusion.1), channel_id=1, source_target_pairs={{0,12},{1,13},{2,14},{3,15},{4,0},{5,1},{6,2},{7,3},{8,4},{9,5},{1... | collective-permute-start | bytes 786440 | tf_op jit(solution)/shard_map/ppermute | solution.py:59
  27.9 2.2 %collective-permute-start.3 = (f32[256,256]{1,0:T(8,128)S(1)}, f32[256,256]{1,0:T(8,128)S(1)}, u32[]{:S(2)}, u32[]{:S(2)}) collective-permute-start(f32[256,256]{1,0:T(8,128)S(1)} %add_add_fusion.1), channel_id=1, source_target_pairs={{0,8},{1,9},{2,10},{3,11},{4,12},{5,13},{6,14},{7,15},{8,0},{9,1},... | collective-permute-start | bytes 786440 | tf_op jit(solution)/shard_map/ppermute | solution.py:59
  31.7 6.5 %collective-permute-done.4 = f32[256,256]{1,0:T(8,128)S(1)} collective-permute-done((f32[256,256]{1,0:T(8,128)S(1)}, f32[256,256]{1,0:T(8,128)S(1)}, u32[]{:S(2)}, u32[]{:S(2)}) %collective-permute-start.4) | collective-permute-done | bytes 262176 | tf_op jit(solution)/shard_map/ppermute | solution.py:59
  40.1 2.5 %collective-permute-start.7 = (f32[256,256]{1,0:T(8,128)S(1)}, f32[256,256]{1,0:T(8,128)S(1)}, u32[]{:S(2)}, u32[]{:S(2)}) collective-permute-start(f32[256,256]{1,0:T(8,128)S(1)} %get-tuple-element.32.refs_3_), channel_id=1, source_target_pairs={{0,3},{1,0},{2,1},{3,2},{4,7},{5,4},{6,5},{7,6},{8,11},{9,8},{10,9... | collective-permute-start | bytes 786440 | tf_op jit(solution)/shard_map/ppermute | solution.py:59
  43.6 2.2 %copy-done.1 = f32[1024,1024]{1,0:T(8,128)S(1)} copy-done((f32[1024,1024]{1,0:T(8,128)S(1)}, f32[1024,1024]{1,0:T(8,128)}, u32[]{:S(2)}) %copy-start.1) | copy-done | bytes 4194328
  47.7 2.0 %crossed.5 = (f32[256,1024]{1,0:T(8,128)S(1)}, f32[256,256]{1,0:T(8,128)S(1)}) custom-call(s32[1]{0:T(128)} %bitcast.2.refs_0_, f32[1024,1024]{1,0:T(8,128)S(1)} %copy-done.1, bf16[1024,1024]{1,0:T(8,128)(2,1)S(1)} %copy-done.4, f32[256,256]{1,0:T(8,128)S(1)} %collective-permute-done.8.refs_3_, ...), custom_call_target="tpu_custom_call", output_to_operand_aliasing={{0}: (4, {}), {1}: (5, {})} | custom-call | flops 1006632960 | bytes 4194304 | tf_op jit(solution)/shard_map/crossed/pallas_call | solution.py:190
  49.8 2.0 %crossed.6 = (f32[256,1024]{1,0:T(8,128)S(1)}, f32[256,256]{1,0:T(8,128)S(1)}) custom-call(s32[1]{0:T(128)} %bitcast.1.refs_0_, f32[1024,1024]{1,0:T(8,128)S(1)} %copy-done.1, bf16[1024,1024]{1,0:T(8,128)(2,1)S(1)} %copy-done.4, f32[256,256]{1,0:T(8,128)S(1)} %collective-permute-done.7.refs_3_, ...), custom_call_target="tpu_custom_call", output_to_operand_aliasing={{0}: (4, {}), {1}: (5, {})} | custom-call | flops 1006632960 | bytes 4194304 | tf_op jit(solution)/shard_map/crossed/pallas_call | solution.py:190
  51.8 2.0 %crossed.7 = (f32[256,1024]{1,0:T(8,128)S(1)}, f32[256,256]{1,0:T(8,128)S(1)}) custom-call(s32[1]{0:T(128)} %bitcast.refs_0_, f32[1024,1024]{1,0:T(8,128)S(1)} %copy-done.1, bf16[1024,1024]{1,0:T(8,128)(2,1)S(1)} %copy-done.4, f32[256,256]{1,0:T(8,128)S(1)} %collective-permute-done.6.refs_3_, ...), custom_call_target="tpu_custom_call", output_to_operand_aliasing={{0}: (4, {}), {1}: (5, {})} | custom-call | flops 1006632960 | bytes 4194304 | tf_op jit(solution)/shard_map/crossed/pallas_call | solution.py:190
  56.1 4.1 %collective-permute-start.20 = (f32[128,256]{1,0:T(8,128)S(1)}, f32[128,256]{1,0:T(8,128)S(1)}, u32[]{:S(2)}, u32[]{:S(2)}) collective-permute-start(f32[128,256]{1,0:T(8,128)S(1)} %dynamic-slice_add_fusion.1), channel_id=1, source_target_pairs={{0,96},{1,97},{2,98},{3,99},{4,100},{5,101},{6,102},{7,103},{8,104... | collective-permute-start | bytes 393224 | tf_op jit(solution)/shard_map/ppermute | solution.py:59
  63.9 3.2 %collective-permute-start.12 = (f32[32,1024]{1,0:T(8,128)S(1)}, f32[32,1024]{1,0:T(8,128)S(1)}, u32[]{:S(2)}, u32[]{:S(2)}) collective-permute-start(f32[32,1024]{1,0:T(8,128)S(1)} %get-tuple-element.39), channel_id=1, source_target_pairs={{0,96},{1,97},{2,98},{3,99},{4,100},{5,101},{6,102},{7,103},{8,104... | collective-permute-start | bytes 393224 | tf_op jit(solution)/shard_map/ppermute | solution.py:59
  67.2 5.8 %collective-permute-done.19 = f32[128,256]{1,0:T(8,128)S(1)} collective-permute-done((f32[128,256]{1,0:T(8,128)S(1)}, f32[128,256]{1,0:T(8,128)S(1)}, u32[]{:S(2)}, u32[]{:S(2)}) %collective-permute-start.19) | collective-permute-done | bytes 131104 | tf_op jit(solution)/shard_map/ppermute | solution.py:59
  75.5 2.0 %collective-permute-start.14 = (f32[32,1024]{1,0:T(8,128)S(1)}, f32[32,1024]{1,0:T(8,128)S(1)}, u32[]{:S(2)}, u32[]{:S(2)}) collective-permute-start(f32[32,1024]{1,0:T(8,128)S(1)} %get-tuple-element.34.after), channel_id=1, source_target_pairs={{0,64},{1,65},{2,66},{3,67},{4,68},{5,69},{6,70},{7,71},{8,72},{9,... | collective-permute-start | bytes 393224 | tf_op jit(solution)/shard_map/ppermute | solution.py:59
  78.9 5.3 %collective-permute-done.13 = f32[32,1024]{1,0:T(8,128)S(1)} collective-permute-done((f32[32,1024]{1,0:T(8,128)S(1)}, f32[32,1024]{1,0:T(8,128)S(1)}, u32[]{:S(2)}, u32[]{:S(2)}) %collective-permute-start.13) | collective-permute-done | bytes 131104 | tf_op jit(solution)/shard_map/ppermute | solution.py:59
  85.0 9.9 %inverse.1 = f32[256,256]{1,0:T(8,128)S(1)} custom-call(f32[256,256]{1,0:T(8,128)S(1)} %maximum_select_fusion.1.gram, f32[32,1024]{1,0:T(8,128)S(1)} %get-tuple-element.34.after), custom_call_target="tpu_custom_call" | custom-call | flops 10000000000 | bytes 1048576 | tf_op jit(solution)/shard_map/inverse/pallas_call | solution.py:269
  96.0 2.3 %reduced.1 = (f32[256,1024]{1,0:T(8,128)S(1)}, bf16[256,1024]{1,0:T(8,128)(2,1)S(1)}, bf16[256,1024]{1,0:T(8,128)(2,1)S(1)}, f32[8,256]{1,0:T(8,128)S(1)}) custom-call(f32[256,1024]{1,0:T(8,128)S(1)} %maximum_select_fusion.crossed, f32[256,256]{1,0:T(8,128)S(1)} %inverse.1), custom_call_target="tpu_custom_call" | custom-call | flops 805306368 | bytes 3145728 | tf_op jit(solution)/shard_map/reduced/pallas_call | solution.py:305
  101.5 4.8 %all-to-all-start = ((f32[16,1,256]{2,1,0:T(1,128)}), f32[16,1,256]{2,1,0:T(1,128)S(1)}, u32[]{:S(2)}, u32[]{:S(2)}) async-start(f32[16,1,256]{2,1,0:T(1,128)} %broadcast_in_dim.16), calls=%async_computation | async-start | bytes 32768 | tf_op jit(solution)/shard_map/all_to_all | solution.py:409
  106.3 2.2 %copy-done.2 = f32[1024,1024]{1,0:T(8,128)S(1)} copy-done((f32[1024,1024]{1,0:T(8,128)S(1)}, f32[1024,1024]{1,0:T(8,128)}, u32[]{:S(2)}) %copy-start.2) | copy-done | bytes 4194328
  110.6 5.1 %momentum.4 = f32[1024,1024]{1,0:T(8,128)} custom-call(f32[1024,1024]{1,0:T(8,128)S(1)} %copy-done.2, bf16[1024,1024]{1,0:T(8,128)(2,1)S(1)} %copy-done.4, f32[1024,256]{1,0:T(8,128)S(1)} %basis.3, bf16[256,1024]{1,0:T(8,128)(2,1)S(1)} %copy-done.8, bf16[256,1024]{1,0:T(8,128)(2,1)S(1)} %copy-done.11), custom_call_target="tpu_custom_call" | custom-call | flops 3221225472 | bytes 12582912 | tf_op jit(solution)/shard_map/momentum/pallas_call | solution.py:330
  119.0 4.9 %update.1 = (bf16[1024,1024]{1,0:T(8,128)(2,1)}, f32[1024,256]{1,0:T(8,128)}) custom-call(f32[16,256]{1,0:T(8,128)S(1)} %bitcast.8, f32[1024,256]{1,0:T(8,128)S(1)} %basis.3, f32[256,1024]{1,0:T(8,128)S(1)} %copy-done.15, bf16[256,1024]{1,0:T(8,128)(2,1)S(1)} %copy-done.9, bf16[256,1024]{1,0:T(8,128)(2,1)S(1)} %copy-done.12), custom_call_target="tpu_custom_call" | custom-call | flops 3221225472 | bytes 6291456 | tf_op jit(solution)/shard_map/update/pallas_call | solution.py:358
  (87 shorter events, 34.3 us)
Async XLA Ops:
  10.8 32.8 %copy-start.4 = (bf16[1024,1024]{1,0:T(8,128)(2,1)S(1)}, bf16[1024,1024]{1,0:T(8,128)(2,1)}, u32[]{:S(2)}) copy-start(bf16[1024,1024]{1,0:T(8,128)(2,1)} %gradient.3) | copy-start | bytes 6291460
  11.7 8.2 %collective-permute-start = (f32[256,256]{1,0:T(8,128)}, f32[256,256]{1,0:T(8,128)}, u32[]{:S(2)}, u32[]{:S(2)}) collective-permute-start(f32[256,256]{1,0:T(8,128)} %get-tuple-element.35), channel_id=1, source_target_pairs={{0,2},{1,3},{2,0},{3,1},{4,6},{5,7},{6,4},{7,5},{8,10},{9,11},{10,... | collective-permute-start | bytes 786440 | tf_op jit(solution)/shard_map/ppermute | solution.py:59
  14.8 8.1 %collective-permute-start.2 = (f32[256,256]{1,0:T(8,128)}, f32[256,256]{1,0:T(8,128)}, u32[]{:S(2)}, u32[]{:S(2)}) collective-permute-start(f32[256,256]{1,0:T(8,128)} %get-tuple-element.36), channel_id=1, source_target_pairs={{0,3},{1,0},{2,1},{3,2},{4,7},{5,4},{6,5},{7,6},{8,11},{9,8},{10,9... | collective-permute-start | bytes 786440 | tf_op jit(solution)/shard_map/ppermute | solution.py:59
  15.9 7.7 %collective-permute-start.1 = (f32[256,256]{1,0:T(8,128)S(1)}, f32[256,256]{1,0:T(8,128)}, u32[]{:S(2)}, u32[]{:S(2)}) collective-permute-start(f32[256,256]{1,0:T(8,128)S(1)} %get-tuple-element.37), channel_id=1, source_target_pairs={{0,1},{1,2},{2,3},{3,0},{4,5},{5,6},{6,7},{7,4},{8,9},{9,10},{10,1... | collective-permute-start | bytes 786440 | tf_op jit(solution)/shard_map/ppermute | solution.py:59
  24.8 7.0 %collective-permute-start.5 = (f32[256,256]{1,0:T(8,128)S(1)}, f32[256,256]{1,0:T(8,128)S(1)}, u32[]{:S(2)}, u32[]{:S(2)}) collective-permute-start(f32[256,256]{1,0:T(8,128)S(1)} %add_add_fusion.1), channel_id=1, source_target_pairs={{0,12},{1,13},{2,14},{3,15},{4,0},{5,1},{6,2},{7,3},{8,4},{9,5},{1... | collective-permute-start | bytes 786440 | tf_op jit(solution)/shard_map/ppermute | solution.py:59
  27.9 10.4 %collective-permute-start.4 = (f32[256,256]{1,0:T(8,128)S(1)}, f32[256,256]{1,0:T(8,128)S(1)}, u32[]{:S(2)}, u32[]{:S(2)}) collective-permute-start(f32[256,256]{1,0:T(8,128)S(1)} %add_add_fusion.1), channel_id=1, source_target_pairs={{0,4},{1,5},{2,6},{3,7},{4,8},{5,9},{6,10},{7,11},{8,12},{9,13},{1... | collective-permute-start | bytes 786440 | tf_op jit(solution)/shard_map/ppermute | solution.py:59
  27.9 10.4 %collective-permute-start.3 = (f32[256,256]{1,0:T(8,128)S(1)}, f32[256,256]{1,0:T(8,128)S(1)}, u32[]{:S(2)}, u32[]{:S(2)}) collective-permute-start(f32[256,256]{1,0:T(8,128)S(1)} %add_add_fusion.1), channel_id=1, source_target_pairs={{0,8},{1,9},{2,10},{3,11},{4,12},{5,13},{6,14},{7,15},{8,0},{9,1},... | collective-permute-start | bytes 786440 | tf_op jit(solution)/shard_map/ppermute | solution.py:59
  39.4 8.3 %collective-permute-start.8 = (f32[256,256]{1,0:T(8,128)S(1)}, f32[256,256]{1,0:T(8,128)S(1)}, u32[]{:S(2)}, u32[]{:S(2)}) collective-permute-start(f32[256,256]{1,0:T(8,128)S(1)} %get-tuple-element.32.refs_3_), channel_id=1, source_target_pairs={{0,1},{1,2},{2,3},{3,0},{4,5},{5,6},{6,7},{7,4},{8,9},{9,10},{10,1... | collective-permute-start | bytes 786440 | tf_op jit(solution)/shard_map/ppermute | solution.py:59
  40.1 9.7 %collective-permute-start.7 = (f32[256,256]{1,0:T(8,128)S(1)}, f32[256,256]{1,0:T(8,128)S(1)}, u32[]{:S(2)}, u32[]{:S(2)}) collective-permute-start(f32[256,256]{1,0:T(8,128)S(1)} %get-tuple-element.32.refs_3_), channel_id=1, source_target_pairs={{0,3},{1,0},{2,1},{3,2},{4,7},{5,4},{6,5},{7,6},{8,11},{9,8},{10,9... | collective-permute-start | bytes 786440 | tf_op jit(solution)/shard_map/ppermute | solution.py:59
  42.6 9.2 %collective-permute-start.6 = (f32[256,256]{1,0:T(8,128)S(1)}, f32[256,256]{1,0:T(8,128)S(1)}, u32[]{:S(2)}, u32[]{:S(2)}) collective-permute-start(f32[256,256]{1,0:T(8,128)S(1)} %get-tuple-element.32.refs_3_), channel_id=1, source_target_pairs={{0,2},{1,3},{2,0},{3,1},{4,6},{5,7},{6,4},{7,5},{8,10},{9,11},{10,... | collective-permute-start | bytes 786440 | tf_op jit(solution)/shard_map/ppermute | solution.py:59
  53.9 8.2 %collective-permute-start.9 = (f32[128,1024]{1,0:T(8,128)S(1)}, f32[128,1024]{1,0:T(8,128)S(1)}, u32[]{:S(2)}, u32[]{:S(2)}) collective-permute-start(f32[128,1024]{1,0:T(8,128)S(1)} %constant_dynamic-slice_fusion.4), channel_id=1, source_target_pairs={{0,16},{1,17},{2,18},{3,19},{4,20},{5,21},{6,22},{7,23},{8,24},{9,... | collective-permute-start | bytes 1572872 | tf_op jit(solution)/shard_map/ppermute | solution.py:59
  54.0 2.1 %collective-permute-start.17 = (f32[128,256]{1,0:T(8,128)S(1)}, f32[128,256]{1,0:T(8,128)S(1)}, u32[]{:S(2)}, u32[]{:S(2)}) collective-permute-start(f32[128,256]{1,0:T(8,128)S(1)} %constant_dynamic-slice_fusion), channel_id=1, source_target_pairs={{0,16},{1,17},{2,18},{3,19},{4,20},{5,21},{6,22},{7,23},{8,24},{9,... | collective-permute-start | bytes 393224 | tf_op jit(solution)/shard_map/ppermute | solution.py:59
  56.1 11.0 %collective-permute-start.20 = (f32[128,256]{1,0:T(8,128)S(1)}, f32[128,256]{1,0:T(8,128)S(1)}, u32[]{:S(2)}, u32[]{:S(2)}) collective-permute-start(f32[128,256]{1,0:T(8,128)S(1)} %dynamic-slice_add_fusion.1), channel_id=1, source_target_pairs={{0,96},{1,97},{2,98},{3,99},{4,100},{5,101},{6,102},{7,103},{8,104... | collective-permute-start | bytes 393224 | tf_op jit(solution)/shard_map/ppermute | solution.py:59
  60.2 12.8 %collective-permute-start.19 = (f32[128,256]{1,0:T(8,128)S(1)}, f32[128,256]{1,0:T(8,128)S(1)}, u32[]{:S(2)}, u32[]{:S(2)}) collective-permute-start(f32[128,256]{1,0:T(8,128)S(1)} %dynamic-slice_add_fusion.1), channel_id=1, source_target_pairs={{0,32},{1,33},{2,34},{3,35},{4,36},{5,37},{6,38},{7,39},{8,40},{9,... | collective-permute-start | bytes 393224 | tf_op jit(solution)/shard_map/ppermute | solution.py:59
  60.2 12.8 %collective-permute-start.18 = (f32[128,256]{1,0:T(8,128)S(1)}, f32[128,256]{1,0:T(8,128)S(1)}, u32[]{:S(2)}, u32[]{:S(2)}) collective-permute-start(f32[128,256]{1,0:T(8,128)S(1)} %dynamic-slice_add_fusion.1), channel_id=1, source_target_pairs={{0,64},{1,65},{2,66},{3,67},{4,68},{5,69},{6,70},{7,71},{8,72},{9,... | collective-permute-start | bytes 393224 | tf_op jit(solution)/shard_map/ppermute | solution.py:59
  62.2 10.9 %collective-permute-start.10 = (f32[32,1024]{1,0:T(8,128)S(1)}, f32[32,1024]{1,0:T(8,128)S(1)}, u32[]{:S(2)}, u32[]{:S(2)}) collective-permute-start(f32[32,1024]{1,0:T(8,128)S(1)} %get-tuple-element.38), channel_id=1, source_target_pairs={{0,64},{1,65},{2,66},{3,67},{4,68},{5,69},{6,70},{7,71},{8,72},{9,... | collective-permute-start | bytes 393224 | tf_op jit(solution)/shard_map/ppermute | solution.py:59
  63.9 9.2 %collective-permute-start.12 = (f32[32,1024]{1,0:T(8,128)S(1)}, f32[32,1024]{1,0:T(8,128)S(1)}, u32[]{:S(2)}, u32[]{:S(2)}) collective-permute-start(f32[32,1024]{1,0:T(8,128)S(1)} %get-tuple-element.39), channel_id=1, source_target_pairs={{0,96},{1,97},{2,98},{3,99},{4,100},{5,101},{6,102},{7,103},{8,104... | collective-permute-start | bytes 393224 | tf_op jit(solution)/shard_map/ppermute | solution.py:59
  67.2 7.9 %collective-permute-start.11 = (f32[32,1024]{1,0:T(8,128)S(1)}, f32[32,1024]{1,0:T(8,128)S(1)}, u32[]{:S(2)}, u32[]{:S(2)}) collective-permute-start(f32[32,1024]{1,0:T(8,128)S(1)} %get-tuple-element.40), channel_id=1, source_target_pairs={{0,32},{1,33},{2,34},{3,35},{4,36},{5,37},{6,38},{7,39},{8,40},{9,... | collective-permute-start | bytes 393224 | tf_op jit(solution)/shard_map/ppermute | solution.py:59
  73.1 4.4 %collective-permute-start.21 = (f32[128,256]{1,0:T(8,128)S(1)}, f32[128,256]{1,0:T(8,128)S(1)}, u32[]{:S(2)}, u32[]{:S(2)}) collective-permute-start(f32[128,256]{1,0:T(8,128)S(1)} %add_add_fusion.2), channel_id=1, source_target_pairs={{0,16},{1,17},{2,18},{3,19},{4,20},{5,21},{6,22},{7,23},{8,24},{9,... | collective-permute-start | bytes 393224 | tf_op jit(solution)/shard_map/ppermute | solution.py:59
  75.2 9.0 %collective-permute-start.13 = (f32[32,1024]{1,0:T(8,128)S(1)}, f32[32,1024]{1,0:T(8,128)S(1)}, u32[]{:S(2)}, u32[]{:S(2)}) collective-permute-start(f32[32,1024]{1,0:T(8,128)S(1)} %get-tuple-element.34.after), channel_id=1, source_target_pairs={{0,32},{1,33},{2,34},{3,35},{4,36},{5,37},{6,38},{7,39},{8,40},{9,... | collective-permute-start | bytes 393224 | tf_op jit(solution)/shard_map/ppermute | solution.py:59
  75.5 8.8 %collective-permute-start.14 = (f32[32,1024]{1,0:T(8,128)S(1)}, f32[32,1024]{1,0:T(8,128)S(1)}, u32[]{:S(2)}, u32[]{:S(2)}) collective-permute-start(f32[32,1024]{1,0:T(8,128)S(1)} %get-tuple-element.34.after), channel_id=1, source_target_pairs={{0,64},{1,65},{2,66},{3,67},{4,68},{5,69},{6,70},{7,71},{8,72},{9,... | collective-permute-start | bytes 393224 | tf_op jit(solution)/shard_map/ppermute | solution.py:59
  77.5 7.4 %collective-permute-start.15 = (f32[32,1024]{1,0:T(8,128)S(1)}, f32[32,1024]{1,0:T(8,128)S(1)}, u32[]{:S(2)}, u32[]{:S(2)}) collective-permute-start(f32[32,1024]{1,0:T(8,128)S(1)} %get-tuple-element.34.after), channel_id=1, source_target_pairs={{0,96},{1,97},{2,98},{3,99},{4,100},{5,101},{6,102},{7,103},{8,104... | collective-permute-start | bytes 393224 | tf_op jit(solution)/shard_map/ppermute | solution.py:59
  84.9 11.0 %collective-permute-start.16 = (f32[128,1024]{1,0:T(8,128)S(1)}, f32[128,1024]{1,0:T(8,128)S(1)}, u32[]{:S(2)}, u32[]{:S(2)}) collective-permute-start(f32[128,1024]{1,0:T(8,128)S(1)} %constant_dynamic-update-slice_fusion.4), channel_id=1, source_target_pairs={{0,16},{1,17},{2,18},{3,19},{4,20},{5,21},{6,22},{7,23},{8,24},{9,... | collective-permute-start | bytes 1572872 | tf_op jit(solution)/shard_map/ppermute | solution.py:59
  101.5 14.2 %all-to-all-start = ((f32[16,1,256]{2,1,0:T(1,128)}), f32[16,1,256]{2,1,0:T(1,128)S(1)}, u32[]{:S(2)}, u32[]{:S(2)}) async-start(f32[16,1,256]{2,1,0:T(1,128)} %broadcast_in_dim.16), calls=%async_computation | async-start | bytes 32768 | tf_op jit(solution)/shard_map/all_to_all | solution.py:409
  (15 other events, 21.2 us)

commit v3 on v0

v3 whole, which is shorter than its diff:
```python
import math

import jax
import jax.numpy as jnp
from jax import lax
from jax.experimental import pallas as pl
from jax.experimental.pallas import tpu as pltpu
from jax.sharding import PartitionSpec as P

M = 8192
N = 16384
R = 256
BLOCK = 1024
TILE = 256


momentum_keep = 0.95
epsilon_norm = 1e-06
highest = lax.Precision.HIGHEST
both = ("fsdp", "tp")
f32, bf16 = jnp.float32, jnp.bfloat16


def pairs(target):
    out = []
    for z in range(4):
        for core in range(2):
            for y in range(4):
                for x in range(4):
                    tz, tcore, ty, tx = target(z, core, y, x)
                    here = (z * 2 + core) * 16 + y * 4 + x
                    there = (tz * 2 + tcore) * 16 + ty * 4 + tx
                    out.append((here, there))
    return out


def first_axis(k):
    def target(z, core, y, x):
        return (z, core, y, (x + k) % 4) if core == 0 else (z, core, (y + k) % 4, x)

    return pairs(target)


def second_axis(k):
    def target(z, core, y, x):
        return (z, core, (y + k) % 4, x) if core == 0 else (z, core, y, (x + k) % 4)

    return pairs(target)


def along_z(k):
    return pairs(lambda z, core, y, x: ((z + k) % 4, core, y, x))


other_core = pairs(lambda z, core, y, x: (z, 1 - core, y, x))


def send(value, where):
    return lax.ppermute(value, both, where)


def to_three(parts, where):
    two, one, three = [send(parts[k], where(k)) for k in (2, 1, 3)]
    return one, two, three


def sum_four(own, one, two, three):
    return (own + two) + (one + three)


def place():
    fsdp, tp = lax.axis_index("fsdp"), lax.axis_index("tp")
    core = lax.rem(fsdp, 2)
    return lax.div(fsdp, 2), core, jnp.where(core == 0, lax.rem(tp, 4), lax.div(tp, 4))


def span(index, rows):
    return pl.ds(pl.multiple_of(index * rows, rows), rows)


def ahead(position, k):
    return lax.rem(position + k, 4)


def pieces(value, count):
    out = []
    for n in range(count):
        part = value.astype(bf16)
        out.append(part)
        if n < count - 1:
            value = value - part.astype(f32)
    return out


def dot(left, right, dims=((1,), (0,)), precision=None):
    return lax.dot_general(
        left, right, (dims, ((), ())), precision=precision, preferred_element_type=f32
    )


def piece_dot(left, right, dims=((1,), (0,))):
    count = len(left)
    total = None
    for rank in range(count - 1, -1, -1):
        for n in range(rank + 1):
            term = dot(left[n], right[rank - n], dims)
            total = term if total is None else total + term
    return total


def params():
    return pltpu.CompilerParams(vmem_limit_bytes=20 * 2**20)


def cost(flops, bytes_accessed):
    return pl.CostEstimate(flops=flops, bytes_accessed=bytes_accessed, transcendentals=0)


def vmem():
    return pl.BlockSpec(memory_space=pltpu.VMEM)


def hbm():
    return pl.BlockSpec(memory_space=pltpu.HBM)


def anywhere():
    return pl.BlockSpec(memory_space=pl.ANY)


def tile(n):
    return pl.ds(n * TILE, TILE)


TILES = BLOCK // TILE
QUARTER = BLOCK // 4


def call(kernel, name, out, flops=0, in_specs=None, **more):
    def run(*operands):
        return pl.pallas_call(
            kernel,
            in_specs=in_specs or [vmem()] * len(operands),
            out_specs=[vmem()] * len(out),
            out_shape=[jax.ShapeDtypeStruct(shape, kind) for shape, kind in out],
            compiler_params=params(),
            cost_estimate=cost(flops, 2**20),
            name=name,
            **more,
        )(*operands)

    return run


def quarters_kernel(partial, *parts):
    me = place()[2]
    for k in range(4):
        parts[k][...] = partial[span(ahead(me, k), QUARTER)]


def quarters(partial):
    return call(quarters_kernel, "quarters", [((QUARTER, R), f32)] * 4)(partial)


CROSSED_PIECES = 2
HALF = R // 2
B = 64
GRAM_ROWS = 24
CORE_ROWS = HALF + GRAM_ROWS


def packed_pieces():
    for core in range(2):
        for n in range(4):
            for s in range(0, GRAM_ROWS, 8):
                row = core * 96 + n * GRAM_ROWS + s
                top, left = core * GRAM_ROWS + s, n * R
                if row < HALF:
                    yield top, left, R, row, 0
                else:
                    yield top, left, HALF, row, HALF
                    yield top, left + HALF, HALF, row + B, HALF


def crossed_kernel(k, momentum, gradient, part, *refs):
    me = place()[2]
    turned = pieces(part[...].T, 3)
    gram = piece_dot(turned, pieces(part[...], 3))
    spot = span(ahead(me, 4 - k), QUARTER)
    value = momentum[spot] + gradient[spot].astype(f32)
    cross = piece_dot(turned[:CROSSED_PIECES], pieces(value, CROSSED_PIECES))
    if k != 0:
        cross, gram = refs[0][...] + cross, refs[1][...] + gram
    refs[-2][...], refs[-1][...] = cross, gram


def crossed_share(k, momentum, gradient, part, before=()):
    return call(
        lambda *refs: crossed_kernel(k, *refs),
        "crossed",
        [((R, BLOCK), f32), ((R, R), f32)],
        2 * QUARTER * (BLOCK + R) * R * 6,
        input_output_aliases={3: 0, 4: 1} if before else {},
    )(momentum, gradient, part, *before)


def depart_kernel(crossed, gram, keep, give, packed):
    core = place()[1]
    for top, left, width, row, column in packed_pieces():
        packed[top : top + 8, left : left + width] = gram[row : row + 8, column : column + width]
    for whose, out in ((core, keep), (1 - core, give)):
        out[:HALF] = crossed[span(whose, HALF)]
        out[HALF:] = packed[span(whose, GRAM_ROWS)]


def depart(crossed, gram):
    return call(
        depart_kernel,
        "depart",
        [((CORE_ROWS, BLOCK), f32)] * 2,
        scratch_shapes=[pltpu.VMEM((2 * GRAM_ROWS, BLOCK), f32)],
    )(crossed, gram)


Z_ROWS = HALF // 4


def spread_kernel(keep, got, *refs):
    z = place()[0]
    parts, total = refs[:4], refs[4]
    total[...] = keep[...] + got[...]
    for k in range(4):
        parts[k][:Z_ROWS] = total[span(ahead(z, k), Z_ROWS)]
        parts[k][Z_ROWS:] = total[HALF:]


def spread(keep, got):
    return call(
        spread_kernel,
        "spread",
        [((Z_ROWS + GRAM_ROWS, BLOCK), f32)] * 4,
        scratch_shapes=[pltpu.VMEM((CORE_ROWS, BLOCK), f32)],
    )(keep, got)


def settle_kernel(own, one, two, three, cross, gram):
    total = sum_four(own[...], one[...], two[...], three[...])
    cross[...], gram[...] = total[:Z_ROWS], total[Z_ROWS:]


def settle(*parts):
    return call(
        settle_kernel, "settle", [((Z_ROWS, BLOCK), f32), ((GRAM_ROWS, BLOCK), f32)]
    )(*parts)


GROUP = 8


def block_inverse(block):
    tiles, width = B // 8, 2 * B
    lane = lax.broadcasted_iota(jnp.int32, (8, width), 1)
    sub = lax.broadcasted_iota(jnp.int32, (8, width), 0)
    wide = jnp.concatenate([block, jnp.zeros_like(block)], axis=1)
    a = [wide[8 * t : 8 * t + 8] + (lane == sub + 8 * t + B).astype(f32) for t in range(tiles)]
    for start in range(0, B, GROUP):
        top = start // 8
        left = tiles - top
        columns = [
            [
                jnp.broadcast_to(a[t][:, start + c : start + c + 1], (8, width))
                for t in range(top, tiles)
            ]
            for c in range(GROUP)
        ]
        for c in range(GROUP):
            pivot = jnp.broadcast_to(columns[c][0][c : c + 1, :], (8, width))
            scale = 1.0 / pivot
            factor = [columns[c][t] * scale for t in range(left)]
            factor[0] = jnp.where(sub > c, factor[0], 0.0)
            for later in range(c + 1, GROUP):
                value = jnp.broadcast_to(columns[later][0][c : c + 1, :], (8, width))
                for t in range(left):
                    columns[later][t] = columns[later][t] - factor[t] * value
            row = jnp.broadcast_to(a[top][c : c + 1, :], (8, width))
            for t in range(left):
                a[top + t] = a[top + t] - factor[t] * row
    out = []
    for t in range(tiles):
        pivots = jnp.sum(jnp.where(lane == sub + 8 * t, a[t], 0.0), axis=1, keepdims=True)
        out.append(a[t][:, B:] * lax.rsqrt(pivots))
    return jnp.concatenate(out, 0)


def eliminate(work, out, blocks, shift):
    for n in blocks:
        low, high = n * B, n * B + B
        inverse = block_inverse(work[low - shift : high - shift, low:high])
        rows = dot(inverse, work[low - shift : high - shift, :], precision=highest)
        out[low:high, :] = rows[:, R:]
        if high < R:
            work[high - shift :, :] = work[high - shift :, :] - dot(
                rows[:, high:R], rows, ((0,), (0,)), precision=highest
            )


def identity_rows(low, high):
    row = lax.broadcasted_iota(jnp.int32, (high - low, R), 0) + low
    return (row == lax.broadcasted_iota(jnp.int32, (high - low, R), 1)).astype(f32)


def inverse_kernel(gram, other, after, out, work, packed):
    core = place()[1]
    packed[span(core, GRAM_ROWS)] = gram[...]
    packed[span(1 - core, GRAM_ROWS)] = other[...]
    for top, left, width, row, column in packed_pieces():
        work[row : row + 8, column : column + width] = packed[top : top + 8, left : left + width]
    work[HALF:, :HALF] = jnp.zeros((HALF, HALF), f32)
    work[:, R:] = identity_rows(0, R)
    eliminate(work, out, range(R // B), 0)


def inverse_factor(gram, other, after):
    return call(
        inverse_kernel,
        "inverse",
        [((R, R), f32)],
        10**9,
        in_specs=[vmem(), vmem(), anywhere()],
        scratch_shapes=[pltpu.VMEM((R, 2 * R), f32), pltpu.VMEM((2 * GRAM_ROWS, BLOCK), f32)],
    )(gram, other, after)[0]


def ordered_kernel(own, one, two, three, after, out):
    z = place()[0]
    for k, part in enumerate((own, one, two, three)):
        out[span(ahead(z, 4 - k), Z_ROWS)] = part[...]


def ordered(parts, after):
    return call(
        ordered_kernel,
        "ordered",
        [((HALF, BLOCK), f32)],
        in_specs=[vmem()] * 4 + [anywhere()],
    )(*parts, after)[0]


def basis_kernel(own, one, two, three, inverse, basis):
    me = place()[2]
    for k, part in enumerate((own, one, two, three)):
        basis[span(ahead(me, 4 - k), QUARTER)] = dot(
            part[...], inverse[...], ((1,), (1,)), precision=highest
        )


def form_basis(parts, inverse):
    return call(basis_kernel, "basis", [((BLOCK, R), f32)], 2 * BLOCK * R * R * 6)(*parts, inverse)[0]


def reduced_kernel(half, other, inverse, high, low, squares, crossed):
    core = place()[1]
    crossed[span(core, HALF)] = half[...]
    crossed[span(1 - core, HALF)] = other[...]
    value = dot(inverse[...], crossed[...], precision=highest)
    high[...], low[...] = pieces(value, 2)
    square = value * value
    folded = square[:, :128]
    for n in range(1, BLOCK // 128):
        folded = folded + square[:, n * 128 : n * 128 + 128]
    total = jnp.sum(folded.T, axis=0, keepdims=True)
    squares[...] = jnp.broadcast_to(total, squares.shape)


def form_reduced(half, other, inverse):
    return call(
        reduced_kernel,
        "reduced",
        [((R, BLOCK), bf16), ((R, BLOCK), bf16), ((8, R), f32)],
        2 * BLOCK * R * R * 6,
        scratch_shapes=[pltpu.VMEM((R, BLOCK), f32)],
    )(half, other, inverse)


def momentum_kernel(momentum, gradient, basis, high, low, out, m, g, m_sem, g_sem, o_sem):
    reads = [
        (
            pltpu.make_async_copy(momentum.at[tile(n)], m.at[tile(n)], m_sem.at[n]),
            pltpu.make_async_copy(gradient.at[tile(n)], g.at[tile(n)], g_sem.at[n]),
        )
        for n in range(TILES)
    ]
    for pair in reads:
        for copy in pair:
            copy.start()
    right = [high[...], low[...]]
    writes = []
    for n in range(TILES):
        product = piece_dot(pieces(basis[tile(n)], 2), right)
        for copy in reads[n]:
            copy.wait()
        buffer = m[tile(n)] + g[tile(n)].astype(f32)
        m[tile(n)] = buffer - (1.0 - momentum_keep) * product
        writes.append(pltpu.make_async_copy(m.at[tile(n)], out.at[tile(n)], o_sem.at[n]))
        writes[n].start()
    for copy in writes:
        copy.wait()


def form_momentum(momentum, gradient, basis, high, low):
    return pl.pallas_call(
        momentum_kernel,
        in_specs=[hbm()] * 2 + [vmem()] * 3,
        out_specs=hbm(),
        out_shape=jax.ShapeDtypeStruct((BLOCK, BLOCK), f32),
        scratch_shapes=[
            pltpu.VMEM((BLOCK, BLOCK), f32),
            pltpu.VMEM((BLOCK, BLOCK), bf16),
            pltpu.SemaphoreType.DMA((TILES,)),
            pltpu.SemaphoreType.DMA((TILES,)),
            pltpu.SemaphoreType.DMA((TILES,)),
        ],
        compiler_params=params(),
        cost_estimate=cost(2 * BLOCK * BLOCK * R * 6, 12 * 2**20),
        name="momentum",
    )(*[pltpu.with_memory_space_constraint(v, pltpu.HBM) for v in (momentum, gradient)], basis, high, low)


def update_kernel(squares, basis, high, low, update, new_basis, u, v, u_sem, v_sem):
    norm = jnp.sqrt(jnp.sum(squares[...], axis=0, keepdims=True)) + epsilon_norm
    right = [high[...], low[...]]
    copies = []
    for n in range(TILES):
        scaled = basis[tile(n)] * (math.sqrt(M * N / R) / norm)
        u[tile(n)] = piece_dot(pieces(scaled, 2), right).astype(bf16)
        copies.append(pltpu.make_async_copy(u.at[tile(n)], update.at[tile(n)], u_sem.at[n]))
        copies[-1].start()
        reduced = high[:, tile(n)].astype(f32) + low[:, tile(n)].astype(f32)
        v[tile(n)] = reduced.T / norm
        copies.append(pltpu.make_async_copy(v.at[tile(n)], new_basis.at[tile(n)], v_sem.at[n]))
        copies[-1].start()
    for copy in copies:
        copy.wait()


def form_update(squares, basis, high, low):
    return pl.pallas_call(
        update_kernel,
        in_specs=[vmem()] * 4,
        out_specs=[hbm()] * 2,
        out_shape=[
            jax.ShapeDtypeStruct((BLOCK, BLOCK), bf16),
            jax.ShapeDtypeStruct((BLOCK, R), f32),
        ],
        scratch_shapes=[
            pltpu.VMEM((BLOCK, BLOCK), bf16),
            pltpu.VMEM((BLOCK, R), f32),
            pltpu.SemaphoreType.DMA((TILES,)),
            pltpu.SemaphoreType.DMA((TILES,)),
        ],
        compiler_params=params(),
        cost_estimate=cost(2 * BLOCK * BLOCK * R * 6, 6 * 2**20),
        name="update",
    )(squares, basis, high, low)


def local(momentum, gradient, basis_prev):
    buffer = momentum + gradient.astype(f32)
    partial = dot(buffer, basis_prev, precision=highest)
    parts = quarters(partial)
    quarter = sum_four(parts[0], *to_three(parts, first_axis))
    quarter = sum_four(quarter, *to_three([quarter] * 4, second_axis))
    parts = [quarter, *to_three([quarter] * 4, first_axis)]

    sums = ()
    for k in (0, 1, 3, 2):
        sums = crossed_share(k, momentum, gradient, parts[k], sums)

    keep, give = depart(*sums)
    shares = spread(keep, send(give, other_core))
    crossed, gram = settle(shares[0], *to_three(shares, along_z))
    inverse = inverse_factor(gram, send(gram, other_core), crossed)
    half = ordered([crossed, *to_three([crossed] * 4, along_z)], inverse)
    basis = form_basis(parts, inverse)
    high, low, squares = form_reduced(half, send(half, other_core), inverse)
    everyone = jnp.broadcast_to(squares[None, :1], (16, 1, R))
    squares = lax.all_to_all(everyone, "tp", 0, 0).reshape(16, R)
    new_momentum = form_momentum(momentum, gradient, basis, high, low)
    update, new_basis = form_update(squares, basis, high, low)
    return (update, new_momentum, new_basis)


def solution(mesh):
    in_specs = (P("fsdp", "tp"), P("fsdp", "tp"), P("tp", None))
    out_specs = (P("fsdp", "tp"), P("fsdp", "tp"), P("tp", None))
    return jax.shard_map(local, mesh=mesh, in_specs=in_specs, out_specs=out_specs, check_vma=False)
```

time: 382 us -> 97.5 us (0.26)
  waiting for transfers between devices: 210 us -> 31.7 us
  other arithmetic: 59.3 us -> 0.14 us
  blocking collectives: 40.3 us -> 0 us
  matrix products: 46 us -> 6.33 us
  starting transfers between devices: 0.3 us -> 31.9 us
  Pallas kernels: 0 us -> 24.4 us
  between operations: 15.2 us -> 1.02 us
  local copies, waits for them, and re-layouts: 9.19 us -> 1.84 us
    psum x3 -> x0, waiting for transfers between devices: 210 us -> none  [the longest x1 89.4 us: local(): products = lax.psum(matmul(buffer, basis_prev), 'tp')]
    another operation x9 -> x0, other arithmetic: 55.5 us -> none  [the longest x6 34 us: orthonormal(): lower_factor = jnp.linalg.cholesky(gram_matrix)]
    psum x1 -> x0, blocking collectives: 40.3 us -> none  [local(): squares = lax.psum(jnp.sum(reduced * reduced, axis=0), 'tp')]
    dot_general x5 -> x1, matrix products: 39.3 us -> 6.33 us  [dot(): lax.dot_general(left, right, (dims, ((), ())), precision=precision, prefe...]
    ppermute x0 -> x18, waiting for transfers between devices: none -> 29.6 us  [send(): return lax.ppermute(value, both, where)]
    ppermute x0 -> x18, starting transfers between devices: none -> 27.7 us  [send(): return lax.ppermute(value, both, where)]
    pallas_call x0 -> x14, Pallas kernels: none -> 24.4 us  [the longest x12 16.2 us: run(): pl.pallas_call(kernel, in_specs=in_specs or [vmem()] * len(operands), out...]
    another operation x5 -> x0, matrix products: 6.66 us -> none  [the longest x3 4.51 us: orthonormal(): lax.linalg.triangular_solve(lower_factor, products, left_side=False, lowe...]
  transfers between devices with their start and end apart: 3 -> 19, of which waited for: 3 -> 12; matrix products, arithmetic and copies ran while one was open for 0% -> 0% of each run, Pallas kernels for 0% -> 20%
where the time goes in v3:
time: 97.5 us; the launch traced here: 97.4 us
  starting transfers between devices  31.9 us (33%)
  waiting for transfers between devices  31.7 us (33%)
  Pallas kernels  24.4 us (25%)
  matrix products  6.33 us (6%)
  local copies, waits for them, and re-layouts  1.84 us (2%)
  between operations  1.02 us (1%)
    ppermute x18, waiting for transfers between devices, send(): return lax.ppermute(value, both, where)  29.6 us
    ppermute x18, starting transfers between devices, send(): return lax.ppermute(value, both, where)  27.7 us
    pallas_call x12, Pallas kernels, run(): pl.pallas_call(kernel, in_specs=in_specs or [vmem()] * len(operands), out...  16.2 us
    dot_general x1, matrix products, dot(): lax.dot_general(left, right, (dims, ((), ())), precision=precision, prefe...  6.33 us
    pallas_call x1, Pallas kernels, form_momentum(): pl.pallas_call(momentum_kernel, in_specs=[hbm()] * 2 + [vmem()] * 3, out_...  5.5 us
    all_to_all x1, starting transfers between devices, local(): squares = lax.all_to_all(everyone, 'tp', 0, 0).reshape(16, R)  4.14 us
    pallas_call x1, Pallas kernels, form_update(): pl.pallas_call(update_kernel, in_specs=[vmem()] * 4, out_specs=[hbm()] *...  2.78 us
    all_to_all x1, waiting for transfers between devices, local(): squares = lax.all_to_all(everyone, 'tp', 0, 0).reshape(16, R)  2.07 us
  transfers between devices with their start and end apart: 19, of which 12 were waited for; matrix products, arithmetic and copies ran while one was open for 0% of the time, Pallas kernels for 20%

profile of v3, /device:TPU:0, one launch (start us, length us, event | category | flops | bytes accessed | tf_op | source)
XLA Modules:
  0.0 97.4 jit_solution(17765283982944930636)
XLA Ops:
  1.9 6.3 %fusion.partial = f32[1024,256]{1,0:T(8,128)S(1)} fusion(f32[1024,256]{1,0:T(8,128)S(1)} %copy-done, f32[1024,1024]{1,0:T(8,128)} %momentum.3, bf16[1024,1024]{1,0:T(8,128)(2,1)} %gradient.1), kind=kOutput, calls=%fused_computation | convolution fusion | flops 3223322624 | bytes 8388608 | tf_op jit(solution)/shard_map/dot_general | solution.py:96
  8.3 3.2 %collective-permute-start = (f32[256,256]{1,0:T(8,128)S(1)}, f32[256,256]{1,0:T(8,128)S(1)}, u32[]{:S(2)}, u32[]{:S(2)}) collective-permute-start(f32[256,256]{1,0:T(8,128)S(1)} %get-tuple-element.29), channel_id=1, source_target_pairs={{0,2},{1,3},{2,0},{3,1},{4,6},{5,7},{6,4},{7,5},{8,10},{9,11},{10,... | collective-permute-start | bytes 786440 | tf_op jit(solution)/shard_map/ppermute | solution.py:59
  12.1 2.6 %collective-permute-start.2 = (f32[256,256]{1,0:T(8,128)S(1)}, f32[256,256]{1,0:T(8,128)S(1)}, u32[]{:S(2)}, u32[]{:S(2)}) collective-permute-start(f32[256,256]{1,0:T(8,128)S(1)} %get-tuple-element.31), channel_id=1, source_target_pairs={{0,3},{1,0},{2,1},{3,2},{4,7},{5,4},{6,5},{7,6},{8,11},{9,8},{10,9... | collective-permute-start | bytes 786440 | tf_op jit(solution)/shard_map/ppermute | solution.py:59
  14.7 1.5 %collective-permute-done = f32[256,256]{1,0:T(8,128)S(1)} collective-permute-done((f32[256,256]{1,0:T(8,128)S(1)}, f32[256,256]{1,0:T(8,128)S(1)}, u32[]{:S(2)}, u32[]{:S(2)}) %collective-permute-start) | collective-permute-done | bytes 262176 | tf_op jit(solution)/shard_map/ppermute | solution.py:59
  16.3 2.8 %collective-permute-done.1 = f32[256,256]{1,0:T(8,128)S(1)} collective-permute-done((f32[256,256]{1,0:T(8,128)S(1)}, f32[256,256]{1,0:T(8,128)S(1)}, u32[]{:S(2)}, u32[]{:S(2)}) %collective-permute-start.1) | collective-permute-done | bytes 262176 | tf_op jit(solution)/shard_map/ppermute | solution.py:59
  19.3 3.1 %collective-permute-start.5 = (f32[256,256]{1,0:T(8,128)S(1)}, f32[256,256]{1,0:T(8,128)S(1)}, u32[]{:S(2)}, u32[]{:S(2)}) collective-permute-start(f32[256,256]{1,0:T(8,128)S(1)} %add_add_fusion.1), channel_id=1, source_target_pairs={{0,12},{1,13},{2,14},{3,15},{4,0},{5,1},{6,2},{7,3},{8,4},{9,5},{1... | collective-permute-start | bytes 786440 | tf_op jit(solution)/shard_map/ppermute | solution.py:59
  22.4 2.2 %collective-permute-start.3 = (f32[256,256]{1,0:T(8,128)S(1)}, f32[256,256]{1,0:T(8,128)S(1)}, u32[]{:S(2)}, u32[]{:S(2)}) collective-permute-start(f32[256,256]{1,0:T(8,128)S(1)} %add_add_fusion.1), channel_id=1, source_target_pairs={{0,8},{1,9},{2,10},{3,11},{4,12},{5,13},{6,14},{7,15},{8,0},{9,1},... | collective-permute-start | bytes 786440 | tf_op jit(solution)/shard_map/ppermute | solution.py:59
  24.6 1.7 %collective-permute-done.5 = f32[256,256]{1,0:T(8,128)S(1)} collective-permute-done((f32[256,256]{1,0:T(8,128)S(1)}, f32[256,256]{1,0:T(8,128)S(1)}, u32[]{:S(2)}, u32[]{:S(2)}) %collective-permute-start.5) | collective-permute-done | bytes 262176 | tf_op jit(solution)/shard_map/ppermute | solution.py:59
  26.3 6.5 %collective-permute-done.4 = f32[256,256]{1,0:T(8,128)S(1)} collective-permute-done((f32[256,256]{1,0:T(8,128)S(1)}, f32[256,256]{1,0:T(8,128)S(1)}, u32[]{:S(2)}, u32[]{:S(2)}) %collective-permute-start.4) | collective-permute-done | bytes 262176 | tf_op jit(solution)/shard_map/ppermute | solution.py:59
  32.9 2.4 %collective-permute-start.8 = (f32[256,256]{1,0:T(8,128)S(1)}, f32[256,256]{1,0:T(8,128)S(1)}, u32[]{:S(2)}, u32[]{:S(2)}) collective-permute-start(f32[256,256]{1,0:T(8,128)S(1)} %add_add_fusion.refs_2_.own), channel_id=1, source_target_pairs={{0,1},{1,2},{2,3},{3,0},{4,5},{5,6},{6,7},{7,4},{8,9},{9,10},{10,1... | collective-permute-start | bytes 786440 | tf_op jit(solution)/shard_map/ppermute | solution.py:59
  35.3 1.7 %collective-permute-start.7 = (f32[256,256]{1,0:T(8,128)S(1)}, f32[256,256]{1,0:T(8,128)S(1)}, u32[]{:S(2)}, u32[]{:S(2)}) collective-permute-start(f32[256,256]{1,0:T(8,128)S(1)} %add_add_fusion.refs_2_.own), channel_id=1, source_target_pairs={{0,3},{1,0},{2,1},{3,2},{4,7},{5,4},{6,5},{7,6},{8,11},{9,8},{10,9... | collective-permute-start | bytes 786440 | tf_op jit(solution)/shard_map/ppermute | solution.py:59
  39.2 2.0 %collective-permute-done.8.refs_2_.one = f32[256,256]{1,0:T(8,128)S(1)} collective-permute-done((f32[256,256]{1,0:T(8,128)S(1)}, f32[256,256]{1,0:T(8,128)S(1)}, u32[]{:S(2)}, u32[]{:S(2)}) %collective-permute-start.8) | collective-permute-done | bytes 262176 | tf_op jit(solution)/shard_map/ppermute | solution.py:59
  43.0 2.5 %collective-permute-done.6.refs_2_.two = f32[256,256]{1,0:T(8,128)S(1)} collective-permute-done((f32[256,256]{1,0:T(8,128)S(1)}, f32[256,256]{1,0:T(8,128)S(1)}, u32[]{:S(2)}, u32[]{:S(2)}) %collective-permute-start.6) | collective-permute-done | bytes 262176 | tf_op jit(solution)/shard_map/ppermute | solution.py:59
  46.6 2.0 %collective-permute-done.9.got = f32[152,1024]{1,0:T(8,128)S(1)} collective-permute-done((f32[152,1024]{1,0:T(8,128)S(1)}, f32[152,1024]{1,0:T(8,128)S(1)}, u32[]{:S(2)}, u32[]{:S(2)}) %collective-permute-start.9) | collective-permute-done | bytes 622624 | tf_op jit(solution)/shard_map/ppermute | solution.py:59
  48.7 2.0 %collective-permute-start.10 = (f32[56,1024]{1,0:T(8,128)S(1)}, f32[56,1024]{1,0:T(8,128)S(1)}, u32[]{:S(2)}, u32[]{:S(2)}) collective-permute-start(f32[56,1024]{1,0:T(8,128)S(1)} %get-tuple-element.43), channel_id=1, source_target_pairs={{0,32},{1,33},{2,34},{3,35},{4,36},{5,37},{6,38},{7,39},{8,40},{9,... | collective-permute-start | bytes 688136 | tf_op jit(solution)/shard_map/ppermute | solution.py:59
  50.7 3.6 %collective-permute-start.11 = (f32[56,1024]{1,0:T(8,128)S(1)}, f32[56,1024]{1,0:T(8,128)S(1)}, u32[]{:S(2)}, u32[]{:S(2)}) collective-permute-start(f32[56,1024]{1,0:T(8,128)S(1)} %get-tuple-element.44), channel_id=1, source_target_pairs={{0,64},{1,65},{2,66},{3,67},{4,68},{5,69},{6,70},{7,71},{8,72},{9,... | collective-permute-start | bytes 688136 | tf_op jit(solution)/shard_map/ppermute | solution.py:59
  55.3 3.4 %collective-permute-done.10.one = f32[56,1024]{1,0:T(8,128)S(1)} collective-permute-done((f32[56,1024]{1,0:T(8,128)S(1)}, f32[56,1024]{1,0:T(8,128)S(1)}, u32[]{:S(2)}, u32[]{:S(2)}) %collective-permute-start.10) | collective-permute-done | bytes 229408 | tf_op jit(solution)/shard_map/ppermute | solution.py:59
  58.7 6.1 %collective-permute-done.11.two = f32[56,1024]{1,0:T(8,128)S(1)} collective-permute-done((f32[56,1024]{1,0:T(8,128)S(1)}, f32[56,1024]{1,0:T(8,128)S(1)}, u32[]{:S(2)}, u32[]{:S(2)}) %collective-permute-start.11) | collective-permute-done | bytes 229408 | tf_op jit(solution)/shard_map/ppermute | solution.py:59
  65.0 2.2 %collective-permute-start.15 = (f32[32,1024]{1,0:T(8,128)S(1)}, f32[32,1024]{1,0:T(8,128)S(1)}, u32[]{:S(2)}, u32[]{:S(2)}) collective-permute-start(f32[32,1024]{1,0:T(8,128)S(1)} %get-tuple-element.46.after.own), channel_id=1, source_target_pairs={{0,96},{1,97},{2,98},{3,99},{4,100},{5,101},{6,102},{7,103},{8,104... | collective-permute-start | bytes 393224 | tf_op jit(solution)/shard_map/ppermute | solution.py:59
  68.7 9.9 %inverse.1.after = f32[256,256]{1,0:T(8,128)S(1)} custom-call(f32[24,1024]{1,0:T(8,128)S(1)} %get-tuple-element.47.gram, f32[24,1024]{1,0:T(8,128)S(1)} %collective-permute-done.16.other, f32[32,1024]{1,0:T(8,128)S(1)} %get-tuple-element.46.after.own), custom_call_target="tpu_custom_call" | custom-call | flops 1000000000 | bytes 1048576 | tf_op jit(solution)/shard_map/inverse/pallas_call | solution.py:141
  82.7 4.1 %all-to-all-start = ((f32[16,1,256]{2,1,0:T(1,128)}), f32[16,1,256]{2,1,0:T(1,128)S(1)}, u32[]{:S(2)}, u32[]{:S(2)}) async-start(f32[16,1,256]{2,1,0:T(1,128)} %broadcast_in_dim.9), calls=%async_computation | async-start | bytes 32768 | tf_op jit(solution)/shard_map/all_to_all | solution.py:487
  86.8 5.5 %momentum.2 = f32[1024,1024]{1,0:T(8,128)} custom-call(f32[1024,1024]{1,0:T(8,128)} %momentum.3, bf16[1024,1024]{1,0:T(8,128)(2,1)} %gradient.1, f32[1024,256]{1,0:T(8,128)S(1)} %basis.1, bf16[256,1024]{1,0:T(8,128)(2,1)S(1)} %get-tuple-element.49.high, bf16[256,1024]{1,0:T(8,128)(2,1)S(1)} %get-tuple-element.50.low), custom_call_target="tpu_custom_call" | custom-call | flops 3221225472 | bytes 12582912 | tf_op jit(solution)/shard_map/momentum/pallas_call | solution.py:411
  92.3 2.1 %all-to-all-done = f32[16,1,256]{2,1,0:T(1,128)S(1)} async-done(((f32[16,1,256]{2,1,0:T(1,128)}), f32[16,1,256]{2,1,0:T(1,128)S(1)}, u32[]{:S(2)}, u32[]{:S(2)}) %all-to-all-start) | async-done | bytes 16416 | tf_op jit(solution)/shard_map/all_to_all | solution.py:487
  94.4 2.8 %update.1 = (bf16[1024,1024]{1,0:T(8,128)(2,1)}, f32[1024,256]{1,0:T(8,128)}) custom-call(f32[16,256]{1,0:T(8,128)S(1)} %bitcast.5, f32[1024,256]{1,0:T(8,128)S(1)} %basis.1, bf16[256,1024]{1,0:T(8,128)(2,1)S(1)} %get-tuple-element.49.high, bf16[256,1024]{1,0:T(8,128)(2,1)S(1)} %get-tuple-element.50.low), custom_call_target="tpu_custom_call" | custom-call | flops 3221225472 | bytes 6291456 | tf_op jit(solution)/shard_map/update/pallas_call | solution.py:447
  (40 shorter events, 14.0 us)
Async XLA Ops:
  0.6 1.2 %copy-start = (f32[1024,256]{1,0:T(8,128)S(1)}, f32[1024,256]{1,0:T(8,128)}, u32[]{:S(2)}) copy-start(f32[1024,256]{1,0:T(8,128)} %param.5) | copy-start | bytes 3145732
  0.6 37.7 %copy-start.2 = (bf16[1024,1024]{1,0:T(8,128)(2,1)S(1)}, bf16[1024,1024]{1,0:T(8,128)(2,1)}, u32[]{:S(2)}) copy-start(bf16[1024,1024]{1,0:T(8,128)(2,1)} %gradient.1) | copy-start | bytes 6291460
  0.7 37.7 %copy-start.1 = (f32[1024,1024]{1,0:T(8,128)S(1)}, f32[1024,1024]{1,0:T(8,128)}, u32[]{:S(2)}) copy-start(f32[1024,1024]{1,0:T(8,128)} %momentum.3) | copy-start | bytes 12582916
  8.3 8.0 %collective-permute-start = (f32[256,256]{1,0:T(8,128)S(1)}, f32[256,256]{1,0:T(8,128)S(1)}, u32[]{:S(2)}, u32[]{:S(2)}) collective-permute-start(f32[256,256]{1,0:T(8,128)S(1)} %get-tuple-element.29), channel_id=1, source_target_pairs={{0,2},{1,3},{2,0},{3,1},{4,6},{5,7},{6,4},{7,5},{8,10},{9,11},{10,... | collective-permute-start | bytes 786440 | tf_op jit(solution)/shard_map/ppermute | solution.py:59
  11.5 7.6 %collective-permute-start.1 = (f32[256,256]{1,0:T(8,128)S(1)}, f32[256,256]{1,0:T(8,128)S(1)}, u32[]{:S(2)}, u32[]{:S(2)}) collective-permute-start(f32[256,256]{1,0:T(8,128)S(1)} %get-tuple-element.30), channel_id=1, source_target_pairs={{0,1},{1,2},{2,3},{3,0},{4,5},{5,6},{6,7},{7,4},{8,9},{9,10},{10,1... | collective-permute-start | bytes 786440 | tf_op jit(solution)/shard_map/ppermute | solution.py:59
  12.1 7.2 %collective-permute-start.2 = (f32[256,256]{1,0:T(8,128)S(1)}, f32[256,256]{1,0:T(8,128)S(1)}, u32[]{:S(2)}, u32[]{:S(2)}) collective-permute-start(f32[256,256]{1,0:T(8,128)S(1)} %get-tuple-element.31), channel_id=1, source_target_pairs={{0,3},{1,0},{2,1},{3,2},{4,7},{5,4},{6,5},{7,6},{8,11},{9,8},{10,9... | collective-permute-start | bytes 786440 | tf_op jit(solution)/shard_map/ppermute | solution.py:59
  19.3 7.0 %collective-permute-start.5 = (f32[256,256]{1,0:T(8,128)S(1)}, f32[256,256]{1,0:T(8,128)S(1)}, u32[]{:S(2)}, u32[]{:S(2)}) collective-permute-start(f32[256,256]{1,0:T(8,128)S(1)} %add_add_fusion.1), channel_id=1, source_target_pairs={{0,12},{1,13},{2,14},{3,15},{4,0},{5,1},{6,2},{7,3},{8,4},{9,5},{1... | collective-permute-start | bytes 786440 | tf_op jit(solution)/shard_map/ppermute | solution.py:59
  22.4 10.4 %collective-permute-start.4 = (f32[256,256]{1,0:T(8,128)S(1)}, f32[256,256]{1,0:T(8,128)S(1)}, u32[]{:S(2)}, u32[]{:S(2)}) collective-permute-start(f32[256,256]{1,0:T(8,128)S(1)} %add_add_fusion.1), channel_id=1, source_target_pairs={{0,4},{1,5},{2,6},{3,7},{4,8},{5,9},{6,10},{7,11},{8,12},{9,13},{1... | collective-permute-start | bytes 786440 | tf_op jit(solution)/shard_map/ppermute | solution.py:59
  22.4 10.4 %collective-permute-start.3 = (f32[256,256]{1,0:T(8,128)S(1)}, f32[256,256]{1,0:T(8,128)S(1)}, u32[]{:S(2)}, u32[]{:S(2)}) collective-permute-start(f32[256,256]{1,0:T(8,128)S(1)} %add_add_fusion.1), channel_id=1, source_target_pairs={{0,8},{1,9},{2,10},{3,11},{4,12},{5,13},{6,14},{7,15},{8,0},{9,1},... | collective-permute-start | bytes 786440 | tf_op jit(solution)/shard_map/ppermute | solution.py:59
  32.9 8.4 %collective-permute-start.8 = (f32[256,256]{1,0:T(8,128)S(1)}, f32[256,256]{1,0:T(8,128)S(1)}, u32[]{:S(2)}, u32[]{:S(2)}) collective-permute-start(f32[256,256]{1,0:T(8,128)S(1)} %add_add_fusion.refs_2_.own), channel_id=1, source_target_pairs={{0,1},{1,2},{2,3},{3,0},{4,5},{5,6},{6,7},{7,4},{8,9},{9,10},{10,1... | collective-permute-start | bytes 786440 | tf_op jit(solution)/shard_map/ppermute | solution.py:59
  35.3 6.8 %collective-permute-start.7 = (f32[256,256]{1,0:T(8,128)S(1)}, f32[256,256]{1,0:T(8,128)S(1)}, u32[]{:S(2)}, u32[]{:S(2)}) collective-permute-start(f32[256,256]{1,0:T(8,128)S(1)} %add_add_fusion.refs_2_.own), channel_id=1, source_target_pairs={{0,3},{1,0},{2,1},{3,2},{4,7},{5,4},{6,5},{7,6},{8,11},{9,8},{10,9... | collective-permute-start | bytes 786440 | tf_op jit(solution)/shard_map/ppermute | solution.py:59
  36.9 8.5 %collective-permute-start.6 = (f32[256,256]{1,0:T(8,128)S(1)}, f32[256,256]{1,0:T(8,128)S(1)}, u32[]{:S(2)}, u32[]{:S(2)}) collective-permute-start(f32[256,256]{1,0:T(8,128)S(1)} %add_add_fusion.refs_2_.own), channel_id=1, source_target_pairs={{0,2},{1,3},{2,0},{3,1},{4,6},{5,7},{6,4},{7,5},{8,10},{9,11},{10,... | collective-permute-start | bytes 786440 | tf_op jit(solution)/shard_map/ppermute | solution.py:59
  46.5 2.1 %collective-permute-start.9 = (f32[152,1024]{1,0:T(8,128)S(1)}, f32[152,1024]{1,0:T(8,128)S(1)}, u32[]{:S(2)}, u32[]{:S(2)}) collective-permute-start(f32[152,1024]{1,0:T(8,128)S(1)} %get-tuple-element.41), channel_id=1, source_target_pairs={{0,16},{1,17},{2,18},{3,19},{4,20},{5,21},{6,22},{7,23},{8,24},{9,... | collective-permute-start | bytes 1867784 | tf_op jit(solution)/shard_map/ppermute | solution.py:59
  48.7 10.0 %collective-permute-start.10 = (f32[56,1024]{1,0:T(8,128)S(1)}, f32[56,1024]{1,0:T(8,128)S(1)}, u32[]{:S(2)}, u32[]{:S(2)}) collective-permute-start(f32[56,1024]{1,0:T(8,128)S(1)} %get-tuple-element.43), channel_id=1, source_target_pairs={{0,32},{1,33},{2,34},{3,35},{4,36},{5,37},{6,38},{7,39},{8,40},{9,... | collective-permute-start | bytes 688136 | tf_op jit(solution)/shard_map/ppermute | solution.py:59
  50.7 14.1 %collective-permute-start.11 = (f32[56,1024]{1,0:T(8,128)S(1)}, f32[56,1024]{1,0:T(8,128)S(1)}, u32[]{:S(2)}, u32[]{:S(2)}) collective-permute-start(f32[56,1024]{1,0:T(8,128)S(1)} %get-tuple-element.44), channel_id=1, source_target_pairs={{0,64},{1,65},{2,66},{3,67},{4,68},{5,69},{6,70},{7,71},{8,72},{9,... | collective-permute-start | bytes 688136 | tf_op jit(solution)/shard_map/ppermute | solution.py:59
  54.3 10.5 %collective-permute-start.12 = (f32[56,1024]{1,0:T(8,128)S(1)}, f32[56,1024]{1,0:T(8,128)S(1)}, u32[]{:S(2)}, u32[]{:S(2)}) collective-permute-start(f32[56,1024]{1,0:T(8,128)S(1)} %get-tuple-element.45), channel_id=1, source_target_pairs={{0,96},{1,97},{2,98},{3,99},{4,100},{5,101},{6,102},{7,103},{8,104... | collective-permute-start | bytes 688136 | tf_op jit(solution)/shard_map/ppermute | solution.py:59
  64.9 3.8 %collective-permute-start.16 = (f32[24,1024]{1,0:T(8,128)S(1)}, f32[24,1024]{1,0:T(8,128)S(1)}, u32[]{:S(2)}, u32[]{:S(2)}) collective-permute-start(f32[24,1024]{1,0:T(8,128)S(1)} %get-tuple-element.47.gram), channel_id=1, source_target_pairs={{0,16},{1,17},{2,18},{3,19},{4,20},{5,21},{6,22},{7,23},{8,24},{9,... | collective-permute-start | bytes 294920 | tf_op jit(solution)/shard_map/ppermute | solution.py:59
  65.0 13.6 %collective-permute-start.15 = (f32[32,1024]{1,0:T(8,128)S(1)}, f32[32,1024]{1,0:T(8,128)S(1)}, u32[]{:S(2)}, u32[]{:S(2)}) collective-permute-start(f32[32,1024]{1,0:T(8,128)S(1)} %get-tuple-element.46.after.own), channel_id=1, source_target_pairs={{0,96},{1,97},{2,98},{3,99},{4,100},{5,101},{6,102},{7,103},{8,104... | collective-permute-start | bytes 393224 | tf_op jit(solution)/shard_map/ppermute | solution.py:59
  67.2 11.4 %collective-permute-start.14 = (f32[32,1024]{1,0:T(8,128)S(1)}, f32[32,1024]{1,0:T(8,128)S(1)}, u32[]{:S(2)}, u32[]{:S(2)}) collective-permute-start(f32[32,1024]{1,0:T(8,128)S(1)} %get-tuple-element.46.after.own), channel_id=1, source_target_pairs={{0,64},{1,65},{2,66},{3,67},{4,68},{5,69},{6,70},{7,71},{8,72},{9,... | collective-permute-start | bytes 393224 | tf_op jit(solution)/shard_map/ppermute | solution.py:59
  68.3 10.3 %collective-permute-start.13 = (f32[32,1024]{1,0:T(8,128)S(1)}, f32[32,1024]{1,0:T(8,128)S(1)}, u32[]{:S(2)}, u32[]{:S(2)}) collective-permute-start(f32[32,1024]{1,0:T(8,128)S(1)} %get-tuple-element.46.after.own), channel_id=1, source_target_pairs={{0,32},{1,33},{2,34},{3,35},{4,36},{5,37},{6,38},{7,39},{8,40},{9,... | collective-permute-start | bytes 393224 | tf_op jit(solution)/shard_map/ppermute | solution.py:59
  78.7 2.0 %collective-permute-start.17 = (f32[128,1024]{1,0:T(8,128)S(1)}, f32[128,1024]{1,0:T(8,128)S(1)}, u32[]{:S(2)}, u32[]{:S(2)}) collective-permute-start(f32[128,1024]{1,0:T(8,128)S(1)} %ordered.1.half), channel_id=1, source_target_pairs={{0,16},{1,17},{2,18},{3,19},{4,20},{5,21},{6,22},{7,23},{8,24},{9,... | collective-permute-start | bytes 1572872 | tf_op jit(solution)/shard_map/ppermute | solution.py:59
  82.7 11.7 %all-to-all-start = ((f32[16,1,256]{2,1,0:T(1,128)}), f32[16,1,256]{2,1,0:T(1,128)S(1)}, u32[]{:S(2)}, u32[]{:S(2)}) async-start(f32[16,1,256]{2,1,0:T(1,128)} %broadcast_in_dim.9), calls=%async_computation | async-start | bytes 32768 | tf_op jit(solution)/shard_map/all_to_all | solution.py:487

commit v4 on v3

--- a/solution.py
+++ b/solution.py
@@ -62,6 +62,10 @@
 def to_three(parts, where):
     two, one, three = [send(parts[k], where(k)) for k in (2, 1, 3)]
     return one, two, three
+
+
+def to_all(part, where):
+    return to_three([part] * 4, where)
 
 
 def sum_four(own, one, two, three):
@@ -227,111 +231,114 @@
 
 def spread_kernel(keep, got, *refs):
     z = place()[0]
-    parts, total = refs[:4], refs[4]
+    parts, gram, total = refs[:4], refs[4], refs[5]
     total[...] = keep[...] + got[...]
     for k in range(4):
-        parts[k][:Z_ROWS] = total[span(ahead(z, k), Z_ROWS)]
-        parts[k][Z_ROWS:] = total[HALF:]
+        parts[k][...] = total[span(ahead(z, k), Z_ROWS)]
+    gram[...] = total[HALF:]
 
 
 def spread(keep, got):
     return call(
         spread_kernel,
         "spread",
-        [((Z_ROWS + GRAM_ROWS, BLOCK), f32)] * 4,
+        [((Z_ROWS, BLOCK), f32)] * 4 + [((GRAM_ROWS, BLOCK), f32)],
         scratch_shapes=[pltpu.VMEM((CORE_ROWS, BLOCK), f32)],
     )(keep, got)
 
 
-def settle_kernel(own, one, two, three, cross, gram):
-    total = sum_four(own[...], one[...], two[...], three[...])
-    cross[...], gram[...] = total[:Z_ROWS], total[Z_ROWS:]
-
-
-def settle(*parts):
-    return call(
-        settle_kernel, "settle", [((Z_ROWS, BLOCK), f32), ((GRAM_ROWS, BLOCK), f32)]
-    )(*parts)
-
-
-GROUP = 8
-
-
-def block_inverse(block):
-    tiles, width = B // 8, 2 * B
-    lane = lax.broadcasted_iota(jnp.int32, (8, width), 1)
-    sub = lax.broadcasted_iota(jnp.int32, (8, width), 0)
-    wide = jnp.concatenate([block, jnp.zeros_like(block)], axis=1)
-    a = [wide[8 * t : 8 * t + 8] + (lane == sub + 8 * t + B).astype(f32) for t in range(tiles)]
-    for start in range(0, B, GROUP):
-        top = start // 8
-        left = tiles - top
-        columns = [
-            [
-                jnp.broadcast_to(a[t][:, start + c : start + c + 1], (8, width))
-                for t in range(top, tiles)
-            ]
-            for c in range(GROUP)
-        ]
-        for c in range(GROUP):
-            pivot = jnp.broadcast_to(columns[c][0][c : c + 1, :], (8, width))
-            scale = 1.0 / pivot
-            factor = [columns[c][t] * scale for t in range(left)]
-            factor[0] = jnp.where(sub > c, factor[0], 0.0)
-            for later in range(c + 1, GROUP):
-                value = jnp.broadcast_to(columns[later][0][c : c + 1, :], (8, width))
-                for t in range(left):
-                    columns[later][t] = columns[later][t] - factor[t] * value
-            row = jnp.broadcast_to(a[top][c : c + 1, :], (8, width))
-            for t in range(left):
-                a[top + t] = a[top + t] - factor[t] * row
+def lower_inverse(block):
+    lane = lax.broadcasted_iota(jnp.int32, (8, HALF), 1)
+    sub = lax.broadcasted_iota(jnp.int32, (8, HALF), 0)
+
+    def column(value, k):
+        return jnp.broadcast_to(value[:, k : k + 1], (8, HALF))
+
+    def row(value, k):
+        return jnp.broadcast_to(value[k : k + 1, :], (8, HALF))
+
+    tiles = HALF // 8
+    a = [block[8 * t : 8 * t + 8] for t in range(tiles)]
+    scales = []
+    later = [column(a[0], c) for c in range(8)]
+    for t in range(tiles):
+        start = 8 * t
+        diagonal, factors, inverses, upper = later, {}, [], {}
+        if t + 1 < tiles:
+            below = [column(a[t + 1], start + c) for c in range(8)]
+            later = [column(a[t + 1], start + 8 + c) for c in range(8)]
+        own, scale = [], None
+        for c in range(8):
+            inverse = 1.0 / row(diagonal[c], c)
+            inverses.append(inverse)
+            scale = inverse if c == 0 else jnp.where(sub == c, inverse, scale)
+            own.append(jnp.where(sub > c, diagonal[c], 0.0))
+            for d in range(c + 1, 8):
+                upper[c, d] = row(diagonal[d], c) * inverse
+                diagonal[d] = diagonal[d] - own[c] * upper[c, d]
+        scales.append(scale)
+        if t + 1 < tiles:
+            factors[t + 1] = []
+            for c in range(8):
+                factors[t + 1].append(below[c])
+                for d in range(c + 1, 8):
+                    below[d] = below[d] - below[c] * upper[c, d]
+                scaled = below[c] * inverses[c]
+                for d in range(8):
+                    later[d] = later[d] - below[c] * row(scaled, d)
+        value, rows = a[t], []
+        for c in range(8):
+            line = jnp.where(lane == start + c, 1.0, row(value, c)) * inverses[c]
+            value = jnp.where((lane == start + c) & (sub > c), 0.0, value) - own[c] * line
+            rows.append(jnp.where((lane > start + c) & (lane < start + 8), 0.0, line))
+        a[t] = value
+        group = (lane >= start) & (lane < start + 8)
+        for n in range(t + 1, tiles):
+            if n not in factors:
+                columns, factors[n] = [column(a[n], start + c) for c in range(8)], []
+                for c in range(8):
+                    factors[n].append(columns[c])
+                    for d in range(c + 1, 8):
+                        columns[d] = columns[d] - columns[c] * upper[c, d]
+            total = jnp.where(group, 0.0, a[n])
+            for c in range(8):
+                total = total - factors[n][c] * rows[c]
+            a[n] = total
     out = []
     for t in range(tiles):
-        pivots = jnp.sum(jnp.where(lane == sub + 8 * t, a[t], 0.0), axis=1, keepdims=True)
-        out.append(a[t][:, B:] * lax.rsqrt(pivots))
+        unit = jnp.where(lane == sub + 8 * t, 1.0, jnp.where(lane < sub + 8 * t, a[t], 0.0))
+        out.append(unit * jnp.sqrt(scales[t]))
     return jnp.concatenate(out, 0)
 
 
-def eliminate(work, out, blocks, shift):
-    for n in blocks:
-        low, high = n * B, n * B + B
-        inverse = block_inverse(work[low - shift : high - shift, low:high])
-        rows = dot(inverse, work[low - shift : high - shift, :], precision=highest)
-        out[low:high, :] = rows[:, R:]
-        if high < R:
-            work[high - shift :, :] = work[high - shift :, :] - dot(
-                rows[:, high:R], rows, ((0,), (0,)), precision=highest
-            )
-
-
-def identity_rows(low, high):
-    row = lax.broadcasted_iota(jnp.int32, (high - low, R), 0) + low
-    return (row == lax.broadcasted_iota(jnp.int32, (high - low, R), 1)).astype(f32)
-
-
-def inverse_kernel(gram, other, after, out, work, packed):
+def inverse_kernel(gram, other, out, work, packed):
     core = place()[1]
     packed[span(core, GRAM_ROWS)] = gram[...]
     packed[span(1 - core, GRAM_ROWS)] = other[...]
     for top, left, width, row, column in packed_pieces():
         work[row : row + 8, column : column + width] = packed[top : top + 8, left : left + width]
-    work[HALF:, :HALF] = jnp.zeros((HALF, HALF), f32)
-    work[:, R:] = identity_rows(0, R)
-    eliminate(work, out, range(R // B), 0)
-
-
-def inverse_factor(gram, other, after):
+    first = lower_inverse(work[:HALF, :HALF])
+    right = dot(first, work[:HALF, HALF:], precision=highest)
+    schur = work[HALF:, HALF:] - dot(right, right, ((0,), (0,)), precision=highest)
+    corner = dot(right, first, ((0,), (0,)), precision=highest)
+    second = lower_inverse(schur)
+    out[:HALF, :HALF] = first
+    out[:HALF, HALF:] = jnp.zeros((HALF, HALF), f32)
+    out[HALF:, :HALF] = -dot(second, corner, precision=highest)
+    out[HALF:, HALF:] = second
+
+
+def inverse_factor(gram, other):
     return call(
         inverse_kernel,
         "inverse",
         [((R, R), f32)],
         10**9,
-        in_specs=[vmem(), vmem(), anywhere()],
-        scratch_shapes=[pltpu.VMEM((R, 2 * R), f32), pltpu.VMEM((2 * GRAM_ROWS, BLOCK), f32)],
-    )(gram, other, after)[0]
-
-
-def ordered_kernel(own, one, two, three, after, out):
+        scratch_shapes=[pltpu.VMEM((R, R), f32), pltpu.VMEM((2 * GRAM_ROWS, BLOCK), f32)],
+    )(gram, other)[0]
+
+
+def ordered_kernel(own, three, one, two, after, out):
     z = place()[0]
     for k, part in enumerate((own, one, two, three)):
         out[span(ahead(z, 4 - k), Z_ROWS)] = part[...]
@@ -343,7 +350,7 @@
         "ordered",
         [((HALF, BLOCK), f32)],
         in_specs=[vmem()] * 4 + [anywhere()],
-    )(*parts, after)[0]
+    )(parts[0], parts[3], parts[1], parts[2], after)[0]
 
 
 def basis_kernel(own, one, two, three, inverse, basis):
@@ -469,18 +476,21 @@
     partial = dot(buffer, basis_prev, precision=highest)
     parts = quarters(partial)
     quarter = sum_four(parts[0], *to_three(parts, first_axis))
-    quarter = sum_four(quarter, *to_three([quarter] * 4, second_axis))
-    parts = [quarter, *to_three([quarter] * 4, first_axis)]
+    one, two, three = to_all(quarter, second_axis)
+    quarter = (three + one) + (two + quarter)
+    parts = [quarter, *to_all(quarter, first_axis)]
 
     sums = ()
-    for k in (0, 1, 3, 2):
+    for k in (0, 2, 1, 3):
         sums = crossed_share(k, momentum, gradient, parts[k], sums)
 
     keep, give = depart(*sums)
-    shares = spread(keep, send(give, other_core))
-    crossed, gram = settle(shares[0], *to_three(shares, along_z))
-    inverse = inverse_factor(gram, send(gram, other_core), crossed)
-    half = ordered([crossed, *to_three([crossed] * 4, along_z)], inverse)
+    *shares, gram = spread(keep, send(give, other_core))
+    crossed = sum_four(shares[0], *to_three(shares, along_z))
+    one, two, three = to_all(gram, along_z)
+    gram = (three + one) + (two + gram)
+    inverse = inverse_factor(gram, send(gram, other_core))
+    half = ordered([crossed, *to_all(crossed, along_z)], inverse)
     basis = form_basis(parts, inverse)
     high, low, squares = form_reduced(half, send(half, other_core), inverse)
     everyone = jnp.broadcast_to(squares[None, :1], (16, 1, R))

time: 97.5 us -> 93.2 us (0.956)
  waiting for transfers between devices: 31.7 us -> 22.4 us
  starting transfers between devices: 31.9 us -> 40.7 us
  Pallas kernels: 24.4 us -> 20.6 us
    ppermute x18 -> x21, waiting for transfers between devices: 29.6 us -> 20.3 us  [send(): return lax.ppermute(value, both, where)]
    ppermute x18 -> x21, starting transfers between devices: 27.7 us -> 34.7 us  [send(): return lax.ppermute(value, both, where)]
    pallas_call x12 -> x11, Pallas kernels: 16.2 us -> 12.3 us  [run(): pl.pallas_call(kernel, in_specs=in_specs or [vmem()] * len(operands), out...]
    all_to_all x1, starting transfers between devices: 4.14 us -> 5.98 us  [local(): squares = lax.all_to_all(everyone, 'tp', 0, 0).reshape(16, R)]
  transfers between devices with their start and end apart: 19 -> 22, of which waited for: 12 -> 14; matrix products, arithmetic and copies ran while one was open for 0% -> 0% of each run, Pallas kernels for 20% -> 16%
where the time goes in v4:
time: 93.2 us; the launch traced here: 93 us
  starting transfers between devices  40.7 us (44%)
  waiting for transfers between devices  22.4 us (24%)
  Pallas kernels  20.6 us (22%)
  matrix products  6.33 us (7%)
  local copies, waits for them, and re-layouts  1.84 us (2%)
  between operations  1.03 us (1%)
    ppermute x21, starting transfers between devices, send(): return lax.ppermute(value, both, where)  34.7 us
    ppermute x21, waiting for transfers between devices, send(): return lax.ppermute(value, both, where)  20.3 us
    pallas_call x11, Pallas kernels, run(): pl.pallas_call(kernel, in_specs=in_specs or [vmem()] * len(operands), out...  12.3 us
    dot_general x1, matrix products, dot(): lax.dot_general(left, right, (dims, ((), ())), precision=precision, prefe...  6.33 us
    all_to_all x1, starting transfers between devices, local(): squares = lax.all_to_all(everyone, 'tp', 0, 0).reshape(16, R)  5.98 us
    pallas_call x1, Pallas kernels, form_momentum(): pl.pallas_call(momentum_kernel, in_specs=[hbm()] * 2 + [vmem()] * 3, out_...  5.5 us
    pallas_call x1, Pallas kernels, form_update(): pl.pallas_call(update_kernel, in_specs=[vmem()] * 4, out_specs=[hbm()] *...  2.78 us
    all_to_all x1, waiting for transfers between devices, local(): squares = lax.all_to_all(everyone, 'tp', 0, 0).reshape(16, R)  2.07 us
  transfers between devices with their start and end apart: 22, of which 14 were waited for; matrix products, arithmetic and copies ran while one was open for 0% of the time, Pallas kernels for 16%

profile of v4, /device:TPU:0, one launch (start us, length us, event | category | flops | bytes accessed | tf_op | source)
XLA Modules:
  0.0 93.0 jit_solution(4229773682011069553)
XLA Ops:
  1.9 6.3 %fusion.partial = f32[1024,256]{1,0:T(8,128)S(1)} fusion(f32[1024,256]{1,0:T(8,128)S(1)} %copy-done, f32[1024,1024]{1,0:T(8,128)} %momentum.3, bf16[1024,1024]{1,0:T(8,128)(2,1)} %gradient.1), kind=kOutput, calls=%fused_computation | convolution fusion | flops 3223322624 | bytes 8388608 | tf_op jit(solution)/shard_map/dot_general | solution.py:100
  8.3 3.2 %collective-permute-start = (f32[256,256]{1,0:T(8,128)S(1)}, f32[256,256]{1,0:T(8,128)S(1)}, u32[]{:S(2)}, u32[]{:S(2)}) collective-permute-start(f32[256,256]{1,0:T(8,128)S(1)} %get-tuple-element.28), channel_id=1, source_target_pairs={{0,2},{1,3},{2,0},{3,1},{4,6},{5,7},{6,4},{7,5},{8,10},{9,11},{10,... | collective-permute-start | bytes 786440 | tf_op jit(solution)/shard_map/ppermute | solution.py:59
  12.1 2.6 %collective-permute-start.2 = (f32[256,256]{1,0:T(8,128)S(1)}, f32[256,256]{1,0:T(8,128)S(1)}, u32[]{:S(2)}, u32[]{:S(2)}) collective-permute-start(f32[256,256]{1,0:T(8,128)S(1)} %get-tuple-element.30), channel_id=1, source_target_pairs={{0,3},{1,0},{2,1},{3,2},{4,7},{5,4},{6,5},{7,6},{8,11},{9,8},{10,9... | collective-permute-start | bytes 786440 | tf_op jit(solution)/shard_map/ppermute | solution.py:59
  14.7 1.5 %collective-permute-done = f32[256,256]{1,0:T(8,128)S(1)} collective-permute-done((f32[256,256]{1,0:T(8,128)S(1)}, f32[256,256]{1,0:T(8,128)S(1)}, u32[]{:S(2)}, u32[]{:S(2)}) %collective-permute-start) | collective-permute-done | bytes 262176 | tf_op jit(solution)/shard_map/ppermute | solution.py:59
  16.3 2.8 %collective-permute-done.1 = f32[256,256]{1,0:T(8,128)S(1)} collective-permute-done((f32[256,256]{1,0:T(8,128)S(1)}, f32[256,256]{1,0:T(8,128)S(1)}, u32[]{:S(2)}, u32[]{:S(2)}) %collective-permute-start.1) | collective-permute-done | bytes 262176 | tf_op jit(solution)/shard_map/ppermute | solution.py:59
  19.3 3.3 %collective-permute-start.5 = (f32[256,256]{1,0:T(8,128)S(1)}, f32[256,256]{1,0:T(8,128)S(1)}, u32[]{:S(2)}, u32[]{:S(2)}) collective-permute-start(f32[256,256]{1,0:T(8,128)S(1)} %add_add_fusion.1), channel_id=1, source_target_pairs={{0,8},{1,9},{2,10},{3,11},{4,12},{5,13},{6,14},{7,15},{8,0},{9,1},... | collective-permute-start | bytes 786440 | tf_op jit(solution)/shard_map/ppermute | solution.py:59
  23.3 2.6 %collective-permute-start.3 = (f32[256,256]{1,0:T(8,128)S(1)}, f32[256,256]{1,0:T(8,128)S(1)}, u32[]{:S(2)}, u32[]{:S(2)}) collective-permute-start(f32[256,256]{1,0:T(8,128)S(1)} %add_add_fusion.1), channel_id=1, source_target_pairs={{0,12},{1,13},{2,14},{3,15},{4,0},{5,1},{6,2},{7,3},{8,4},{9,5},{1... | collective-permute-start | bytes 786440 | tf_op jit(solution)/shard_map/ppermute | solution.py:59
  27.3 2.9 %collective-permute-done.4 = f32[256,256]{1,0:T(8,128)S(1)} collective-permute-done((f32[256,256]{1,0:T(8,128)S(1)}, f32[256,256]{1,0:T(8,128)S(1)}, u32[]{:S(2)}, u32[]{:S(2)}) %collective-permute-start.4) | collective-permute-done | bytes 262176 | tf_op jit(solution)/shard_map/ppermute | solution.py:59
  30.5 2.2 %collective-permute-start.8 = (f32[256,256]{1,0:T(8,128)S(1)}, f32[256,256]{1,0:T(8,128)S(1)}, u32[]{:S(2)}, u32[]{:S(2)}) collective-permute-start(f32[256,256]{1,0:T(8,128)S(1)} %add_add_fusion.refs_2_.own), channel_id=1, source_target_pairs={{0,2},{1,3},{2,0},{3,1},{4,6},{5,7},{6,4},{7,5},{8,10},{9,11},{10,... | collective-permute-start | bytes 786440 | tf_op jit(solution)/shard_map/ppermute | solution.py:59
  32.6 1.9 %collective-permute-start.7 = (f32[256,256]{1,0:T(8,128)S(1)}, f32[256,256]{1,0:T(8,128)S(1)}, u32[]{:S(2)}, u32[]{:S(2)}) collective-permute-start(f32[256,256]{1,0:T(8,128)S(1)} %add_add_fusion.refs_2_.own), channel_id=1, source_target_pairs={{0,1},{1,2},{2,3},{3,0},{4,5},{5,6},{6,7},{7,4},{8,9},{9,10},{10,1... | collective-permute-start | bytes 786440 | tf_op jit(solution)/shard_map/ppermute | solution.py:59
  36.7 1.8 %collective-permute-done.8.refs_2_.two = f32[256,256]{1,0:T(8,128)S(1)} collective-permute-done((f32[256,256]{1,0:T(8,128)S(1)}, f32[256,256]{1,0:T(8,128)S(1)}, u32[]{:S(2)}, u32[]{:S(2)}) %collective-permute-start.8) | collective-permute-done | bytes 262176 | tf_op jit(solution)/shard_map/ppermute | solution.py:59
  39.4 1.8 %collective-permute-done.7.refs_2_.one = f32[256,256]{1,0:T(8,128)S(1)} collective-permute-done((f32[256,256]{1,0:T(8,128)S(1)}, f32[256,256]{1,0:T(8,128)S(1)}, u32[]{:S(2)}, u32[]{:S(2)}) %collective-permute-start.7) | collective-permute-done | bytes 262176 | tf_op jit(solution)/shard_map/ppermute | solution.py:59
  43.2 2.0 %collective-permute-done.9.got = f32[152,1024]{1,0:T(8,128)S(1)} collective-permute-done((f32[152,1024]{1,0:T(8,128)S(1)}, f32[152,1024]{1,0:T(8,128)S(1)}, u32[]{:S(2)}, u32[]{:S(2)}) %collective-permute-start.9) | collective-permute-done | bytes 622624 | tf_op jit(solution)/shard_map/ppermute | solution.py:59
  45.4 4.0 %collective-permute-start.18 = (f32[24,1024]{1,0:T(8,128)S(1)}, f32[24,1024]{1,0:T(8,128)S(1)}, u32[]{:S(2)}, u32[]{:S(2)}) collective-permute-start(f32[24,1024]{1,0:T(8,128)S(1)} %get-tuple-element.45), channel_id=1, source_target_pairs={{0,64},{1,65},{2,66},{3,67},{4,68},{5,69},{6,70},{7,71},{8,72},{9,... | collective-permute-start | bytes 294920 | tf_op jit(solution)/shard_map/ppermute | solution.py:59
  50.4 2.2 %collective-permute-start.16 = (f32[24,1024]{1,0:T(8,128)S(1)}, f32[24,1024]{1,0:T(8,128)S(1)}, u32[]{:S(2)}, u32[]{:S(2)}) collective-permute-start(f32[24,1024]{1,0:T(8,128)S(1)} %get-tuple-element.45), channel_id=1, source_target_pairs={{0,96},{1,97},{2,98},{3,99},{4,100},{5,101},{6,102},{7,103},{8,104... | collective-permute-start | bytes 294920 | tf_op jit(solution)/shard_map/ppermute | solution.py:59
  53.4 3.1 %collective-permute-start.12 = (f32[32,1024]{1,0:T(8,128)S(1)}, f32[32,1024]{1,0:T(8,128)S(1)}, u32[]{:S(2)}, u32[]{:S(2)}) collective-permute-start(f32[32,1024]{1,0:T(8,128)S(1)} %get-tuple-element.44), channel_id=1, source_target_pairs={{0,96},{1,97},{2,98},{3,99},{4,100},{5,101},{6,102},{7,103},{8,104... | collective-permute-start | bytes 393224 | tf_op jit(solution)/shard_map/ppermute | solution.py:59
  57.1 3.1 %collective-permute-done.10 = f32[32,1024]{1,0:T(8,128)S(1)} collective-permute-done((f32[32,1024]{1,0:T(8,128)S(1)}, f32[32,1024]{1,0:T(8,128)S(1)}, u32[]{:S(2)}, u32[]{:S(2)}) %collective-permute-start.10) | collective-permute-done | bytes 131104 | tf_op jit(solution)/shard_map/ppermute | solution.py:59
  61.3 1.8 %collective-permute-start.15 = (f32[32,1024]{1,0:T(8,128)S(1)}, f32[32,1024]{1,0:T(8,128)S(1)}, u32[]{:S(2)}, u32[]{:S(2)}) collective-permute-start(f32[32,1024]{1,0:T(8,128)S(1)} %add_add_fusion.2.own), channel_id=1, source_target_pairs={{0,64},{1,65},{2,66},{3,67},{4,68},{5,69},{6,70},{7,71},{8,72},{9,... | collective-permute-start | bytes 393224 | tf_op jit(solution)/shard_map/ppermute | solution.py:59
  63.1 1.8 %collective-permute-start.14 = (f32[32,1024]{1,0:T(8,128)S(1)}, f32[32,1024]{1,0:T(8,128)S(1)}, u32[]{:S(2)}, u32[]{:S(2)}) collective-permute-start(f32[32,1024]{1,0:T(8,128)S(1)} %add_add_fusion.2.own), channel_id=1, source_target_pairs={{0,32},{1,33},{2,34},{3,35},{4,36},{5,37},{6,38},{7,39},{8,40},{9,... | collective-permute-start | bytes 393224 | tf_op jit(solution)/shard_map/ppermute | solution.py:59
  66.3 6.1 %inverse.1.after = f32[256,256]{1,0:T(8,128)S(1)} custom-call(f32[24,1024]{1,0:T(8,128)S(1)} %add_add_fusion.3.gram, f32[24,1024]{1,0:T(8,128)S(1)} %collective-permute-done.19.other), custom_call_target="tpu_custom_call" | custom-call | flops 1000000000 | bytes 1048576 | tf_op jit(solution)/shard_map/inverse/pallas_call | solution.py:145
  76.5 6.0 %all-to-all-start = ((f32[16,1,256]{2,1,0:T(1,128)}), f32[16,1,256]{2,1,0:T(1,128)S(1)}, u32[]{:S(2)}, u32[]{:S(2)}) async-start(f32[16,1,256]{2,1,0:T(1,128)} %broadcast_in_dim.9), calls=%async_computation | async-start | bytes 32768 | tf_op jit(solution)/shard_map/all_to_all | solution.py:497
  82.5 5.5 %momentum.2 = f32[1024,1024]{1,0:T(8,128)} custom-call(f32[1024,1024]{1,0:T(8,128)} %momentum.3, bf16[1024,1024]{1,0:T(8,128)(2,1)} %gradient.1, f32[1024,256]{1,0:T(8,128)S(1)} %basis.1, bf16[256,1024]{1,0:T(8,128)(2,1)S(1)} %get-tuple-element.47.high, bf16[256,1024]{1,0:T(8,128)(2,1)S(1)} %get-tuple-element.48.low), custom_call_target="tpu_custom_call" | custom-call | flops 3221225472 | bytes 12582912 | tf_op jit(solution)/shard_map/momentum/pallas_call | solution.py:418
  88.0 2.1 %all-to-all-done = f32[16,1,256]{2,1,0:T(1,128)S(1)} async-done(((f32[16,1,256]{2,1,0:T(1,128)}), f32[16,1,256]{2,1,0:T(1,128)S(1)}, u32[]{:S(2)}, u32[]{:S(2)}) %all-to-all-start) | async-done | bytes 16416 | tf_op jit(solution)/shard_map/all_to_all | solution.py:497
  90.1 2.8 %update.1 = (bf16[1024,1024]{1,0:T(8,128)(2,1)}, f32[1024,256]{1,0:T(8,128)}) custom-call(f32[16,256]{1,0:T(8,128)S(1)} %bitcast.5, f32[1024,256]{1,0:T(8,128)S(1)} %basis.1, bf16[256,1024]{1,0:T(8,128)(2,1)S(1)} %get-tuple-element.47.high, bf16[256,1024]{1,0:T(8,128)(2,1)S(1)} %get-tuple-element.48.low), custom_call_target="tpu_custom_call" | custom-call | flops 3221225472 | bytes 6291456 | tf_op jit(solution)/shard_map/update/pallas_call | solution.py:454
  (47 shorter events, 18.7 us)
Async XLA Ops:
  0.6 35.2 %copy-start.2 = (bf16[1024,1024]{1,0:T(8,128)(2,1)S(1)}, bf16[1024,1024]{1,0:T(8,128)(2,1)}, u32[]{:S(2)}) copy-start(bf16[1024,1024]{1,0:T(8,128)(2,1)} %gradient.1) | copy-start | bytes 6291460
  0.7 35.2 %copy-start.1 = (f32[1024,1024]{1,0:T(8,128)S(1)}, f32[1024,1024]{1,0:T(8,128)}, u32[]{:S(2)}) copy-start(f32[1024,1024]{1,0:T(8,128)} %momentum.3) | copy-start | bytes 12582916
  8.3 8.0 %collective-permute-start = (f32[256,256]{1,0:T(8,128)S(1)}, f32[256,256]{1,0:T(8,128)S(1)}, u32[]{:S(2)}, u32[]{:S(2)}) collective-permute-start(f32[256,256]{1,0:T(8,128)S(1)} %get-tuple-element.28), channel_id=1, source_target_pairs={{0,2},{1,3},{2,0},{3,1},{4,6},{5,7},{6,4},{7,5},{8,10},{9,11},{10,... | collective-permute-start | bytes 786440 | tf_op jit(solution)/shard_map/ppermute | solution.py:59
  11.5 7.6 %collective-permute-start.1 = (f32[256,256]{1,0:T(8,128)S(1)}, f32[256,256]{1,0:T(8,128)S(1)}, u32[]{:S(2)}, u32[]{:S(2)}) collective-permute-start(f32[256,256]{1,0:T(8,128)S(1)} %get-tuple-element.29), channel_id=1, source_target_pairs={{0,1},{1,2},{2,3},{3,0},{4,5},{5,6},{6,7},{7,4},{8,9},{9,10},{10,1... | collective-permute-start | bytes 786440 | tf_op jit(solution)/shard_map/ppermute | solution.py:59
  12.1 7.2 %collective-permute-start.2 = (f32[256,256]{1,0:T(8,128)S(1)}, f32[256,256]{1,0:T(8,128)S(1)}, u32[]{:S(2)}, u32[]{:S(2)}) collective-permute-start(f32[256,256]{1,0:T(8,128)S(1)} %get-tuple-element.30), channel_id=1, source_target_pairs={{0,3},{1,0},{2,1},{3,2},{4,7},{5,4},{6,5},{7,6},{8,11},{9,8},{10,9... | collective-permute-start | bytes 786440 | tf_op jit(solution)/shard_map/ppermute | solution.py:59
  19.3 8.0 %collective-permute-start.5 = (f32[256,256]{1,0:T(8,128)S(1)}, f32[256,256]{1,0:T(8,128)S(1)}, u32[]{:S(2)}, u32[]{:S(2)}) collective-permute-start(f32[256,256]{1,0:T(8,128)S(1)} %add_add_fusion.1), channel_id=1, source_target_pairs={{0,8},{1,9},{2,10},{3,11},{4,12},{5,13},{6,14},{7,15},{8,0},{9,1},... | collective-permute-start | bytes 786440 | tf_op jit(solution)/shard_map/ppermute | solution.py:59
  22.6 7.6 %collective-permute-start.4 = (f32[256,256]{1,0:T(8,128)S(1)}, f32[256,256]{1,0:T(8,128)S(1)}, u32[]{:S(2)}, u32[]{:S(2)}) collective-permute-start(f32[256,256]{1,0:T(8,128)S(1)} %add_add_fusion.1), channel_id=1, source_target_pairs={{0,4},{1,5},{2,6},{3,7},{4,8},{5,9},{6,10},{7,11},{8,12},{9,13},{1... | collective-permute-start | bytes 786440 | tf_op jit(solution)/shard_map/ppermute | solution.py:59
  23.3 7.2 %collective-permute-start.3 = (f32[256,256]{1,0:T(8,128)S(1)}, f32[256,256]{1,0:T(8,128)S(1)}, u32[]{:S(2)}, u32[]{:S(2)}) collective-permute-start(f32[256,256]{1,0:T(8,128)S(1)} %add_add_fusion.1), channel_id=1, source_target_pairs={{0,12},{1,13},{2,14},{3,15},{4,0},{5,1},{6,2},{7,3},{8,4},{9,5},{1... | collective-permute-start | bytes 786440 | tf_op jit(solution)/shard_map/ppermute | solution.py:59
  30.5 8.1 %collective-permute-start.8 = (f32[256,256]{1,0:T(8,128)S(1)}, f32[256,256]{1,0:T(8,128)S(1)}, u32[]{:S(2)}, u32[]{:S(2)}) collective-permute-start(f32[256,256]{1,0:T(8,128)S(1)} %add_add_fusion.refs_2_.own), channel_id=1, source_target_pairs={{0,2},{1,3},{2,0},{3,1},{4,6},{5,7},{6,4},{7,5},{8,10},{9,11},{10,... | collective-permute-start | bytes 786440 | tf_op jit(solution)/shard_map/ppermute | solution.py:59
  32.6 8.6 %collective-permute-start.7 = (f32[256,256]{1,0:T(8,128)S(1)}, f32[256,256]{1,0:T(8,128)S(1)}, u32[]{:S(2)}, u32[]{:S(2)}) collective-permute-start(f32[256,256]{1,0:T(8,128)S(1)} %add_add_fusion.refs_2_.own), channel_id=1, source_target_pairs={{0,1},{1,2},{2,3},{3,0},{4,5},{5,6},{6,7},{7,4},{8,9},{9,10},{10,1... | collective-permute-start | bytes 786440 | tf_op jit(solution)/shard_map/ppermute | solution.py:59
  34.5 7.6 %collective-permute-start.6 = (f32[256,256]{1,0:T(8,128)S(1)}, f32[256,256]{1,0:T(8,128)S(1)}, u32[]{:S(2)}, u32[]{:S(2)}) collective-permute-start(f32[256,256]{1,0:T(8,128)S(1)} %add_add_fusion.refs_2_.own), channel_id=1, source_target_pairs={{0,3},{1,0},{2,1},{3,2},{4,7},{5,4},{6,5},{7,6},{8,11},{9,8},{10,9... | collective-permute-start | bytes 786440 | tf_op jit(solution)/shard_map/ppermute | solution.py:59
  43.1 2.1 %collective-permute-start.9 = (f32[152,1024]{1,0:T(8,128)S(1)}, f32[152,1024]{1,0:T(8,128)S(1)}, u32[]{:S(2)}, u32[]{:S(2)}) collective-permute-start(f32[152,1024]{1,0:T(8,128)S(1)} %get-tuple-element.40), channel_id=1, source_target_pairs={{0,16},{1,17},{2,18},{3,19},{4,20},{5,21},{6,22},{7,23},{8,24},{9,... | collective-permute-start | bytes 1867784 | tf_op jit(solution)/shard_map/ppermute | solution.py:59
  45.4 8.1 %collective-permute-start.18 = (f32[24,1024]{1,0:T(8,128)S(1)}, f32[24,1024]{1,0:T(8,128)S(1)}, u32[]{:S(2)}, u32[]{:S(2)}) collective-permute-start(f32[24,1024]{1,0:T(8,128)S(1)} %get-tuple-element.45), channel_id=1, source_target_pairs={{0,64},{1,65},{2,66},{3,67},{4,68},{5,69},{6,70},{7,71},{8,72},{9,... | collective-permute-start | bytes 294920 | tf_op jit(solution)/shard_map/ppermute | solution.py:59
  49.3 7.2 %collective-permute-start.17 = (f32[24,1024]{1,0:T(8,128)S(1)}, f32[24,1024]{1,0:T(8,128)S(1)}, u32[]{:S(2)}, u32[]{:S(2)}) collective-permute-start(f32[24,1024]{1,0:T(8,128)S(1)} %get-tuple-element.45), channel_id=1, source_target_pairs={{0,32},{1,33},{2,34},{3,35},{4,36},{5,37},{6,38},{7,39},{8,40},{9,... | collective-permute-start | bytes 294920 | tf_op jit(solution)/shard_map/ppermute | solution.py:59
  50.4 6.7 %collective-permute-start.16 = (f32[24,1024]{1,0:T(8,128)S(1)}, f32[24,1024]{1,0:T(8,128)S(1)}, u32[]{:S(2)}, u32[]{:S(2)}) collective-permute-start(f32[24,1024]{1,0:T(8,128)S(1)} %get-tuple-element.45), channel_id=1, source_target_pairs={{0,96},{1,97},{2,98},{3,99},{4,100},{5,101},{6,102},{7,103},{8,104... | collective-permute-start | bytes 294920 | tf_op jit(solution)/shard_map/ppermute | solution.py:59
  52.6 7.7 %collective-permute-start.10 = (f32[32,1024]{1,0:T(8,128)S(1)}, f32[32,1024]{1,0:T(8,128)S(1)}, u32[]{:S(2)}, u32[]{:S(2)}) collective-permute-start(f32[32,1024]{1,0:T(8,128)S(1)} %get-tuple-element.42), channel_id=1, source_target_pairs={{0,64},{1,65},{2,66},{3,67},{4,68},{5,69},{6,70},{7,71},{8,72},{9,... | collective-permute-start | bytes 393224 | tf_op jit(solution)/shard_map/ppermute | solution.py:59
  52.6 8.7 %collective-permute-start.11 = (f32[32,1024]{1,0:T(8,128)S(1)}, f32[32,1024]{1,0:T(8,128)S(1)}, u32[]{:S(2)}, u32[]{:S(2)}) collective-permute-start(f32[32,1024]{1,0:T(8,128)S(1)} %get-tuple-element.43), channel_id=1, source_target_pairs={{0,32},{1,33},{2,34},{3,35},{4,36},{5,37},{6,38},{7,39},{8,40},{9,... | collective-permute-start | bytes 393224 | tf_op jit(solution)/shard_map/ppermute | solution.py:59
  53.4 7.9 %collective-permute-start.12 = (f32[32,1024]{1,0:T(8,128)S(1)}, f32[32,1024]{1,0:T(8,128)S(1)}, u32[]{:S(2)}, u32[]{:S(2)}) collective-permute-start(f32[32,1024]{1,0:T(8,128)S(1)} %get-tuple-element.44), channel_id=1, source_target_pairs={{0,96},{1,97},{2,98},{3,99},{4,100},{5,101},{6,102},{7,103},{8,104... | collective-permute-start | bytes 393224 | tf_op jit(solution)/shard_map/ppermute | solution.py:59
  57.0 9.3 %collective-permute-start.19 = (f32[24,1024]{1,0:T(8,128)S(1)}, f32[24,1024]{1,0:T(8,128)S(1)}, u32[]{:S(2)}, u32[]{:S(2)}) collective-permute-start(f32[24,1024]{1,0:T(8,128)S(1)} %add_add_fusion.3.gram), channel_id=1, source_target_pairs={{0,16},{1,17},{2,18},{3,19},{4,20},{5,21},{6,22},{7,23},{8,24},{9,... | collective-permute-start | bytes 294920 | tf_op jit(solution)/shard_map/ppermute | solution.py:59
  61.3 11.1 %collective-permute-start.15 = (f32[32,1024]{1,0:T(8,128)S(1)}, f32[32,1024]{1,0:T(8,128)S(1)}, u32[]{:S(2)}, u32[]{:S(2)}) collective-permute-start(f32[32,1024]{1,0:T(8,128)S(1)} %add_add_fusion.2.own), channel_id=1, source_target_pairs={{0,64},{1,65},{2,66},{3,67},{4,68},{5,69},{6,70},{7,71},{8,72},{9,... | collective-permute-start | bytes 393224 | tf_op jit(solution)/shard_map/ppermute | solution.py:59
  63.1 9.4 %collective-permute-start.14 = (f32[32,1024]{1,0:T(8,128)S(1)}, f32[32,1024]{1,0:T(8,128)S(1)}, u32[]{:S(2)}, u32[]{:S(2)}) collective-permute-start(f32[32,1024]{1,0:T(8,128)S(1)} %add_add_fusion.2.own), channel_id=1, source_target_pairs={{0,32},{1,33},{2,34},{3,35},{4,36},{5,37},{6,38},{7,39},{8,40},{9,... | collective-permute-start | bytes 393224 | tf_op jit(solution)/shard_map/ppermute | solution.py:59
  64.9 7.5 %collective-permute-start.13 = (f32[32,1024]{1,0:T(8,128)S(1)}, f32[32,1024]{1,0:T(8,128)S(1)}, u32[]{:S(2)}, u32[]{:S(2)}) collective-permute-start(f32[32,1024]{1,0:T(8,128)S(1)} %add_add_fusion.2.own), channel_id=1, source_target_pairs={{0,96},{1,97},{2,98},{3,99},{4,100},{5,101},{6,102},{7,103},{8,104... | collective-permute-start | bytes 393224 | tf_op jit(solution)/shard_map/ppermute | solution.py:59
  72.5 2.0 %collective-permute-start.20 = (f32[128,1024]{1,0:T(8,128)S(1)}, f32[128,1024]{1,0:T(8,128)S(1)}, u32[]{:S(2)}, u32[]{:S(2)}) collective-permute-start(f32[128,1024]{1,0:T(8,128)S(1)} %ordered.1.half), channel_id=1, source_target_pairs={{0,16},{1,17},{2,18},{3,19},{4,20},{5,21},{6,22},{7,23},{8,24},{9,... | collective-permute-start | bytes 1572872 | tf_op jit(solution)/shard_map/ppermute | solution.py:59
  76.5 13.6 %all-to-all-start = ((f32[16,1,256]{2,1,0:T(1,128)}), f32[16,1,256]{2,1,0:T(1,128)S(1)}, u32[]{:S(2)}, u32[]{:S(2)}) async-start(f32[16,1,256]{2,1,0:T(1,128)} %broadcast_in_dim.9), calls=%async_computation | async-start | bytes 32768 | tf_op jit(solution)/shard_map/all_to_all | solution.py:497
  (1 other events, 1.2 us)

commit v5 on v4

--- a/solution.py
+++ b/solution.py
@@ -148,12 +148,46 @@
             out_specs=[vmem()] * len(out),
             out_shape=[jax.ShapeDtypeStruct(shape, kind) for shape, kind in out],
             compiler_params=params(),
-            cost_estimate=cost(flops, 2**20),
+            cost_estimate=cost(flops, 2**16),
             name=name,
             **more,
         )(*operands)
 
     return run
+
+
+PRODUCT_PIECES = 2
+
+
+def products_kernel(momentum, gradient, basis, out, held):
+    @pl.when(pl.program_id(0) == 0)
+    def _():
+        for n, part in enumerate(pieces(basis[...], PRODUCT_PIECES)):
+            held[n] = part
+
+    buffer = momentum[...] + gradient[...].astype(f32)
+    right = [held[n] for n in range(PRODUCT_PIECES)]
+    out[...] = piece_dot(pieces(buffer, PRODUCT_PIECES), right)
+
+
+def partial_products(momentum, gradient, basis):
+    rows = lambda i: (i, 0)
+    half = BLOCK // 2
+    return pl.pallas_call(
+        products_kernel,
+        grid=(2,),
+        in_specs=[
+            pl.BlockSpec((half, BLOCK), rows),
+            pl.BlockSpec((half, BLOCK), rows),
+            pl.BlockSpec((BLOCK, R), lambda i: (0, 0)),
+        ],
+        out_specs=pl.BlockSpec((half, R), rows),
+        out_shape=jax.ShapeDtypeStruct((BLOCK, R), f32),
+        scratch_shapes=[pltpu.VMEM((PRODUCT_PIECES, BLOCK, R), bf16)],
+        compiler_params=params(),
+        cost_estimate=cost(2 * BLOCK * BLOCK * R * 3, 7 * 2**20),
+        name="products",
+    )(*[pltpu.with_memory_space_constraint(v, pltpu.HBM) for v in (momentum, gradient, basis)])
 
 
 def quarters_kernel(partial, *parts):
@@ -245,6 +279,19 @@
         [((Z_ROWS, BLOCK), f32)] * 4 + [((GRAM_ROWS, BLOCK), f32)],
         scratch_shapes=[pltpu.VMEM((CORE_ROWS, BLOCK), f32)],
     )(keep, got)
+
+
+def settle_kernel(own, three, one, two, after, out):
+    out[...] = (three[...] + one[...]) + (two[...] + own[...])
+
+
+def settle(own, one, two, three, after):
+    return call(
+        settle_kernel,
+        "settle",
+        [((GRAM_ROWS, BLOCK), f32)],
+        in_specs=[vmem()] * 4 + [anywhere()],
+    )(own, three, one, two, after)[0]
 
 
 def lower_inverse(block):
@@ -333,7 +380,6 @@
         inverse_kernel,
         "inverse",
         [((R, R), f32)],
-        10**9,
         scratch_shapes=[pltpu.VMEM((R, R), f32), pltpu.VMEM((2 * GRAM_ROWS, BLOCK), f32)],
     )(gram, other)[0]
 
@@ -365,27 +411,41 @@
     return call(basis_kernel, "basis", [((BLOCK, R), f32)], 2 * BLOCK * R * R * 6)(*parts, inverse)[0]
 
 
-def reduced_kernel(half, other, inverse, high, low, squares, crossed):
+def reduced_kernel(half, other, inverse, high, low, squares, crossed, line, sem):
     core = place()[1]
     crossed[span(core, HALF)] = half[...]
     crossed[span(1 - core, HALF)] = other[...]
-    value = dot(inverse[...], crossed[...], precision=highest)
-    high[...], low[...] = pieces(value, 2)
+    value = piece_dot(pieces(inverse[...], 2), pieces(crossed[...], 2))
     square = value * value
     folded = square[:, :128]
     for n in range(1, BLOCK // 128):
         folded = folded + square[:, n * 128 : n * 128 + 128]
     total = jnp.sum(folded.T, axis=0, keepdims=True)
-    squares[...] = jnp.broadcast_to(total, squares.shape)
+    line[...] = jnp.broadcast_to(total[None], line.shape)
+    copy = pltpu.make_async_copy(line, squares, sem)
+    copy.start()
+    high[...], low[...] = pieces(value, 2)
+    copy.wait()
 
 
 def form_reduced(half, other, inverse):
-    return call(
+    return pl.pallas_call(
         reduced_kernel,
-        "reduced",
-        [((R, BLOCK), bf16), ((R, BLOCK), bf16), ((8, R), f32)],
-        2 * BLOCK * R * R * 6,
-        scratch_shapes=[pltpu.VMEM((R, BLOCK), f32)],
+        in_specs=[vmem()] * 3,
+        out_specs=[vmem(), vmem(), hbm()],
+        out_shape=[
+            jax.ShapeDtypeStruct((R, BLOCK), bf16),
+            jax.ShapeDtypeStruct((R, BLOCK), bf16),
+            pltpu.HBM((16, 1, R), f32),
+        ],
+        scratch_shapes=[
+            pltpu.VMEM((R, BLOCK), f32),
+            pltpu.VMEM((16, 1, R), f32),
+            pltpu.SemaphoreType.DMA(()),
+        ],
+        compiler_params=params(),
+        cost_estimate=cost(2 * BLOCK * R * R * 3, 3 * 2**20),
+        name="reduced",
     )(half, other, inverse)
 
 
@@ -472,9 +532,7 @@
 
 
 def local(momentum, gradient, basis_prev):
-    buffer = momentum + gradient.astype(f32)
-    partial = dot(buffer, basis_prev, precision=highest)
-    parts = quarters(partial)
+    parts = quarters(partial_products(momentum, gradient, basis_prev))
     quarter = sum_four(parts[0], *to_three(parts, first_axis))
     one, two, three = to_all(quarter, second_axis)
     quarter = (three + one) + (two + quarter)
@@ -487,14 +545,12 @@
     keep, give = depart(*sums)
     *shares, gram = spread(keep, send(give, other_core))
     crossed = sum_four(shares[0], *to_three(shares, along_z))
-    one, two, three = to_all(gram, along_z)
-    gram = (three + one) + (two + gram)
+    gram = settle(gram, *to_all(gram, along_z), crossed)
     inverse = inverse_factor(gram, send(gram, other_core))
     half = ordered([crossed, *to_all(crossed, along_z)], inverse)
     basis = form_basis(parts, inverse)
     high, low, squares = form_reduced(half, send(half, other_core), inverse)
-    everyone = jnp.broadcast_to(squares[None, :1], (16, 1, R))
-    squares = lax.all_to_all(everyone, "tp", 0, 0).reshape(16, R)
+    squares = lax.all_to_all(squares, "tp", 0, 0).reshape(16, R)
     new_momentum = form_momentum(momentum, gradient, basis, high, low)
     update, new_basis = form_update(squares, basis, high, low)
     return (update, new_momentum, new_basis)

time: 93.2 us -> 88.6 us (0.951)
  matrix products: 6.33 us -> 0 us
  Pallas kernels: 20.6 us -> 25.4 us
  waiting for transfers between devices: 22.4 us -> 19.3 us
  local copies, waits for them, and re-layouts: 1.84 us -> 0.01 us
  starting transfers between devices: 40.7 us -> 42.5 us
    dot_general x1 -> x0, matrix products: 6.33 us -> none  [dot(): lax.dot_general(left, right, (dims, ((), ())), precision=precision, prefe...]
    pallas_call x0 -> x2, Pallas kernels: none -> 6.21 us  [the longest x1 4.72 us: partial_products(): pl.pallas_call(products_kernel, grid=(2,), in_specs=[pl.BlockSpec((half,...]
    ppermute x21, waiting for transfers between devices: 20.3 us -> 17.2 us  [send(): return lax.ppermute(value, both, where)]
    ppermute x21, starting transfers between devices: 34.7 us -> 36.5 us  [send(): return lax.ppermute(value, both, where)]
    pallas_call x11, Pallas kernels: 12.3 us -> 11 us  [run(): pl.pallas_call(kernel, in_specs=in_specs or [vmem()] * len(operands), out...]
    unnamed x7 -> x5, local copies, waits for them, and re-layouts: 1.21 us -> 0.01 us
  transfers between devices with their start and end apart: 22 -> 22, of which waited for: 14 -> 14; matrix products, arithmetic and copies ran while one was open for 0% -> 0% of each run, Pallas kernels for 16% -> 17%
where the time goes in v5:
time: 88.6 us; the launch traced here: 88.4 us
  starting transfers between devices  42.5 us (48%)
  Pallas kernels  25.4 us (29%)
  waiting for transfers between devices  19.3 us (22%)
  between operations  0.99 us (1%)
    ppermute x21, starting transfers between devices, send(): return lax.ppermute(value, both, where)  36.5 us
    ppermute x21, waiting for transfers between devices, send(): return lax.ppermute(value, both, where)  17.2 us
    pallas_call x11, Pallas kernels, run(): pl.pallas_call(kernel, in_specs=in_specs or [vmem()] * len(operands), out...  11 us
    all_to_all x1, starting transfers between devices, local(): squares = lax.all_to_all(squares, 'tp', 0, 0).reshape(16, R)  5.98 us
    pallas_call x1, Pallas kernels, form_momentum(): pl.pallas_call(momentum_kernel, in_specs=[hbm()] * 2 + [vmem()] * 3, out_...  5.5 us
    pallas_call x1, Pallas kernels, partial_products(): pl.pallas_call(products_kernel, grid=(2,), in_specs=[pl.BlockSpec((half,...  4.72 us
    pallas_call x1, Pallas kernels, form_update(): pl.pallas_call(update_kernel, in_specs=[vmem()] * 4, out_specs=[hbm()] *...  2.78 us
    all_to_all x1, waiting for transfers between devices, local(): squares = lax.all_to_all(squares, 'tp', 0, 0).reshape(16, R)  2.08 us
  transfers between devices with their start and end apart: 22, of which 14 were waited for; matrix products, arithmetic and copies ran while one was open for 0% of the time, Pallas kernels for 17%

profile of v5, /device:TPU:0, one launch (start us, length us, event | category | flops | bytes accessed | tf_op | source)
XLA Modules:
  0.0 88.4 jit_solution(15780550353106247053)
XLA Ops:
  0.7 4.7 %products.1.partial = f32[1024,256]{1,0:T(8,128)S(1)} custom-call(f32[1024,1024]{1,0:T(8,128)} %momentum.5, bf16[1024,1024]{1,0:T(8,128)(2,1)} %gradient.3, f32[1024,256]{1,0:T(8,128)} %basis.2), custom_call_target="tpu_custom_call" | custom-call | flops 1610612736 | bytes 7340032 | tf_op jit(solution)/shard_map/products/pallas_call | solution.py:176
  5.5 3.2 %collective-permute-start = (f32[256,256]{1,0:T(8,128)S(1)}, f32[256,256]{1,0:T(8,128)S(1)}, u32[]{:S(2)}, u32[]{:S(2)}) collective-permute-start(f32[256,256]{1,0:T(8,128)S(1)} %get-tuple-element.28), channel_id=1, source_target_pairs={{0,2},{1,3},{2,0},{3,1},{4,6},{5,7},{6,4},{7,5},{8,10},{9,11},{10,... | collective-permute-start | bytes 786440 | tf_op jit(solution)/shard_map/ppermute | solution.py:59
  9.3 2.6 %collective-permute-start.2 = (f32[256,256]{1,0:T(8,128)S(1)}, f32[256,256]{1,0:T(8,128)S(1)}, u32[]{:S(2)}, u32[]{:S(2)}) collective-permute-start(f32[256,256]{1,0:T(8,128)S(1)} %get-tuple-element.30), channel_id=1, source_target_pairs={{0,3},{1,0},{2,1},{3,2},{4,7},{5,4},{6,5},{7,6},{8,11},{9,8},{10,9... | collective-permute-start | bytes 786440 | tf_op jit(solution)/shard_map/ppermute | solution.py:59
  11.9 1.5 %collective-permute-done = f32[256,256]{1,0:T(8,128)S(1)} collective-permute-done((f32[256,256]{1,0:T(8,128)S(1)}, f32[256,256]{1,0:T(8,128)S(1)}, u32[]{:S(2)}, u32[]{:S(2)}) %collective-permute-start) | collective-permute-done | bytes 262176 | tf_op jit(solution)/shard_map/ppermute | solution.py:59
  13.4 2.8 %collective-permute-done.1 = f32[256,256]{1,0:T(8,128)S(1)} collective-permute-done((f32[256,256]{1,0:T(8,128)S(1)}, f32[256,256]{1,0:T(8,128)S(1)}, u32[]{:S(2)}, u32[]{:S(2)}) %collective-permute-start.1) | collective-permute-done | bytes 262176 | tf_op jit(solution)/shard_map/ppermute | solution.py:59
  16.5 3.3 %collective-permute-start.5 = (f32[256,256]{1,0:T(8,128)S(1)}, f32[256,256]{1,0:T(8,128)S(1)}, u32[]{:S(2)}, u32[]{:S(2)}) collective-permute-start(f32[256,256]{1,0:T(8,128)S(1)} %add_add_fusion.1), channel_id=1, source_target_pairs={{0,8},{1,9},{2,10},{3,11},{4,12},{5,13},{6,14},{7,15},{8,0},{9,1},... | collective-permute-start | bytes 786440 | tf_op jit(solution)/shard_map/ppermute | solution.py:59
  20.4 2.6 %collective-permute-start.3 = (f32[256,256]{1,0:T(8,128)S(1)}, f32[256,256]{1,0:T(8,128)S(1)}, u32[]{:S(2)}, u32[]{:S(2)}) collective-permute-start(f32[256,256]{1,0:T(8,128)S(1)} %add_add_fusion.1), channel_id=1, source_target_pairs={{0,12},{1,13},{2,14},{3,15},{4,0},{5,1},{6,2},{7,3},{8,4},{9,5},{1... | collective-permute-start | bytes 786440 | tf_op jit(solution)/shard_map/ppermute | solution.py:59
  24.4 2.9 %collective-permute-done.4 = f32[256,256]{1,0:T(8,128)S(1)} collective-permute-done((f32[256,256]{1,0:T(8,128)S(1)}, f32[256,256]{1,0:T(8,128)S(1)}, u32[]{:S(2)}, u32[]{:S(2)}) %collective-permute-start.4) | collective-permute-done | bytes 262176 | tf_op jit(solution)/shard_map/ppermute | solution.py:59
  27.7 2.2 %collective-permute-start.8 = (f32[256,256]{1,0:T(8,128)S(1)}, f32[256,256]{1,0:T(8,128)S(1)}, u32[]{:S(2)}, u32[]{:S(2)}) collective-permute-start(f32[256,256]{1,0:T(8,128)S(1)} %add_add_fusion.refs_2_.own), channel_id=1, source_target_pairs={{0,2},{1,3},{2,0},{3,1},{4,6},{5,7},{6,4},{7,5},{8,10},{9,11},{10,... | collective-permute-start | bytes 786440 | tf_op jit(solution)/shard_map/ppermute | solution.py:59
  29.8 1.9 %collective-permute-start.7 = (f32[256,256]{1,0:T(8,128)S(1)}, f32[256,256]{1,0:T(8,128)S(1)}, u32[]{:S(2)}, u32[]{:S(2)}) collective-permute-start(f32[256,256]{1,0:T(8,128)S(1)} %add_add_fusion.refs_2_.own), channel_id=1, source_target_pairs={{0,1},{1,2},{2,3},{3,0},{4,5},{5,6},{6,7},{7,4},{8,9},{9,10},{10,1... | collective-permute-start | bytes 786440 | tf_op jit(solution)/shard_map/ppermute | solution.py:59
  33.9 1.8 %collective-permute-done.8.refs_2_.two = f32[256,256]{1,0:T(8,128)S(1)} collective-permute-done((f32[256,256]{1,0:T(8,128)S(1)}, f32[256,256]{1,0:T(8,128)S(1)}, u32[]{:S(2)}, u32[]{:S(2)}) %collective-permute-start.8) | collective-permute-done | bytes 262176 | tf_op jit(solution)/shard_map/ppermute | solution.py:59
  36.6 1.8 %collective-permute-done.7.refs_2_.one = f32[256,256]{1,0:T(8,128)S(1)} collective-permute-done((f32[256,256]{1,0:T(8,128)S(1)}, f32[256,256]{1,0:T(8,128)S(1)}, u32[]{:S(2)}, u32[]{:S(2)}) %collective-permute-start.7) | collective-permute-done | bytes 262176 | tf_op jit(solution)/shard_map/ppermute | solution.py:59
  40.4 2.0 %collective-permute-done.9.got = f32[152,1024]{1,0:T(8,128)S(1)} collective-permute-done((f32[152,1024]{1,0:T(8,128)S(1)}, f32[152,1024]{1,0:T(8,128)S(1)}, u32[]{:S(2)}, u32[]{:S(2)}) %collective-permute-start.9) | collective-permute-done | bytes 622624 | tf_op jit(solution)/shard_map/ppermute | solution.py:59
  42.6 4.0 %collective-permute-start.10 = (f32[32,1024]{1,0:T(8,128)S(1)}, f32[32,1024]{1,0:T(8,128)S(1)}, u32[]{:S(2)}, u32[]{:S(2)}) collective-permute-start(f32[32,1024]{1,0:T(8,128)S(1)} %get-tuple-element.42), channel_id=1, source_target_pairs={{0,64},{1,65},{2,66},{3,67},{4,68},{5,69},{6,70},{7,71},{8,72},{9,... | collective-permute-start | bytes 393224 | tf_op jit(solution)/shard_map/ppermute | solution.py:59
  47.5 2.2 %collective-permute-start.12 = (f32[32,1024]{1,0:T(8,128)S(1)}, f32[32,1024]{1,0:T(8,128)S(1)}, u32[]{:S(2)}, u32[]{:S(2)}) collective-permute-start(f32[32,1024]{1,0:T(8,128)S(1)} %get-tuple-element.44), channel_id=1, source_target_pairs={{0,96},{1,97},{2,98},{3,99},{4,100},{5,101},{6,102},{7,103},{8,104... | collective-permute-start | bytes 393224 | tf_op jit(solution)/shard_map/ppermute | solution.py:59
  50.8 3.7 %collective-permute-start.16 = (f32[24,1024]{1,0:T(8,128)S(1)}, f32[24,1024]{1,0:T(8,128)S(1)}, u32[]{:S(2)}, u32[]{:S(2)}) collective-permute-start(f32[24,1024]{1,0:T(8,128)S(1)} %get-tuple-element.45.own), channel_id=1, source_target_pairs={{0,96},{1,97},{2,98},{3,99},{4,100},{5,101},{6,102},{7,103},{8,104... | collective-permute-start | bytes 294920 | tf_op jit(solution)/shard_map/ppermute | solution.py:59
  54.8 2.6 %collective-permute-start.15 = (f32[32,1024]{1,0:T(8,128)S(1)}, f32[32,1024]{1,0:T(8,128)S(1)}, u32[]{:S(2)}, u32[]{:S(2)}) collective-permute-start(f32[32,1024]{1,0:T(8,128)S(1)} %add_add_fusion.2.after.own), channel_id=1, source_target_pairs={{0,64},{1,65},{2,66},{3,67},{4,68},{5,69},{6,70},{7,71},{8,72},{9,... | collective-permute-start | bytes 393224 | tf_op jit(solution)/shard_map/ppermute | solution.py:59
  57.4 2.2 %collective-permute-start.14 = (f32[32,1024]{1,0:T(8,128)S(1)}, f32[32,1024]{1,0:T(8,128)S(1)}, u32[]{:S(2)}, u32[]{:S(2)}) collective-permute-start(f32[32,1024]{1,0:T(8,128)S(1)} %add_add_fusion.2.after.own), channel_id=1, source_target_pairs={{0,32},{1,33},{2,34},{3,35},{4,36},{5,37},{6,38},{7,39},{8,40},{9,... | collective-permute-start | bytes 393224 | tf_op jit(solution)/shard_map/ppermute | solution.py:59
  62.2 6.1 %inverse.1.after = f32[256,256]{1,0:T(8,128)S(1)} custom-call(f32[24,1024]{1,0:T(8,128)S(1)} %settle.1.gram, f32[24,1024]{1,0:T(8,128)S(1)} %collective-permute-done.19.other), custom_call_target="tpu_custom_call" | custom-call | bytes 65536 | tf_op jit(solution)/shard_map/inverse/pallas_call | solution.py:145
  70.4 1.5 %reduced.1 = (bf16[256,1024]{1,0:T(8,128)(2,1)S(1)}, bf16[256,1024]{1,0:T(8,128)(2,1)S(1)}, f32[16,1,256]{2,1,0:T(1,128)}) custom-call(f32[128,1024]{1,0:T(8,128)S(1)} %ordered.1.half, f32[128,1024]{1,0:T(8,128)S(1)} %collective-permute-done.20.other, f32[256,256]{1,0:T(8,128)S(1)} %inverse.1.after), custom_call_target="tpu_custom_call" | custom-call | flops 402653184 | bytes 3145728 | tf_op jit(solution)/shard_map/reduced/pallas_call | solution.py:432
  71.9 6.0 %all-to-all-start = ((f32[16,1,256]{2,1,0:T(1,128)}), f32[16,1,256]{2,1,0:T(1,128)S(1)}, u32[]{:S(2)}, u32[]{:S(2)}) async-start(f32[16,1,256]{2,1,0:T(1,128)} %get-tuple-element.46), calls=%async_computation | async-start | bytes 32768 | tf_op jit(solution)/shard_map/all_to_all | solution.py:553
  77.9 5.5 %momentum.4 = f32[1024,1024]{1,0:T(8,128)} custom-call(f32[1024,1024]{1,0:T(8,128)} %momentum.5, bf16[1024,1024]{1,0:T(8,128)(2,1)} %gradient.3, f32[1024,256]{1,0:T(8,128)S(1)} %basis.3, bf16[256,1024]{1,0:T(8,128)(2,1)S(1)} %get-tuple-element.47.high, bf16[256,1024]{1,0:T(8,128)(2,1)S(1)} %get-tuple-element.48.low), custom_call_target="tpu_custom_call" | custom-call | flops 3221225472 | bytes 12582912 | tf_op jit(solution)/shard_map/momentum/pallas_call | solution.py:478
  83.4 2.1 %all-to-all-done = f32[16,1,256]{2,1,0:T(1,128)S(1)} async-done(((f32[16,1,256]{2,1,0:T(1,128)}), f32[16,1,256]{2,1,0:T(1,128)S(1)}, u32[]{:S(2)}, u32[]{:S(2)}) %all-to-all-start) | async-done | bytes 16416 | tf_op jit(solution)/shard_map/all_to_all | solution.py:553
  85.5 2.8 %update.1 = (bf16[1024,1024]{1,0:T(8,128)(2,1)}, f32[1024,256]{1,0:T(8,128)}) custom-call(f32[16,256]{1,0:T(8,128)S(1)} %bitcast.3, f32[1024,256]{1,0:T(8,128)S(1)} %basis.3, bf16[256,1024]{1,0:T(8,128)(2,1)S(1)} %get-tuple-element.47.high, bf16[256,1024]{1,0:T(8,128)(2,1)S(1)} %get-tuple-element.48.low), custom_call_target="tpu_custom_call" | custom-call | flops 3221225472 | bytes 6291456 | tf_op jit(solution)/shard_map/update/pallas_call | solution.py:514
  (43 shorter events, 15.5 us)
Async XLA Ops:
  0.6 32.4 %copy-start.1 = (bf16[1024,1024]{1,0:T(8,128)(2,1)S(1)}, bf16[1024,1024]{1,0:T(8,128)(2,1)}, u32[]{:S(2)}) copy-start(bf16[1024,1024]{1,0:T(8,128)(2,1)} %gradient.3) | copy-start | bytes 6291460
  0.6 32.4 %copy-start = (f32[1024,1024]{1,0:T(8,128)S(1)}, f32[1024,1024]{1,0:T(8,128)}, u32[]{:S(2)}) copy-start(f32[1024,1024]{1,0:T(8,128)} %momentum.5) | copy-start | bytes 12582916
  5.5 8.0 %collective-permute-start = (f32[256,256]{1,0:T(8,128)S(1)}, f32[256,256]{1,0:T(8,128)S(1)}, u32[]{:S(2)}, u32[]{:S(2)}) collective-permute-start(f32[256,256]{1,0:T(8,128)S(1)} %get-tuple-element.28), channel_id=1, source_target_pairs={{0,2},{1,3},{2,0},{3,1},{4,6},{5,7},{6,4},{7,5},{8,10},{9,11},{10,... | collective-permute-start | bytes 786440 | tf_op jit(solution)/shard_map/ppermute | solution.py:59
  8.7 7.6 %collective-permute-start.1 = (f32[256,256]{1,0:T(8,128)S(1)}, f32[256,256]{1,0:T(8,128)S(1)}, u32[]{:S(2)}, u32[]{:S(2)}) collective-permute-start(f32[256,256]{1,0:T(8,128)S(1)} %get-tuple-element.29), channel_id=1, source_target_pairs={{0,1},{1,2},{2,3},{3,0},{4,5},{5,6},{6,7},{7,4},{8,9},{9,10},{10,1... | collective-permute-start | bytes 786440 | tf_op jit(solution)/shard_map/ppermute | solution.py:59
  9.3 7.2 %collective-permute-start.2 = (f32[256,256]{1,0:T(8,128)S(1)}, f32[256,256]{1,0:T(8,128)S(1)}, u32[]{:S(2)}, u32[]{:S(2)}) collective-permute-start(f32[256,256]{1,0:T(8,128)S(1)} %get-tuple-element.30), channel_id=1, source_target_pairs={{0,3},{1,0},{2,1},{3,2},{4,7},{5,4},{6,5},{7,6},{8,11},{9,8},{10,9... | collective-permute-start | bytes 786440 | tf_op jit(solution)/shard_map/ppermute | solution.py:59
  16.5 8.0 %collective-permute-start.5 = (f32[256,256]{1,0:T(8,128)S(1)}, f32[256,256]{1,0:T(8,128)S(1)}, u32[]{:S(2)}, u32[]{:S(2)}) collective-permute-start(f32[256,256]{1,0:T(8,128)S(1)} %add_add_fusion.1), channel_id=1, source_target_pairs={{0,8},{1,9},{2,10},{3,11},{4,12},{5,13},{6,14},{7,15},{8,0},{9,1},... | collective-permute-start | bytes 786440 | tf_op jit(solution)/shard_map/ppermute | solution.py:59
  19.8 7.6 %collective-permute-start.4 = (f32[256,256]{1,0:T(8,128)S(1)}, f32[256,256]{1,0:T(8,128)S(1)}, u32[]{:S(2)}, u32[]{:S(2)}) collective-permute-start(f32[256,256]{1,0:T(8,128)S(1)} %add_add_fusion.1), channel_id=1, source_target_pairs={{0,4},{1,5},{2,6},{3,7},{4,8},{5,9},{6,10},{7,11},{8,12},{9,13},{1... | collective-permute-start | bytes 786440 | tf_op jit(solution)/shard_map/ppermute | solution.py:59
  20.4 7.2 %collective-permute-start.3 = (f32[256,256]{1,0:T(8,128)S(1)}, f32[256,256]{1,0:T(8,128)S(1)}, u32[]{:S(2)}, u32[]{:S(2)}) collective-permute-start(f32[256,256]{1,0:T(8,128)S(1)} %add_add_fusion.1), channel_id=1, source_target_pairs={{0,12},{1,13},{2,14},{3,15},{4,0},{5,1},{6,2},{7,3},{8,4},{9,5},{1... | collective-permute-start | bytes 786440 | tf_op jit(solution)/shard_map/ppermute | solution.py:59
  27.7 8.1 %collective-permute-start.8 = (f32[256,256]{1,0:T(8,128)S(1)}, f32[256,256]{1,0:T(8,128)S(1)}, u32[]{:S(2)}, u32[]{:S(2)}) collective-permute-start(f32[256,256]{1,0:T(8,128)S(1)} %add_add_fusion.refs_2_.own), channel_id=1, source_target_pairs={{0,2},{1,3},{2,0},{3,1},{4,6},{5,7},{6,4},{7,5},{8,10},{9,11},{10,... | collective-permute-start | bytes 786440 | tf_op jit(solution)/shard_map/ppermute | solution.py:59
  29.8 8.6 %collective-permute-start.7 = (f32[256,256]{1,0:T(8,128)S(1)}, f32[256,256]{1,0:T(8,128)S(1)}, u32[]{:S(2)}, u32[]{:S(2)}) collective-permute-start(f32[256,256]{1,0:T(8,128)S(1)} %add_add_fusion.refs_2_.own), channel_id=1, source_target_pairs={{0,1},{1,2},{2,3},{3,0},{4,5},{5,6},{6,7},{7,4},{8,9},{9,10},{10,1... | collective-permute-start | bytes 786440 | tf_op jit(solution)/shard_map/ppermute | solution.py:59
  31.7 7.6 %collective-permute-start.6 = (f32[256,256]{1,0:T(8,128)S(1)}, f32[256,256]{1,0:T(8,128)S(1)}, u32[]{:S(2)}, u32[]{:S(2)}) collective-permute-start(f32[256,256]{1,0:T(8,128)S(1)} %add_add_fusion.refs_2_.own), channel_id=1, source_target_pairs={{0,3},{1,0},{2,1},{3,2},{4,7},{5,4},{6,5},{7,6},{8,11},{9,8},{10,9... | collective-permute-start | bytes 786440 | tf_op jit(solution)/shard_map/ppermute | solution.py:59
  40.3 2.1 %collective-permute-start.9 = (f32[152,1024]{1,0:T(8,128)S(1)}, f32[152,1024]{1,0:T(8,128)S(1)}, u32[]{:S(2)}, u32[]{:S(2)}) collective-permute-start(f32[152,1024]{1,0:T(8,128)S(1)} %get-tuple-element.40), channel_id=1, source_target_pairs={{0,16},{1,17},{2,18},{3,19},{4,20},{5,21},{6,22},{7,23},{8,24},{9,... | collective-permute-start | bytes 1867784 | tf_op jit(solution)/shard_map/ppermute | solution.py:59
  42.6 8.2 %collective-permute-start.10 = (f32[32,1024]{1,0:T(8,128)S(1)}, f32[32,1024]{1,0:T(8,128)S(1)}, u32[]{:S(2)}, u32[]{:S(2)}) collective-permute-start(f32[32,1024]{1,0:T(8,128)S(1)} %get-tuple-element.42), channel_id=1, source_target_pairs={{0,64},{1,65},{2,66},{3,67},{4,68},{5,69},{6,70},{7,71},{8,72},{9,... | collective-permute-start | bytes 393224 | tf_op jit(solution)/shard_map/ppermute | solution.py:59
  46.5 8.2 %collective-permute-start.11 = (f32[32,1024]{1,0:T(8,128)S(1)}, f32[32,1024]{1,0:T(8,128)S(1)}, u32[]{:S(2)}, u32[]{:S(2)}) collective-permute-start(f32[32,1024]{1,0:T(8,128)S(1)} %get-tuple-element.43), channel_id=1, source_target_pairs={{0,32},{1,33},{2,34},{3,35},{4,36},{5,37},{6,38},{7,39},{8,40},{9,... | collective-permute-start | bytes 393224 | tf_op jit(solution)/shard_map/ppermute | solution.py:59
  47.5 7.2 %collective-permute-start.12 = (f32[32,1024]{1,0:T(8,128)S(1)}, f32[32,1024]{1,0:T(8,128)S(1)}, u32[]{:S(2)}, u32[]{:S(2)}) collective-permute-start(f32[32,1024]{1,0:T(8,128)S(1)} %get-tuple-element.44), channel_id=1, source_target_pairs={{0,96},{1,97},{2,98},{3,99},{4,100},{5,101},{6,102},{7,103},{8,104... | collective-permute-start | bytes 393224 | tf_op jit(solution)/shard_map/ppermute | solution.py:59
  49.8 9.9 %collective-permute-start.18 = (f32[24,1024]{1,0:T(8,128)S(1)}, f32[24,1024]{1,0:T(8,128)S(1)}, u32[]{:S(2)}, u32[]{:S(2)}) collective-permute-start(f32[24,1024]{1,0:T(8,128)S(1)} %get-tuple-element.45.own), channel_id=1, source_target_pairs={{0,64},{1,65},{2,66},{3,67},{4,68},{5,69},{6,70},{7,71},{8,72},{9,... | collective-permute-start | bytes 294920 | tf_op jit(solution)/shard_map/ppermute | solution.py:59
  49.8 10.9 %collective-permute-start.17 = (f32[24,1024]{1,0:T(8,128)S(1)}, f32[24,1024]{1,0:T(8,128)S(1)}, u32[]{:S(2)}, u32[]{:S(2)}) collective-permute-start(f32[24,1024]{1,0:T(8,128)S(1)} %get-tuple-element.45.own), channel_id=1, source_target_pairs={{0,32},{1,33},{2,34},{3,35},{4,36},{5,37},{6,38},{7,39},{8,40},{9,... | collective-permute-start | bytes 294920 | tf_op jit(solution)/shard_map/ppermute | solution.py:59
  50.8 9.8 %collective-permute-start.16 = (f32[24,1024]{1,0:T(8,128)S(1)}, f32[24,1024]{1,0:T(8,128)S(1)}, u32[]{:S(2)}, u32[]{:S(2)}) collective-permute-start(f32[24,1024]{1,0:T(8,128)S(1)} %get-tuple-element.45.own), channel_id=1, source_target_pairs={{0,96},{1,97},{2,98},{3,99},{4,100},{5,101},{6,102},{7,103},{8,104... | collective-permute-start | bytes 294920 | tf_op jit(solution)/shard_map/ppermute | solution.py:59
  54.8 13.5 %collective-permute-start.15 = (f32[32,1024]{1,0:T(8,128)S(1)}, f32[32,1024]{1,0:T(8,128)S(1)}, u32[]{:S(2)}, u32[]{:S(2)}) collective-permute-start(f32[32,1024]{1,0:T(8,128)S(1)} %add_add_fusion.2.after.own), channel_id=1, source_target_pairs={{0,64},{1,65},{2,66},{3,67},{4,68},{5,69},{6,70},{7,71},{8,72},{9,... | collective-permute-start | bytes 393224 | tf_op jit(solution)/shard_map/ppermute | solution.py:59
  57.4 10.9 %collective-permute-start.14 = (f32[32,1024]{1,0:T(8,128)S(1)}, f32[32,1024]{1,0:T(8,128)S(1)}, u32[]{:S(2)}, u32[]{:S(2)}) collective-permute-start(f32[32,1024]{1,0:T(8,128)S(1)} %add_add_fusion.2.after.own), channel_id=1, source_target_pairs={{0,32},{1,33},{2,34},{3,35},{4,36},{5,37},{6,38},{7,39},{8,40},{9,... | collective-permute-start | bytes 393224 | tf_op jit(solution)/shard_map/ppermute | solution.py:59
  59.6 8.7 %collective-permute-start.13 = (f32[32,1024]{1,0:T(8,128)S(1)}, f32[32,1024]{1,0:T(8,128)S(1)}, u32[]{:S(2)}, u32[]{:S(2)}) collective-permute-start(f32[32,1024]{1,0:T(8,128)S(1)} %add_add_fusion.2.after.own), channel_id=1, source_target_pairs={{0,96},{1,97},{2,98},{3,99},{4,100},{5,101},{6,102},{7,103},{8,104... | collective-permute-start | bytes 393224 | tf_op jit(solution)/shard_map/ppermute | solution.py:59
  60.7 1.6 %collective-permute-start.19 = (f32[24,1024]{1,0:T(8,128)S(1)}, f32[24,1024]{1,0:T(8,128)S(1)}, u32[]{:S(2)}, u32[]{:S(2)}) collective-permute-start(f32[24,1024]{1,0:T(8,128)S(1)} %settle.1.gram), channel_id=1, source_target_pairs={{0,16},{1,17},{2,18},{3,19},{4,20},{5,21},{6,22},{7,23},{8,24},{9,... | collective-permute-start | bytes 294920 | tf_op jit(solution)/shard_map/ppermute | solution.py:59
  68.4 2.0 %collective-permute-start.20 = (f32[128,1024]{1,0:T(8,128)S(1)}, f32[128,1024]{1,0:T(8,128)S(1)}, u32[]{:S(2)}, u32[]{:S(2)}) collective-permute-start(f32[128,1024]{1,0:T(8,128)S(1)} %ordered.1.half), channel_id=1, source_target_pairs={{0,16},{1,17},{2,18},{3,19},{4,20},{5,21},{6,22},{7,23},{8,24},{9,... | collective-permute-start | bytes 1572872 | tf_op jit(solution)/shard_map/ppermute | solution.py:59
  71.9 13.6 %all-to-all-start = ((f32[16,1,256]{2,1,0:T(1,128)}), f32[16,1,256]{2,1,0:T(1,128)S(1)}, u32[]{:S(2)}, u32[]{:S(2)}) async-start(f32[16,1,256]{2,1,0:T(1,128)} %get-tuple-element.46), calls=%async_computation | async-start | bytes 32768 | tf_op jit(solution)/shard_map/all_to_all | solution.py:553

commit v6 on v5

--- a/solution.py
+++ b/solution.py
@@ -203,15 +203,16 @@
 CROSSED_PIECES = 2
 HALF = R // 2
 B = 64
-GRAM_ROWS = 24
-CORE_ROWS = HALF + GRAM_ROWS
+WIDTH = BLOCK // 2
+GRAM_ROWS = 48
+CORE_ROWS = R + GRAM_ROWS
 
 
 def packed_pieces():
     for core in range(2):
-        for n in range(4):
+        for n in range(2):
             for s in range(0, GRAM_ROWS, 8):
-                row = core * 96 + n * GRAM_ROWS + s
+                row = (core * 2 + n) * GRAM_ROWS + s
                 top, left = core * GRAM_ROWS + s, n * R
                 if row < HALF:
                     yield top, left, R, row, 0
@@ -242,25 +243,48 @@
     )(momentum, gradient, part, *before)
 
 
-def depart_kernel(crossed, gram, keep, give, packed):
+def last_columns(whose, momentum, gradient, turned, before):
+    me = place()[2]
+    columns = span(whose, WIDTH)
+    spots = [span(ahead(me, 4 - k), QUARTER) for k in (3, 1)]
+    value = jnp.concatenate(
+        [momentum[spot, columns] + gradient[spot, columns].astype(f32) for spot in spots], 0
+    )
+    return before[:, columns] + piece_dot(turned[:CROSSED_PIECES], pieces(value, CROSSED_PIECES))
+
+
+def give_kernel(momentum, gradient, three, one, cross, gram, give, total, packed):
+    core = place()[1]
+    part = jnp.concatenate([three[...], one[...]], 0)
+    turned = pieces(part.T, 3)
+    total[...] = gram[...] + piece_dot(turned, pieces(part, 3))
+    for top, left, width, row, column in packed_pieces():
+        packed[top : top + 8, left : left + width] = total[row : row + 8, column : column + width]
+    give[:R] = last_columns(1 - core, momentum, gradient, turned, cross)
+    give[R:] = packed[span(1 - core, GRAM_ROWS)]
+
+
+def keep_kernel(momentum, gradient, three, one, cross, total, keep, packed):
     core = place()[1]
     for top, left, width, row, column in packed_pieces():
-        packed[top : top + 8, left : left + width] = gram[row : row + 8, column : column + width]
-    for whose, out in ((core, keep), (1 - core, give)):
-        out[:HALF] = crossed[span(whose, HALF)]
-        out[HALF:] = packed[span(whose, GRAM_ROWS)]
-
-
-def depart(crossed, gram):
+        packed[top : top + 8, left : left + width] = total[row : row + 8, column : column + width]
+    part = jnp.concatenate([three[...], one[...]], 0)
+    turned = pieces(part.T, CROSSED_PIECES)
+    keep[:R] = last_columns(core, momentum, gradient, turned, cross)
+    keep[R:] = packed[span(core, GRAM_ROWS)]
+
+
+def last_shares(kernel, name, out, *operands):
     return call(
-        depart_kernel,
-        "depart",
-        [((CORE_ROWS, BLOCK), f32)] * 2,
-        scratch_shapes=[pltpu.VMEM((2 * GRAM_ROWS, BLOCK), f32)],
-    )(crossed, gram)
-
-
-Z_ROWS = HALF // 4
+        kernel,
+        name,
+        out,
+        2 * BLOCK * WIDTH * R * 3,
+        scratch_shapes=[pltpu.VMEM((2 * GRAM_ROWS, WIDTH), f32)],
+    )(*operands)
+
+
+Z_ROWS = R // 4
 
 
 def spread_kernel(keep, got, *refs):
@@ -269,15 +293,15 @@
     total[...] = keep[...] + got[...]
     for k in range(4):
         parts[k][...] = total[span(ahead(z, k), Z_ROWS)]
-    gram[...] = total[HALF:]
+    gram[...] = total[R:]
 
 
 def spread(keep, got):
     return call(
         spread_kernel,
         "spread",
-        [((Z_ROWS, BLOCK), f32)] * 4 + [((GRAM_ROWS, BLOCK), f32)],
-        scratch_shapes=[pltpu.VMEM((CORE_ROWS, BLOCK), f32)],
+        [((Z_ROWS, WIDTH), f32)] * 4 + [((GRAM_ROWS, WIDTH), f32)],
+        scratch_shapes=[pltpu.VMEM((CORE_ROWS, WIDTH), f32)],
     )(keep, got)
 
 
@@ -289,7 +313,7 @@
     return call(
         settle_kernel,
         "settle",
-        [((GRAM_ROWS, BLOCK), f32)],
+        [((GRAM_ROWS, WIDTH), f32)],
         in_specs=[vmem()] * 4 + [anywhere()],
     )(own, three, one, two, after)[0]
 
@@ -380,7 +404,7 @@
         inverse_kernel,
         "inverse",
         [((R, R), f32)],
-        scratch_shapes=[pltpu.VMEM((R, R), f32), pltpu.VMEM((2 * GRAM_ROWS, BLOCK), f32)],
+        scratch_shapes=[pltpu.VMEM((R, R), f32), pltpu.VMEM((2 * GRAM_ROWS, WIDTH), f32)],
     )(gram, other)[0]
 
 
@@ -394,7 +418,7 @@
     return call(
         ordered_kernel,
         "ordered",
-        [((HALF, BLOCK), f32)],
+        [((R, WIDTH), f32)],
         in_specs=[vmem()] * 4 + [anywhere()],
     )(parts[0], parts[3], parts[1], parts[2], after)[0]
 
@@ -411,45 +435,60 @@
     return call(basis_kernel, "basis", [((BLOCK, R), f32)], 2 * BLOCK * R * R * 6)(*parts, inverse)[0]
 
 
-def reduced_kernel(half, other, inverse, high, low, squares, crossed, line, sem):
-    core = place()[1]
-    crossed[span(core, HALF)] = half[...]
-    crossed[span(1 - core, HALF)] = other[...]
+def reduced_half(crossed, inverse):
     value = piece_dot(pieces(inverse[...], 2), pieces(crossed[...], 2))
     square = value * value
     folded = square[:, :128]
-    for n in range(1, BLOCK // 128):
+    for n in range(1, WIDTH // 128):
         folded = folded + square[:, n * 128 : n * 128 + 128]
-    total = jnp.sum(folded.T, axis=0, keepdims=True)
-    line[...] = jnp.broadcast_to(total[None], line.shape)
+    return value, jnp.sum(folded.T, axis=0, keepdims=True)
+
+
+def own_kernel(crossed, inverse, high, low, squares):
+    value, total = reduced_half(crossed, inverse)
+    high[...], low[...] = pieces(value, 2)
+    squares[...] = jnp.broadcast_to(total, squares.shape)
+
+
+def whole_kernel(crossed, inverse, own_high, own_low, own_squares, high, low, squares, line, sem):
+    core = place()[1]
+    value, total = reduced_half(crossed, inverse)
+    line[...] = jnp.broadcast_to((own_squares[:1] + total)[None], line.shape)
     copy = pltpu.make_async_copy(line, squares, sem)
     copy.start()
-    high[...], low[...] = pieces(value, 2)
+    ours, theirs = span(core, WIDTH), span(1 - core, WIDTH)
+    high[:, ours], low[:, ours] = own_high[...], own_low[...]
+    high[:, theirs], low[:, theirs] = pieces(value, 2)
     copy.wait()
 
 
-def form_reduced(half, other, inverse):
+def form_own(crossed, inverse):
+    return call(
+        own_kernel,
+        "reduced_own",
+        [((R, WIDTH), bf16), ((R, WIDTH), bf16), ((8, R), f32)],
+        2 * WIDTH * R * R * 3,
+    )(crossed, inverse)
+
+
+def form_reduced(crossed, inverse, own):
     return pl.pallas_call(
-        reduced_kernel,
-        in_specs=[vmem()] * 3,
+        whole_kernel,
+        in_specs=[vmem()] * 5,
         out_specs=[vmem(), vmem(), hbm()],
         out_shape=[
             jax.ShapeDtypeStruct((R, BLOCK), bf16),
             jax.ShapeDtypeStruct((R, BLOCK), bf16),
             pltpu.HBM((16, 1, R), f32),
         ],
-        scratch_shapes=[
-            pltpu.VMEM((R, BLOCK), f32),
-            pltpu.VMEM((16, 1, R), f32),
-            pltpu.SemaphoreType.DMA(()),
-        ],
+        scratch_shapes=[pltpu.VMEM((16, 1, R), f32), pltpu.SemaphoreType.DMA(())],
         compiler_params=params(),
-        cost_estimate=cost(2 * BLOCK * R * R * 3, 3 * 2**20),
+        cost_estimate=cost(2 * WIDTH * R * R * 3, 2**20),
         name="reduced",
-    )(half, other, inverse)
-
-
-def momentum_kernel(momentum, gradient, basis, high, low, out, m, g, m_sem, g_sem, o_sem):
+    )(crossed, inverse, *own)
+
+
+def momentum_kernel(momentum, gradient, basis, high, out, m, g, m_sem, g_sem, o_sem):
     reads = [
         (
             pltpu.make_async_copy(momentum.at[tile(n)], m.at[tile(n)], m_sem.at[n]),
@@ -460,10 +499,9 @@
     for pair in reads:
         for copy in pair:
             copy.start()
-    right = [high[...], low[...]]
     writes = []
     for n in range(TILES):
-        product = piece_dot(pieces(basis[tile(n)], 2), right)
+        product = dot(basis[tile(n)].astype(bf16), high[...])
         for copy in reads[n]:
             copy.wait()
         buffer = m[tile(n)] + g[tile(n)].astype(f32)
@@ -474,10 +512,10 @@
         copy.wait()
 
 
-def form_momentum(momentum, gradient, basis, high, low):
+def form_momentum(momentum, gradient, basis, high):
     return pl.pallas_call(
         momentum_kernel,
-        in_specs=[hbm()] * 2 + [vmem()] * 3,
+        in_specs=[hbm()] * 2 + [vmem()] * 2,
         out_specs=hbm(),
         out_shape=jax.ShapeDtypeStruct((BLOCK, BLOCK), f32),
         scratch_shapes=[
@@ -490,7 +528,7 @@
         compiler_params=params(),
         cost_estimate=cost(2 * BLOCK * BLOCK * R * 6, 12 * 2**20),
         name="momentum",
-    )(*[pltpu.with_memory_space_constraint(v, pltpu.HBM) for v in (momentum, gradient)], basis, high, low)
+    )(*[pltpu.with_memory_space_constraint(v, pltpu.HBM) for v in (momentum, gradient)], basis, high)
 
 
 def update_kernel(squares, basis, high, low, update, new_basis, u, v, u_sem, v_sem):
@@ -539,19 +577,23 @@
     parts = [quarter, *to_all(quarter, first_axis)]
 
     sums = ()
-    for k in (0, 2, 1, 3):
+    for k in (0, 2):
         sums = crossed_share(k, momentum, gradient, parts[k], sums)
 
-    keep, give = depart(*sums)
+    core_shape, gram_shape = ((CORE_ROWS, WIDTH), f32), ((R, R), f32)
+    last = (momentum, gradient, parts[3], parts[1], sums[0])
+    give, gram = last_shares(give_kernel, "give", [core_shape, gram_shape], *last, sums[1])
+    (keep,) = last_shares(keep_kernel, "keep", [core_shape], *last, gram)
     *shares, gram = spread(keep, send(give, other_core))
     crossed = sum_four(shares[0], *to_three(shares, along_z))
     gram = settle(gram, *to_all(gram, along_z), crossed)
     inverse = inverse_factor(gram, send(gram, other_core))
     half = ordered([crossed, *to_all(crossed, along_z)], inverse)
     basis = form_basis(parts, inverse)
-    high, low, squares = form_reduced(half, send(half, other_core), inverse)
-    squares = lax.all_to_all(squares, "tp", 0, 0).reshape(16, R)
-    new_momentum = form_momentum(momentum, gradient, basis, high, low)
+    own = form_own(half, inverse)
+    high, low, squares = form_reduced(send(half, other_core), inverse, own)
+    squares = lax.all_to_all(squares, "tp", 0, 0, axis_index_groups=[[8, 9, 10, 11, 12, 13, 14, 15, 0, 1, 2, 3, 4, 5, 6, 7]]).reshape(16, R)
+    new_momentum = form_momentum(momentum, gradient, basis, high)
     update, new_basis = form_update(squares, basis, high, low)
     return (update, new_momentum, new_basis)
 

time: 88.6 us -> 87.1 us (0.983)
  waiting for transfers between devices: 19.3 us -> 16.8 us
  starting transfers between devices: 42.5 us -> 44.4 us
  Pallas kernels: 25.4 us -> 24.4 us
    all_to_all x1, starting transfers between devices: 5.98 us -> 7.86 us  [local(): lax.all_to_all(squares, 'tp', 0, 0, axis_index_groups=[[8, 9, 10, 11, 12,...]
    all_to_all x1, waiting for transfers between devices: 2.08 us -> 0.34 us  [local(): lax.all_to_all(squares, 'tp', 0, 0, axis_index_groups=[[8, 9, 10, 11, 12,...]
    pallas_call x2, Pallas kernels: 6.99 us -> 5.56 us  [the longest x1 4.44 us: form_momentum(): pl.pallas_call(momentum_kernel, in_specs=[hbm()] * 2 + [vmem()] * 2, out_...]
  transfers between devices with their start and end apart: 22 -> 22, of which waited for: 14 -> 15; matrix products, arithmetic and copies ran while one was open for 0% -> 0% of each run, Pallas kernels for 17% -> 17%
where the time goes in v6:
time: 87.1 us; the launch traced here: 86.7 us
  starting transfers between devices  44.4 us (51%)
  Pallas kernels  24.4 us (28%)
  waiting for transfers between devices  16.8 us (19%)
  between operations  0.96 us (1%)
    ppermute x21, starting transfers between devices, send(): return lax.ppermute(value, both, where)  36.5 us
    ppermute x21, waiting for transfers between devices, send(): return lax.ppermute(value, both, where)  16.5 us
    pallas_call x11, Pallas kernels, run(): pl.pallas_call(kernel, in_specs=in_specs or [vmem()] * len(operands), out...  11.4 us
    all_to_all x1, starting transfers between devices, local(): lax.all_to_all(squares, 'tp', 0, 0, axis_index_groups=[[8, 9, 10, 11, 12,...  7.86 us
    pallas_call x1, Pallas kernels, partial_products(): pl.pallas_call(products_kernel, grid=(2,), in_specs=[pl.BlockSpec((half,...  4.72 us
    pallas_call x1, Pallas kernels, form_momentum(): pl.pallas_call(momentum_kernel, in_specs=[hbm()] * 2 + [vmem()] * 2, out_...  4.44 us
    pallas_call x1, Pallas kernels, form_update(): pl.pallas_call(update_kernel, in_specs=[vmem()] * 4, out_specs=[hbm()] *...  2.78 us
  transfers between devices with their start and end apart: 22, of which 15 were waited for; matrix products, arithmetic and copies ran while one was open for 0% of the time, Pallas kernels for 17%

profile of v6, /device:TPU:0, one launch (start us, length us, event | category | flops | bytes accessed | tf_op | source)
XLA Modules:
  0.0 86.7 jit_solution(3775961598897568731)
XLA Ops:
  0.7 4.7 %products.1.partial = f32[1024,256]{1,0:T(8,128)S(1)} custom-call(f32[1024,1024]{1,0:T(8,128)} %momentum.9, bf16[1024,1024]{1,0:T(8,128)(2,1)} %gradient.7, f32[1024,256]{1,0:T(8,128)} %basis.2), custom_call_target="tpu_custom_call" | custom-call | flops 1610612736 | bytes 7340032 | tf_op jit(solution)/shard_map/products/pallas_call | solution.py:176
  5.5 3.2 %collective-permute-start = (f32[256,256]{1,0:T(8,128)S(1)}, f32[256,256]{1,0:T(8,128)S(1)}, u32[]{:S(2)}, u32[]{:S(2)}) collective-permute-start(f32[256,256]{1,0:T(8,128)S(1)} %get-tuple-element.27), channel_id=1, source_target_pairs={{0,2},{1,3},{2,0},{3,1},{4,6},{5,7},{6,4},{7,5},{8,10},{9,11},{10,... | collective-permute-start | bytes 786440 | tf_op jit(solution)/shard_map/ppermute | solution.py:59
  9.3 2.6 %collective-permute-start.2 = (f32[256,256]{1,0:T(8,128)S(1)}, f32[256,256]{1,0:T(8,128)S(1)}, u32[]{:S(2)}, u32[]{:S(2)}) collective-permute-start(f32[256,256]{1,0:T(8,128)S(1)} %get-tuple-element.29), channel_id=1, source_target_pairs={{0,3},{1,0},{2,1},{3,2},{4,7},{5,4},{6,5},{7,6},{8,11},{9,8},{10,9... | collective-permute-start | bytes 786440 | tf_op jit(solution)/shard_map/ppermute | solution.py:59
  11.9 1.5 %collective-permute-done = f32[256,256]{1,0:T(8,128)S(1)} collective-permute-done((f32[256,256]{1,0:T(8,128)S(1)}, f32[256,256]{1,0:T(8,128)S(1)}, u32[]{:S(2)}, u32[]{:S(2)}) %collective-permute-start) | collective-permute-done | bytes 262176 | tf_op jit(solution)/shard_map/ppermute | solution.py:59
  13.4 2.8 %collective-permute-done.1 = f32[256,256]{1,0:T(8,128)S(1)} collective-permute-done((f32[256,256]{1,0:T(8,128)S(1)}, f32[256,256]{1,0:T(8,128)S(1)}, u32[]{:S(2)}, u32[]{:S(2)}) %collective-permute-start.1) | collective-permute-done | bytes 262176 | tf_op jit(solution)/shard_map/ppermute | solution.py:59
  16.5 3.3 %collective-permute-start.5 = (f32[256,256]{1,0:T(8,128)S(1)}, f32[256,256]{1,0:T(8,128)S(1)}, u32[]{:S(2)}, u32[]{:S(2)}) collective-permute-start(f32[256,256]{1,0:T(8,128)S(1)} %add_add_fusion.1), channel_id=1, source_target_pairs={{0,8},{1,9},{2,10},{3,11},{4,12},{5,13},{6,14},{7,15},{8,0},{9,1},... | collective-permute-start | bytes 786440 | tf_op jit(solution)/shard_map/ppermute | solution.py:59
  20.4 2.6 %collective-permute-start.3 = (f32[256,256]{1,0:T(8,128)S(1)}, f32[256,256]{1,0:T(8,128)S(1)}, u32[]{:S(2)}, u32[]{:S(2)}) collective-permute-start(f32[256,256]{1,0:T(8,128)S(1)} %add_add_fusion.1), channel_id=1, source_target_pairs={{0,12},{1,13},{2,14},{3,15},{4,0},{5,1},{6,2},{7,3},{8,4},{9,5},{1... | collective-permute-start | bytes 786440 | tf_op jit(solution)/shard_map/ppermute | solution.py:59
  23.0 1.4 %collective-permute-done.5 = f32[256,256]{1,0:T(8,128)S(1)} collective-permute-done((f32[256,256]{1,0:T(8,128)S(1)}, f32[256,256]{1,0:T(8,128)S(1)}, u32[]{:S(2)}, u32[]{:S(2)}) %collective-permute-start.5) | collective-permute-done | bytes 262176 | tf_op jit(solution)/shard_map/ppermute | solution.py:59
  24.4 2.9 %collective-permute-done.4 = f32[256,256]{1,0:T(8,128)S(1)} collective-permute-done((f32[256,256]{1,0:T(8,128)S(1)}, f32[256,256]{1,0:T(8,128)S(1)}, u32[]{:S(2)}, u32[]{:S(2)}) %collective-permute-start.4) | collective-permute-done | bytes 262176 | tf_op jit(solution)/shard_map/ppermute | solution.py:59
  27.7 2.2 %collective-permute-start.8 = (f32[256,256]{1,0:T(8,128)S(1)}, f32[256,256]{1,0:T(8,128)S(1)}, u32[]{:S(2)}, u32[]{:S(2)}) collective-permute-start(f32[256,256]{1,0:T(8,128)S(1)} %add_add_fusion.refs_2_.own), channel_id=1, source_target_pairs={{0,2},{1,3},{2,0},{3,1},{4,6},{5,7},{6,4},{7,5},{8,10},{9,11},{10,... | collective-permute-start | bytes 786440 | tf_op jit(solution)/shard_map/ppermute | solution.py:59
  29.8 1.9 %collective-permute-start.7 = (f32[256,256]{1,0:T(8,128)S(1)}, f32[256,256]{1,0:T(8,128)S(1)}, u32[]{:S(2)}, u32[]{:S(2)}) collective-permute-start(f32[256,256]{1,0:T(8,128)S(1)} %add_add_fusion.refs_2_.own), channel_id=1, source_target_pairs={{0,1},{1,2},{2,3},{3,0},{4,5},{5,6},{6,7},{7,4},{8,9},{9,10},{10,1... | collective-permute-start | bytes 786440 | tf_op jit(solution)/shard_map/ppermute | solution.py:59
  31.7 1.4 %collective-permute-start.6 = (f32[256,256]{1,0:T(8,128)S(1)}, f32[256,256]{1,0:T(8,128)S(1)}, u32[]{:S(2)}, u32[]{:S(2)}) collective-permute-start(f32[256,256]{1,0:T(8,128)S(1)} %add_add_fusion.refs_2_.own), channel_id=1, source_target_pairs={{0,3},{1,0},{2,1},{3,2},{4,7},{5,4},{6,5},{7,6},{8,11},{9,8},{10,9... | collective-permute-start | bytes 786440 | tf_op jit(solution)/shard_map/ppermute | solution.py:59
  33.9 1.8 %collective-permute-done.8.refs_2_.two = f32[256,256]{1,0:T(8,128)S(1)} collective-permute-done((f32[256,256]{1,0:T(8,128)S(1)}, f32[256,256]{1,0:T(8,128)S(1)}, u32[]{:S(2)}, u32[]{:S(2)}) %collective-permute-start.8) | collective-permute-done | bytes 262176 | tf_op jit(solution)/shard_map/ppermute | solution.py:59
  36.6 1.8 %collective-permute-done.7.one = f32[256,256]{1,0:T(8,128)S(1)} collective-permute-done((f32[256,256]{1,0:T(8,128)S(1)}, f32[256,256]{1,0:T(8,128)S(1)}, u32[]{:S(2)}, u32[]{:S(2)}) %collective-permute-start.7) | collective-permute-done | bytes 262176 | tf_op jit(solution)/shard_map/ppermute | solution.py:59
  40.7 1.4 %collective-permute-done.9.got = f32[304,512]{1,0:T(8,128)S(1)} collective-permute-done((f32[304,512]{1,0:T(8,128)S(1)}, f32[304,512]{1,0:T(8,128)S(1)}, u32[]{:S(2)}, u32[]{:S(2)}) %collective-permute-start.9) | collective-permute-done | bytes 622624 | tf_op jit(solution)/shard_map/ppermute | solution.py:59
  42.2 4.0 %collective-permute-start.10 = (f32[64,512]{1,0:T(8,128)S(1)}, f32[64,512]{1,0:T(8,128)S(1)}, u32[]{:S(2)}, u32[]{:S(2)}) collective-permute-start(f32[64,512]{1,0:T(8,128)S(1)} %get-tuple-element.37), channel_id=1, source_target_pairs={{0,64},{1,65},{2,66},{3,67},{4,68},{5,69},{6,70},{7,71},{8,72},{9,... | collective-permute-start | bytes 393224 | tf_op jit(solution)/shard_map/ppermute | solution.py:59
  47.2 2.2 %collective-permute-start.12 = (f32[64,512]{1,0:T(8,128)S(1)}, f32[64,512]{1,0:T(8,128)S(1)}, u32[]{:S(2)}, u32[]{:S(2)}) collective-permute-start(f32[64,512]{1,0:T(8,128)S(1)} %get-tuple-element.39), channel_id=1, source_target_pairs={{0,96},{1,97},{2,98},{3,99},{4,100},{5,101},{6,102},{7,103},{8,104... | collective-permute-start | bytes 393224 | tf_op jit(solution)/shard_map/ppermute | solution.py:59
  50.4 3.7 %collective-permute-start.16 = (f32[48,512]{1,0:T(8,128)S(1)}, f32[48,512]{1,0:T(8,128)S(1)}, u32[]{:S(2)}, u32[]{:S(2)}) collective-permute-start(f32[48,512]{1,0:T(8,128)S(1)} %get-tuple-element.40.own), channel_id=1, source_target_pairs={{0,96},{1,97},{2,98},{3,99},{4,100},{5,101},{6,102},{7,103},{8,104... | collective-permute-start | bytes 294920 | tf_op jit(solution)/shard_map/ppermute | solution.py:59
  54.4 2.6 %collective-permute-start.15 = (f32[64,512]{1,0:T(8,128)S(1)}, f32[64,512]{1,0:T(8,128)S(1)}, u32[]{:S(2)}, u32[]{:S(2)}) collective-permute-start(f32[64,512]{1,0:T(8,128)S(1)} %add_add_fusion.2.after.own), channel_id=1, source_target_pairs={{0,64},{1,65},{2,66},{3,67},{4,68},{5,69},{6,70},{7,71},{8,72},{9,... | collective-permute-start | bytes 393224 | tf_op jit(solution)/shard_map/ppermute | solution.py:59
  57.0 2.2 %collective-permute-start.14 = (f32[64,512]{1,0:T(8,128)S(1)}, f32[64,512]{1,0:T(8,128)S(1)}, u32[]{:S(2)}, u32[]{:S(2)}) collective-permute-start(f32[64,512]{1,0:T(8,128)S(1)} %add_add_fusion.2.after.own), channel_id=1, source_target_pairs={{0,32},{1,33},{2,34},{3,35},{4,36},{5,37},{6,38},{7,39},{8,40},{9,... | collective-permute-start | bytes 393224 | tf_op jit(solution)/shard_map/ppermute | solution.py:59
  61.8 6.1 %inverse.1.after = f32[256,256]{1,0:T(8,128)S(1)} custom-call(f32[48,512]{1,0:T(8,128)S(1)} %settle.1.gram, f32[48,512]{1,0:T(8,128)S(1)} %collective-permute-done.19.other), custom_call_target="tpu_custom_call" | custom-call | bytes 65536 | tf_op jit(solution)/shard_map/inverse/pallas_call | solution.py:145
  71.2 7.9 %all-to-all-start = ((f32[16,1,256]{2,1,0:T(1,128)}), f32[16,1,256]{2,1,0:T(1,128)S(1)}, u32[]{:S(2)}, u32[]{:S(2)}) async-start(f32[16,1,256]{2,1,0:T(1,128)} %get-tuple-element.44), calls=%async_computation | async-start | bytes 32768 | tf_op jit(solution)/shard_map/all_to_all | solution.py:595
  79.0 4.4 %momentum.8 = f32[1024,1024]{1,0:T(8,128)} custom-call(f32[1024,1024]{1,0:T(8,128)} %momentum.9, bf16[1024,1024]{1,0:T(8,128)(2,1)} %gradient.7, f32[1024,256]{1,0:T(8,128)S(1)} %basis.3, bf16[256,1024]{1,0:T(8,128)(2,1)S(1)} %get-tuple-element.45.high), custom_call_target="tpu_custom_call" | custom-call | flops 3221225472 | bytes 12582912 | tf_op jit(solution)/shard_map/momentum/pallas_call | solution.py:516
  83.8 2.8 %update.1 = (bf16[1024,1024]{1,0:T(8,128)(2,1)}, f32[1024,256]{1,0:T(8,128)}) custom-call(f32[16,256]{1,0:T(8,128)S(1)} %bitcast.3, f32[1024,256]{1,0:T(8,128)S(1)} %basis.3, bf16[256,1024]{1,0:T(8,128)(2,1)S(1)} %get-tuple-element.45.high, bf16[256,1024]{1,0:T(8,128)(2,1)S(1)} %get-tuple-element.46.low), custom_call_target="tpu_custom_call" | custom-call | flops 3221225472 | bytes 6291456 | tf_op jit(solution)/shard_map/update/pallas_call | solution.py:552
  (43 shorter events, 14.4 us)
Async XLA Ops:
  0.6 32.4 %copy-start.1 = (bf16[1024,1024]{1,0:T(8,128)(2,1)S(1)}, bf16[1024,1024]{1,0:T(8,128)(2,1)}, u32[]{:S(2)}) copy-start(bf16[1024,1024]{1,0:T(8,128)(2,1)} %gradient.7) | copy-start | bytes 6291460
  0.6 32.4 %copy-start = (f32[1024,1024]{1,0:T(8,128)S(1)}, f32[1024,1024]{1,0:T(8,128)}, u32[]{:S(2)}) copy-start(f32[1024,1024]{1,0:T(8,128)} %momentum.9) | copy-start | bytes 12582916
  5.5 8.0 %collective-permute-start = (f32[256,256]{1,0:T(8,128)S(1)}, f32[256,256]{1,0:T(8,128)S(1)}, u32[]{:S(2)}, u32[]{:S(2)}) collective-permute-start(f32[256,256]{1,0:T(8,128)S(1)} %get-tuple-element.27), channel_id=1, source_target_pairs={{0,2},{1,3},{2,0},{3,1},{4,6},{5,7},{6,4},{7,5},{8,10},{9,11},{10,... | collective-permute-start | bytes 786440 | tf_op jit(solution)/shard_map/ppermute | solution.py:59
  8.7 7.6 %collective-permute-start.1 = (f32[256,256]{1,0:T(8,128)S(1)}, f32[256,256]{1,0:T(8,128)S(1)}, u32[]{:S(2)}, u32[]{:S(2)}) collective-permute-start(f32[256,256]{1,0:T(8,128)S(1)} %get-tuple-element.28), channel_id=1, source_target_pairs={{0,1},{1,2},{2,3},{3,0},{4,5},{5,6},{6,7},{7,4},{8,9},{9,10},{10,1... | collective-permute-start | bytes 786440 | tf_op jit(solution)/shard_map/ppermute | solution.py:59
  9.3 7.2 %collective-permute-start.2 = (f32[256,256]{1,0:T(8,128)S(1)}, f32[256,256]{1,0:T(8,128)S(1)}, u32[]{:S(2)}, u32[]{:S(2)}) collective-permute-start(f32[256,256]{1,0:T(8,128)S(1)} %get-tuple-element.29), channel_id=1, source_target_pairs={{0,3},{1,0},{2,1},{3,2},{4,7},{5,4},{6,5},{7,6},{8,11},{9,8},{10,9... | collective-permute-start | bytes 786440 | tf_op jit(solution)/shard_map/ppermute | solution.py:59
  16.5 8.0 %collective-permute-start.5 = (f32[256,256]{1,0:T(8,128)S(1)}, f32[256,256]{1,0:T(8,128)S(1)}, u32[]{:S(2)}, u32[]{:S(2)}) collective-permute-start(f32[256,256]{1,0:T(8,128)S(1)} %add_add_fusion.1), channel_id=1, source_target_pairs={{0,8},{1,9},{2,10},{3,11},{4,12},{5,13},{6,14},{7,15},{8,0},{9,1},... | collective-permute-start | bytes 786440 | tf_op jit(solution)/shard_map/ppermute | solution.py:59
  19.8 7.6 %collective-permute-start.4 = (f32[256,256]{1,0:T(8,128)S(1)}, f32[256,256]{1,0:T(8,128)S(1)}, u32[]{:S(2)}, u32[]{:S(2)}) collective-permute-start(f32[256,256]{1,0:T(8,128)S(1)} %add_add_fusion.1), channel_id=1, source_target_pairs={{0,4},{1,5},{2,6},{3,7},{4,8},{5,9},{6,10},{7,11},{8,12},{9,13},{1... | collective-permute-start | bytes 786440 | tf_op jit(solution)/shard_map/ppermute | solution.py:59
  20.4 7.2 %collective-permute-start.3 = (f32[256,256]{1,0:T(8,128)S(1)}, f32[256,256]{1,0:T(8,128)S(1)}, u32[]{:S(2)}, u32[]{:S(2)}) collective-permute-start(f32[256,256]{1,0:T(8,128)S(1)} %add_add_fusion.1), channel_id=1, source_target_pairs={{0,12},{1,13},{2,14},{3,15},{4,0},{5,1},{6,2},{7,3},{8,4},{9,5},{1... | collective-permute-start | bytes 786440 | tf_op jit(solution)/shard_map/ppermute | solution.py:59
  27.7 8.1 %collective-permute-start.8 = (f32[256,256]{1,0:T(8,128)S(1)}, f32[256,256]{1,0:T(8,128)S(1)}, u32[]{:S(2)}, u32[]{:S(2)}) collective-permute-start(f32[256,256]{1,0:T(8,128)S(1)} %add_add_fusion.refs_2_.own), channel_id=1, source_target_pairs={{0,2},{1,3},{2,0},{3,1},{4,6},{5,7},{6,4},{7,5},{8,10},{9,11},{10,... | collective-permute-start | bytes 786440 | tf_op jit(solution)/shard_map/ppermute | solution.py:59
  29.8 8.6 %collective-permute-start.7 = (f32[256,256]{1,0:T(8,128)S(1)}, f32[256,256]{1,0:T(8,128)S(1)}, u32[]{:S(2)}, u32[]{:S(2)}) collective-permute-start(f32[256,256]{1,0:T(8,128)S(1)} %add_add_fusion.refs_2_.own), channel_id=1, source_target_pairs={{0,1},{1,2},{2,3},{3,0},{4,5},{5,6},{6,7},{7,4},{8,9},{9,10},{10,1... | collective-permute-start | bytes 786440 | tf_op jit(solution)/shard_map/ppermute | solution.py:59
  31.7 7.2 %collective-permute-start.6 = (f32[256,256]{1,0:T(8,128)S(1)}, f32[256,256]{1,0:T(8,128)S(1)}, u32[]{:S(2)}, u32[]{:S(2)}) collective-permute-start(f32[256,256]{1,0:T(8,128)S(1)} %add_add_fusion.refs_2_.own), channel_id=1, source_target_pairs={{0,3},{1,0},{2,1},{3,2},{4,7},{5,4},{6,5},{7,6},{8,11},{9,8},{10,9... | collective-permute-start | bytes 786440 | tf_op jit(solution)/shard_map/ppermute | solution.py:59
  39.9 2.1 %collective-permute-start.9 = (f32[304,512]{1,0:T(8,128)S(1)}, f32[304,512]{1,0:T(8,128)S(1)}, u32[]{:S(2)}, u32[]{:S(2)}) collective-permute-start(f32[304,512]{1,0:T(8,128)S(1)} %get-tuple-element.35), channel_id=1, source_target_pairs={{0,16},{1,17},{2,18},{3,19},{4,20},{5,21},{6,22},{7,23},{8,24},{9,... | collective-permute-start | bytes 1867784 | tf_op jit(solution)/shard_map/ppermute | solution.py:59
  42.2 8.2 %collective-permute-start.10 = (f32[64,512]{1,0:T(8,128)S(1)}, f32[64,512]{1,0:T(8,128)S(1)}, u32[]{:S(2)}, u32[]{:S(2)}) collective-permute-start(f32[64,512]{1,0:T(8,128)S(1)} %get-tuple-element.37), channel_id=1, source_target_pairs={{0,64},{1,65},{2,66},{3,67},{4,68},{5,69},{6,70},{7,71},{8,72},{9,... | collective-permute-start | bytes 393224 | tf_op jit(solution)/shard_map/ppermute | solution.py:59
  46.1 8.2 %collective-permute-start.11 = (f32[64,512]{1,0:T(8,128)S(1)}, f32[64,512]{1,0:T(8,128)S(1)}, u32[]{:S(2)}, u32[]{:S(2)}) collective-permute-start(f32[64,512]{1,0:T(8,128)S(1)} %get-tuple-element.38), channel_id=1, source_target_pairs={{0,32},{1,33},{2,34},{3,35},{4,36},{5,37},{6,38},{7,39},{8,40},{9,... | collective-permute-start | bytes 393224 | tf_op jit(solution)/shard_map/ppermute | solution.py:59
  47.2 7.2 %collective-permute-start.12 = (f32[64,512]{1,0:T(8,128)S(1)}, f32[64,512]{1,0:T(8,128)S(1)}, u32[]{:S(2)}, u32[]{:S(2)}) collective-permute-start(f32[64,512]{1,0:T(8,128)S(1)} %get-tuple-element.39), channel_id=1, source_target_pairs={{0,96},{1,97},{2,98},{3,99},{4,100},{5,101},{6,102},{7,103},{8,104... | collective-permute-start | bytes 393224 | tf_op jit(solution)/shard_map/ppermute | solution.py:59
  49.4 9.9 %collective-permute-start.18 = (f32[48,512]{1,0:T(8,128)S(1)}, f32[48,512]{1,0:T(8,128)S(1)}, u32[]{:S(2)}, u32[]{:S(2)}) collective-permute-start(f32[48,512]{1,0:T(8,128)S(1)} %get-tuple-element.40.own), channel_id=1, source_target_pairs={{0,64},{1,65},{2,66},{3,67},{4,68},{5,69},{6,70},{7,71},{8,72},{9,... | collective-permute-start | bytes 294920 | tf_op jit(solution)/shard_map/ppermute | solution.py:59
  49.4 10.9 %collective-permute-start.17 = (f32[48,512]{1,0:T(8,128)S(1)}, f32[48,512]{1,0:T(8,128)S(1)}, u32[]{:S(2)}, u32[]{:S(2)}) collective-permute-start(f32[48,512]{1,0:T(8,128)S(1)} %get-tuple-element.40.own), channel_id=1, source_target_pairs={{0,32},{1,33},{2,34},{3,35},{4,36},{5,37},{6,38},{7,39},{8,40},{9,... | collective-permute-start | bytes 294920 | tf_op jit(solution)/shard_map/ppermute | solution.py:59
  50.4 9.8 %collective-permute-start.16 = (f32[48,512]{1,0:T(8,128)S(1)}, f32[48,512]{1,0:T(8,128)S(1)}, u32[]{:S(2)}, u32[]{:S(2)}) collective-permute-start(f32[48,512]{1,0:T(8,128)S(1)} %get-tuple-element.40.own), channel_id=1, source_target_pairs={{0,96},{1,97},{2,98},{3,99},{4,100},{5,101},{6,102},{7,103},{8,104... | collective-permute-start | bytes 294920 | tf_op jit(solution)/shard_map/ppermute | solution.py:59
  54.4 13.5 %collective-permute-start.15 = (f32[64,512]{1,0:T(8,128)S(1)}, f32[64,512]{1,0:T(8,128)S(1)}, u32[]{:S(2)}, u32[]{:S(2)}) collective-permute-start(f32[64,512]{1,0:T(8,128)S(1)} %add_add_fusion.2.after.own), channel_id=1, source_target_pairs={{0,64},{1,65},{2,66},{3,67},{4,68},{5,69},{6,70},{7,71},{8,72},{9,... | collective-permute-start | bytes 393224 | tf_op jit(solution)/shard_map/ppermute | solution.py:59
  57.0 10.9 %collective-permute-start.14 = (f32[64,512]{1,0:T(8,128)S(1)}, f32[64,512]{1,0:T(8,128)S(1)}, u32[]{:S(2)}, u32[]{:S(2)}) collective-permute-start(f32[64,512]{1,0:T(8,128)S(1)} %add_add_fusion.2.after.own), channel_id=1, source_target_pairs={{0,32},{1,33},{2,34},{3,35},{4,36},{5,37},{6,38},{7,39},{8,40},{9,... | collective-permute-start | bytes 393224 | tf_op jit(solution)/shard_map/ppermute | solution.py:59
  59.2 8.7 %collective-permute-start.13 = (f32[64,512]{1,0:T(8,128)S(1)}, f32[64,512]{1,0:T(8,128)S(1)}, u32[]{:S(2)}, u32[]{:S(2)}) collective-permute-start(f32[64,512]{1,0:T(8,128)S(1)} %add_add_fusion.2.after.own), channel_id=1, source_target_pairs={{0,96},{1,97},{2,98},{3,99},{4,100},{5,101},{6,102},{7,103},{8,104... | collective-permute-start | bytes 393224 | tf_op jit(solution)/shard_map/ppermute | solution.py:59
  60.3 1.6 %collective-permute-start.19 = (f32[48,512]{1,0:T(8,128)S(1)}, f32[48,512]{1,0:T(8,128)S(1)}, u32[]{:S(2)}, u32[]{:S(2)}) collective-permute-start(f32[48,512]{1,0:T(8,128)S(1)} %settle.1.gram), channel_id=1, source_target_pairs={{0,16},{1,17},{2,18},{3,19},{4,20},{5,21},{6,22},{7,23},{8,24},{9,... | collective-permute-start | bytes 294920 | tf_op jit(solution)/shard_map/ppermute | solution.py:59
  68.0 2.0 %collective-permute-start.20 = (f32[256,512]{1,0:T(8,128)S(1)}, f32[256,512]{1,0:T(8,128)S(1)}, u32[]{:S(2)}, u32[]{:S(2)}) collective-permute-start(f32[256,512]{1,0:T(8,128)S(1)} %ordered.1.crossed), channel_id=1, source_target_pairs={{0,16},{1,17},{2,18},{3,19},{4,20},{5,21},{6,22},{7,23},{8,24},{9,... | collective-permute-start | bytes 1572872 | tf_op jit(solution)/shard_map/ppermute | solution.py:59
  71.2 12.6 %all-to-all-start = ((f32[16,1,256]{2,1,0:T(1,128)}), f32[16,1,256]{2,1,0:T(1,128)S(1)}, u32[]{:S(2)}, u32[]{:S(2)}) async-start(f32[16,1,256]{2,1,0:T(1,128)} %get-tuple-element.44), calls=%async_computation | async-start | bytes 32768 | tf_op jit(solution)/shard_map/all_to_all | solution.py:595

commit v7 on v6

--- a/solution.py
+++ b/solution.py
@@ -334,9 +334,10 @@
     later = [column(a[0], c) for c in range(8)]
     for t in range(tiles):
         start = 8 * t
-        diagonal, factors, inverses, upper = later, {}, [], {}
+        diagonal, inverses, upper = later, [], {}
         if t + 1 < tiles:
-            below = [column(a[t + 1], start + c) for c in range(8)]
+            untouched = [column(a[t + 1], start + c) for c in range(8)]
+            below = list(untouched)
             later = [column(a[t + 1], start + 8 + c) for c in range(8)]
         own, scale = [], None
         for c in range(8):
@@ -349,9 +350,7 @@
                 diagonal[d] = diagonal[d] - own[c] * upper[c, d]
         scales.append(scale)
         if t + 1 < tiles:
-            factors[t + 1] = []
             for c in range(8):
-                factors[t + 1].append(below[c])
                 for d in range(c + 1, 8):
                     below[d] = below[d] - below[c] * upper[c, d]
                 scaled = below[c] * inverses[c]
@@ -363,17 +362,16 @@
             value = jnp.where((lane == start + c) & (sub > c), 0.0, value) - own[c] * line
             rows.append(jnp.where((lane > start + c) & (lane < start + 8), 0.0, line))
         a[t] = value
+        for c in range(6, -1, -1):
+            for d in range(c + 1, 8):
+                rows[c] = rows[c] - upper[c, d] * rows[d]
         group = (lane >= start) & (lane < start + 8)
         for n in range(t + 1, tiles):
-            if n not in factors:
-                columns, factors[n] = [column(a[n], start + c) for c in range(8)], []
-                for c in range(8):
-                    factors[n].append(columns[c])
-                    for d in range(c + 1, 8):
-                        columns[d] = columns[d] - columns[c] * upper[c, d]
+            if n > t + 1:
+                untouched = [column(a[n], start + c) for c in range(8)]
             total = jnp.where(group, 0.0, a[n])
             for c in range(8):
-                total = total - factors[n][c] * rows[c]
+                total = total - untouched[c] * rows[c]
             a[n] = total
     out = []
     for t in range(tiles):

time: 87.1 us -> 86.7 us (level)
  transfers between devices with their start and end apart: 22 -> 22, of which waited for: 15 -> 15; matrix products, arithmetic and copies ran while one was open for 0% -> 0% of each run, Pallas kernels for 17% -> 16%
where the time goes in v7:
time: 86.7 us; the launch traced here: 86.4 us
  starting transfers between devices  44.4 us (51%)
  Pallas kernels  24 us (28%)
  waiting for transfers between devices  16.8 us (19%)
  between operations  0.96 us (1%)
    ppermute x21, starting transfers between devices, send(): return lax.ppermute(value, both, where)  36.5 us
    ppermute x21, waiting for transfers between devices, send(): return lax.ppermute(value, both, where)  16.5 us
    pallas_call x11, Pallas kernels, run(): pl.pallas_call(kernel, in_specs=in_specs or [vmem()] * len(operands), out...  11 us
    all_to_all x1, starting transfers between devices, local(): lax.all_to_all(squares, 'tp', 0, 0, axis_index_groups=[[8, 9, 10, 11, 12,...  7.86 us
    pallas_call x1, Pallas kernels, partial_products(): pl.pallas_call(products_kernel, grid=(2,), in_specs=[pl.BlockSpec((half,...  4.72 us
    pallas_call x1, Pallas kernels, form_momentum(): pl.pallas_call(momentum_kernel, in_specs=[hbm()] * 2 + [vmem()] * 2, out_...  4.44 us
    pallas_call x1, Pallas kernels, form_update(): pl.pallas_call(update_kernel, in_specs=[vmem()] * 4, out_specs=[hbm()] *...  2.79 us
  transfers between devices with their start and end apart: 22, of which 15 were waited for; matrix products, arithmetic and copies ran while one was open for 0% of the time, Pallas kernels for 16%

profile of v7, /device:TPU:0, one launch (start us, length us, event | category | flops | bytes accessed | tf_op | source)
XLA Modules:
  0.0 86.4 jit_solution(14583511285171281260)
XLA Ops:
  0.7 4.7 %products.1.partial = f32[1024,256]{1,0:T(8,128)S(1)} custom-call(f32[1024,1024]{1,0:T(8,128)} %momentum.9, bf16[1024,1024]{1,0:T(8,128)(2,1)} %gradient.7, f32[1024,256]{1,0:T(8,128)} %basis.2), custom_call_target="tpu_custom_call" | custom-call | flops 1610612736 | bytes 7340032 | tf_op jit(solution)/shard_map/products/pallas_call | solution.py:176
  5.5 3.2 %collective-permute-start = (f32[256,256]{1,0:T(8,128)S(1)}, f32[256,256]{1,0:T(8,128)S(1)}, u32[]{:S(2)}, u32[]{:S(2)}) collective-permute-start(f32[256,256]{1,0:T(8,128)S(1)} %get-tuple-element.27), channel_id=1, source_target_pairs={{0,2},{1,3},{2,0},{3,1},{4,6},{5,7},{6,4},{7,5},{8,10},{9,11},{10,... | collective-permute-start | bytes 786440 | tf_op jit(solution)/shard_map/ppermute | solution.py:59
  9.3 2.6 %collective-permute-start.2 = (f32[256,256]{1,0:T(8,128)S(1)}, f32[256,256]{1,0:T(8,128)S(1)}, u32[]{:S(2)}, u32[]{:S(2)}) collective-permute-start(f32[256,256]{1,0:T(8,128)S(1)} %get-tuple-element.29), channel_id=1, source_target_pairs={{0,3},{1,0},{2,1},{3,2},{4,7},{5,4},{6,5},{7,6},{8,11},{9,8},{10,9... | collective-permute-start | bytes 786440 | tf_op jit(solution)/shard_map/ppermute | solution.py:59
  11.9 1.5 %collective-permute-done = f32[256,256]{1,0:T(8,128)S(1)} collective-permute-done((f32[256,256]{1,0:T(8,128)S(1)}, f32[256,256]{1,0:T(8,128)S(1)}, u32[]{:S(2)}, u32[]{:S(2)}) %collective-permute-start) | collective-permute-done | bytes 262176 | tf_op jit(solution)/shard_map/ppermute | solution.py:59
  13.4 2.8 %collective-permute-done.1 = f32[256,256]{1,0:T(8,128)S(1)} collective-permute-done((f32[256,256]{1,0:T(8,128)S(1)}, f32[256,256]{1,0:T(8,128)S(1)}, u32[]{:S(2)}, u32[]{:S(2)}) %collective-permute-start.1) | collective-permute-done | bytes 262176 | tf_op jit(solution)/shard_map/ppermute | solution.py:59
  16.5 3.3 %collective-permute-start.5 = (f32[256,256]{1,0:T(8,128)S(1)}, f32[256,256]{1,0:T(8,128)S(1)}, u32[]{:S(2)}, u32[]{:S(2)}) collective-permute-start(f32[256,256]{1,0:T(8,128)S(1)} %add_add_fusion.1), channel_id=1, source_target_pairs={{0,8},{1,9},{2,10},{3,11},{4,12},{5,13},{6,14},{7,15},{8,0},{9,1},... | collective-permute-start | bytes 786440 | tf_op jit(solution)/shard_map/ppermute | solution.py:59
  20.4 2.6 %collective-permute-start.3 = (f32[256,256]{1,0:T(8,128)S(1)}, f32[256,256]{1,0:T(8,128)S(1)}, u32[]{:S(2)}, u32[]{:S(2)}) collective-permute-start(f32[256,256]{1,0:T(8,128)S(1)} %add_add_fusion.1), channel_id=1, source_target_pairs={{0,12},{1,13},{2,14},{3,15},{4,0},{5,1},{6,2},{7,3},{8,4},{9,5},{1... | collective-permute-start | bytes 786440 | tf_op jit(solution)/shard_map/ppermute | solution.py:59
  23.0 1.4 %collective-permute-done.5 = f32[256,256]{1,0:T(8,128)S(1)} collective-permute-done((f32[256,256]{1,0:T(8,128)S(1)}, f32[256,256]{1,0:T(8,128)S(1)}, u32[]{:S(2)}, u32[]{:S(2)}) %collective-permute-start.5) | collective-permute-done | bytes 262176 | tf_op jit(solution)/shard_map/ppermute | solution.py:59
  24.4 2.9 %collective-permute-done.4 = f32[256,256]{1,0:T(8,128)S(1)} collective-permute-done((f32[256,256]{1,0:T(8,128)S(1)}, f32[256,256]{1,0:T(8,128)S(1)}, u32[]{:S(2)}, u32[]{:S(2)}) %collective-permute-start.4) | collective-permute-done | bytes 262176 | tf_op jit(solution)/shard_map/ppermute | solution.py:59
  27.7 2.2 %collective-permute-start.8 = (f32[256,256]{1,0:T(8,128)S(1)}, f32[256,256]{1,0:T(8,128)S(1)}, u32[]{:S(2)}, u32[]{:S(2)}) collective-permute-start(f32[256,256]{1,0:T(8,128)S(1)} %add_add_fusion.refs_2_.own), channel_id=1, source_target_pairs={{0,2},{1,3},{2,0},{3,1},{4,6},{5,7},{6,4},{7,5},{8,10},{9,11},{10,... | collective-permute-start | bytes 786440 | tf_op jit(solution)/shard_map/ppermute | solution.py:59
  29.8 1.9 %collective-permute-start.7 = (f32[256,256]{1,0:T(8,128)S(1)}, f32[256,256]{1,0:T(8,128)S(1)}, u32[]{:S(2)}, u32[]{:S(2)}) collective-permute-start(f32[256,256]{1,0:T(8,128)S(1)} %add_add_fusion.refs_2_.own), channel_id=1, source_target_pairs={{0,1},{1,2},{2,3},{3,0},{4,5},{5,6},{6,7},{7,4},{8,9},{9,10},{10,1... | collective-permute-start | bytes 786440 | tf_op jit(solution)/shard_map/ppermute | solution.py:59
  31.7 1.4 %collective-permute-start.6 = (f32[256,256]{1,0:T(8,128)S(1)}, f32[256,256]{1,0:T(8,128)S(1)}, u32[]{:S(2)}, u32[]{:S(2)}) collective-permute-start(f32[256,256]{1,0:T(8,128)S(1)} %add_add_fusion.refs_2_.own), channel_id=1, source_target_pairs={{0,3},{1,0},{2,1},{3,2},{4,7},{5,4},{6,5},{7,6},{8,11},{9,8},{10,9... | collective-permute-start | bytes 786440 | tf_op jit(solution)/shard_map/ppermute | solution.py:59
  33.9 1.8 %collective-permute-done.8.refs_2_.two = f32[256,256]{1,0:T(8,128)S(1)} collective-permute-done((f32[256,256]{1,0:T(8,128)S(1)}, f32[256,256]{1,0:T(8,128)S(1)}, u32[]{:S(2)}, u32[]{:S(2)}) %collective-permute-start.8) | collective-permute-done | bytes 262176 | tf_op jit(solution)/shard_map/ppermute | solution.py:59
  36.6 1.8 %collective-permute-done.7.one = f32[256,256]{1,0:T(8,128)S(1)} collective-permute-done((f32[256,256]{1,0:T(8,128)S(1)}, f32[256,256]{1,0:T(8,128)S(1)}, u32[]{:S(2)}, u32[]{:S(2)}) %collective-permute-start.7) | collective-permute-done | bytes 262176 | tf_op jit(solution)/shard_map/ppermute | solution.py:59
  40.7 1.4 %collective-permute-done.9.got = f32[304,512]{1,0:T(8,128)S(1)} collective-permute-done((f32[304,512]{1,0:T(8,128)S(1)}, f32[304,512]{1,0:T(8,128)S(1)}, u32[]{:S(2)}, u32[]{:S(2)}) %collective-permute-start.9) | collective-permute-done | bytes 622624 | tf_op jit(solution)/shard_map/ppermute | solution.py:59
  42.2 4.0 %collective-permute-start.10 = (f32[64,512]{1,0:T(8,128)S(1)}, f32[64,512]{1,0:T(8,128)S(1)}, u32[]{:S(2)}, u32[]{:S(2)}) collective-permute-start(f32[64,512]{1,0:T(8,128)S(1)} %get-tuple-element.37), channel_id=1, source_target_pairs={{0,64},{1,65},{2,66},{3,67},{4,68},{5,69},{6,70},{7,71},{8,72},{9,... | collective-permute-start | bytes 393224 | tf_op jit(solution)/shard_map/ppermute | solution.py:59
  47.2 2.2 %collective-permute-start.12 = (f32[64,512]{1,0:T(8,128)S(1)}, f32[64,512]{1,0:T(8,128)S(1)}, u32[]{:S(2)}, u32[]{:S(2)}) collective-permute-start(f32[64,512]{1,0:T(8,128)S(1)} %get-tuple-element.39), channel_id=1, source_target_pairs={{0,96},{1,97},{2,98},{3,99},{4,100},{5,101},{6,102},{7,103},{8,104... | collective-permute-start | bytes 393224 | tf_op jit(solution)/shard_map/ppermute | solution.py:59
  50.4 3.7 %collective-permute-start.16 = (f32[48,512]{1,0:T(8,128)S(1)}, f32[48,512]{1,0:T(8,128)S(1)}, u32[]{:S(2)}, u32[]{:S(2)}) collective-permute-start(f32[48,512]{1,0:T(8,128)S(1)} %get-tuple-element.40.own), channel_id=1, source_target_pairs={{0,96},{1,97},{2,98},{3,99},{4,100},{5,101},{6,102},{7,103},{8,104... | collective-permute-start | bytes 294920 | tf_op jit(solution)/shard_map/ppermute | solution.py:59
  54.4 2.6 %collective-permute-start.15 = (f32[64,512]{1,0:T(8,128)S(1)}, f32[64,512]{1,0:T(8,128)S(1)}, u32[]{:S(2)}, u32[]{:S(2)}) collective-permute-start(f32[64,512]{1,0:T(8,128)S(1)} %add_add_fusion.2.after.own), channel_id=1, source_target_pairs={{0,64},{1,65},{2,66},{3,67},{4,68},{5,69},{6,70},{7,71},{8,72},{9,... | collective-permute-start | bytes 393224 | tf_op jit(solution)/shard_map/ppermute | solution.py:59
  57.0 2.2 %collective-permute-start.14 = (f32[64,512]{1,0:T(8,128)S(1)}, f32[64,512]{1,0:T(8,128)S(1)}, u32[]{:S(2)}, u32[]{:S(2)}) collective-permute-start(f32[64,512]{1,0:T(8,128)S(1)} %add_add_fusion.2.after.own), channel_id=1, source_target_pairs={{0,32},{1,33},{2,34},{3,35},{4,36},{5,37},{6,38},{7,39},{8,40},{9,... | collective-permute-start | bytes 393224 | tf_op jit(solution)/shard_map/ppermute | solution.py:59
  61.8 5.7 %inverse.1.after = f32[256,256]{1,0:T(8,128)S(1)} custom-call(f32[48,512]{1,0:T(8,128)S(1)} %settle.1.gram, f32[48,512]{1,0:T(8,128)S(1)} %collective-permute-done.19.other), custom_call_target="tpu_custom_call" | custom-call | bytes 65536 | tf_op jit(solution)/shard_map/inverse/pallas_call | solution.py:145
  70.8 7.9 %all-to-all-start = ((f32[16,1,256]{2,1,0:T(1,128)}), f32[16,1,256]{2,1,0:T(1,128)S(1)}, u32[]{:S(2)}, u32[]{:S(2)}) async-start(f32[16,1,256]{2,1,0:T(1,128)} %get-tuple-element.44), calls=%async_computation | async-start | bytes 32768 | tf_op jit(solution)/shard_map/all_to_all | solution.py:593
  78.6 4.4 %momentum.8 = f32[1024,1024]{1,0:T(8,128)} custom-call(f32[1024,1024]{1,0:T(8,128)} %momentum.9, bf16[1024,1024]{1,0:T(8,128)(2,1)} %gradient.7, f32[1024,256]{1,0:T(8,128)S(1)} %basis.3, bf16[256,1024]{1,0:T(8,128)(2,1)S(1)} %get-tuple-element.45.high), custom_call_target="tpu_custom_call" | custom-call | flops 3221225472 | bytes 12582912 | tf_op jit(solution)/shard_map/momentum/pallas_call | solution.py:514
  83.4 2.8 %update.1 = (bf16[1024,1024]{1,0:T(8,128)(2,1)}, f32[1024,256]{1,0:T(8,128)}) custom-call(f32[16,256]{1,0:T(8,128)S(1)} %bitcast.3, f32[1024,256]{1,0:T(8,128)S(1)} %basis.3, bf16[256,1024]{1,0:T(8,128)(2,1)S(1)} %get-tuple-element.45.high, bf16[256,1024]{1,0:T(8,128)(2,1)S(1)} %get-tuple-element.46.low), custom_call_target="tpu_custom_call" | custom-call | flops 3221225472 | bytes 6291456 | tf_op jit(solution)/shard_map/update/pallas_call | solution.py:550
  (43 shorter events, 14.4 us)
Async XLA Ops:
  0.6 32.4 %copy-start.1 = (bf16[1024,1024]{1,0:T(8,128)(2,1)S(1)}, bf16[1024,1024]{1,0:T(8,128)(2,1)}, u32[]{:S(2)}) copy-start(bf16[1024,1024]{1,0:T(8,128)(2,1)} %gradient.7) | copy-start | bytes 6291460
  0.6 32.4 %copy-start = (f32[1024,1024]{1,0:T(8,128)S(1)}, f32[1024,1024]{1,0:T(8,128)}, u32[]{:S(2)}) copy-start(f32[1024,1024]{1,0:T(8,128)} %momentum.9) | copy-start | bytes 12582916
  5.5 8.0 %collective-permute-start = (f32[256,256]{1,0:T(8,128)S(1)}, f32[256,256]{1,0:T(8,128)S(1)}, u32[]{:S(2)}, u32[]{:S(2)}) collective-permute-start(f32[256,256]{1,0:T(8,128)S(1)} %get-tuple-element.27), channel_id=1, source_target_pairs={{0,2},{1,3},{2,0},{3,1},{4,6},{5,7},{6,4},{7,5},{8,10},{9,11},{10,... | collective-permute-start | bytes 786440 | tf_op jit(solution)/shard_map/ppermute | solution.py:59
  8.7 7.6 %collective-permute-start.1 = (f32[256,256]{1,0:T(8,128)S(1)}, f32[256,256]{1,0:T(8,128)S(1)}, u32[]{:S(2)}, u32[]{:S(2)}) collective-permute-start(f32[256,256]{1,0:T(8,128)S(1)} %get-tuple-element.28), channel_id=1, source_target_pairs={{0,1},{1,2},{2,3},{3,0},{4,5},{5,6},{6,7},{7,4},{8,9},{9,10},{10,1... | collective-permute-start | bytes 786440 | tf_op jit(solution)/shard_map/ppermute | solution.py:59
  9.3 7.2 %collective-permute-start.2 = (f32[256,256]{1,0:T(8,128)S(1)}, f32[256,256]{1,0:T(8,128)S(1)}, u32[]{:S(2)}, u32[]{:S(2)}) collective-permute-start(f32[256,256]{1,0:T(8,128)S(1)} %get-tuple-element.29), channel_id=1, source_target_pairs={{0,3},{1,0},{2,1},{3,2},{4,7},{5,4},{6,5},{7,6},{8,11},{9,8},{10,9... | collective-permute-start | bytes 786440 | tf_op jit(solution)/shard_map/ppermute | solution.py:59
  16.5 8.0 %collective-permute-start.5 = (f32[256,256]{1,0:T(8,128)S(1)}, f32[256,256]{1,0:T(8,128)S(1)}, u32[]{:S(2)}, u32[]{:S(2)}) collective-permute-start(f32[256,256]{1,0:T(8,128)S(1)} %add_add_fusion.1), channel_id=1, source_target_pairs={{0,8},{1,9},{2,10},{3,11},{4,12},{5,13},{6,14},{7,15},{8,0},{9,1},... | collective-permute-start | bytes 786440 | tf_op jit(solution)/shard_map/ppermute | solution.py:59
  19.8 7.6 %collective-permute-start.4 = (f32[256,256]{1,0:T(8,128)S(1)}, f32[256,256]{1,0:T(8,128)S(1)}, u32[]{:S(2)}, u32[]{:S(2)}) collective-permute-start(f32[256,256]{1,0:T(8,128)S(1)} %add_add_fusion.1), channel_id=1, source_target_pairs={{0,4},{1,5},{2,6},{3,7},{4,8},{5,9},{6,10},{7,11},{8,12},{9,13},{1... | collective-permute-start | bytes 786440 | tf_op jit(solution)/shard_map/ppermute | solution.py:59
  20.4 7.2 %collective-permute-start.3 = (f32[256,256]{1,0:T(8,128)S(1)}, f32[256,256]{1,0:T(8,128)S(1)}, u32[]{:S(2)}, u32[]{:S(2)}) collective-permute-start(f32[256,256]{1,0:T(8,128)S(1)} %add_add_fusion.1), channel_id=1, source_target_pairs={{0,12},{1,13},{2,14},{3,15},{4,0},{5,1},{6,2},{7,3},{8,4},{9,5},{1... | collective-permute-start | bytes 786440 | tf_op jit(solution)/shard_map/ppermute | solution.py:59
  27.7 8.1 %collective-permute-start.8 = (f32[256,256]{1,0:T(8,128)S(1)}, f32[256,256]{1,0:T(8,128)S(1)}, u32[]{:S(2)}, u32[]{:S(2)}) collective-permute-start(f32[256,256]{1,0:T(8,128)S(1)} %add_add_fusion.refs_2_.own), channel_id=1, source_target_pairs={{0,2},{1,3},{2,0},{3,1},{4,6},{5,7},{6,4},{7,5},{8,10},{9,11},{10,... | collective-permute-start | bytes 786440 | tf_op jit(solution)/shard_map/ppermute | solution.py:59
  29.8 8.6 %collective-permute-start.7 = (f32[256,256]{1,0:T(8,128)S(1)}, f32[256,256]{1,0:T(8,128)S(1)}, u32[]{:S(2)}, u32[]{:S(2)}) collective-permute-start(f32[256,256]{1,0:T(8,128)S(1)} %add_add_fusion.refs_2_.own), channel_id=1, source_target_pairs={{0,1},{1,2},{2,3},{3,0},{4,5},{5,6},{6,7},{7,4},{8,9},{9,10},{10,1... | collective-permute-start | bytes 786440 | tf_op jit(solution)/shard_map/ppermute | solution.py:59
  31.7 7.2 %collective-permute-start.6 = (f32[256,256]{1,0:T(8,128)S(1)}, f32[256,256]{1,0:T(8,128)S(1)}, u32[]{:S(2)}, u32[]{:S(2)}) collective-permute-start(f32[256,256]{1,0:T(8,128)S(1)} %add_add_fusion.refs_2_.own), channel_id=1, source_target_pairs={{0,3},{1,0},{2,1},{3,2},{4,7},{5,4},{6,5},{7,6},{8,11},{9,8},{10,9... | collective-permute-start | bytes 786440 | tf_op jit(solution)/shard_map/ppermute | solution.py:59
  39.9 2.1 %collective-permute-start.9 = (f32[304,512]{1,0:T(8,128)S(1)}, f32[304,512]{1,0:T(8,128)S(1)}, u32[]{:S(2)}, u32[]{:S(2)}) collective-permute-start(f32[304,512]{1,0:T(8,128)S(1)} %get-tuple-element.35), channel_id=1, source_target_pairs={{0,16},{1,17},{2,18},{3,19},{4,20},{5,21},{6,22},{7,23},{8,24},{9,... | collective-permute-start | bytes 1867784 | tf_op jit(solution)/shard_map/ppermute | solution.py:59
  42.2 8.2 %collective-permute-start.10 = (f32[64,512]{1,0:T(8,128)S(1)}, f32[64,512]{1,0:T(8,128)S(1)}, u32[]{:S(2)}, u32[]{:S(2)}) collective-permute-start(f32[64,512]{1,0:T(8,128)S(1)} %get-tuple-element.37), channel_id=1, source_target_pairs={{0,64},{1,65},{2,66},{3,67},{4,68},{5,69},{6,70},{7,71},{8,72},{9,... | collective-permute-start | bytes 393224 | tf_op jit(solution)/shard_map/ppermute | solution.py:59
  46.1 8.2 %collective-permute-start.11 = (f32[64,512]{1,0:T(8,128)S(1)}, f32[64,512]{1,0:T(8,128)S(1)}, u32[]{:S(2)}, u32[]{:S(2)}) collective-permute-start(f32[64,512]{1,0:T(8,128)S(1)} %get-tuple-element.38), channel_id=1, source_target_pairs={{0,32},{1,33},{2,34},{3,35},{4,36},{5,37},{6,38},{7,39},{8,40},{9,... | collective-permute-start | bytes 393224 | tf_op jit(solution)/shard_map/ppermute | solution.py:59
  47.2 7.2 %collective-permute-start.12 = (f32[64,512]{1,0:T(8,128)S(1)}, f32[64,512]{1,0:T(8,128)S(1)}, u32[]{:S(2)}, u32[]{:S(2)}) collective-permute-start(f32[64,512]{1,0:T(8,128)S(1)} %get-tuple-element.39), channel_id=1, source_target_pairs={{0,96},{1,97},{2,98},{3,99},{4,100},{5,101},{6,102},{7,103},{8,104... | collective-permute-start | bytes 393224 | tf_op jit(solution)/shard_map/ppermute | solution.py:59
  49.4 9.9 %collective-permute-start.18 = (f32[48,512]{1,0:T(8,128)S(1)}, f32[48,512]{1,0:T(8,128)S(1)}, u32[]{:S(2)}, u32[]{:S(2)}) collective-permute-start(f32[48,512]{1,0:T(8,128)S(1)} %get-tuple-element.40.own), channel_id=1, source_target_pairs={{0,64},{1,65},{2,66},{3,67},{4,68},{5,69},{6,70},{7,71},{8,72},{9,... | collective-permute-start | bytes 294920 | tf_op jit(solution)/shard_map/ppermute | solution.py:59
  49.4 10.9 %collective-permute-start.17 = (f32[48,512]{1,0:T(8,128)S(1)}, f32[48,512]{1,0:T(8,128)S(1)}, u32[]{:S(2)}, u32[]{:S(2)}) collective-permute-start(f32[48,512]{1,0:T(8,128)S(1)} %get-tuple-element.40.own), channel_id=1, source_target_pairs={{0,32},{1,33},{2,34},{3,35},{4,36},{5,37},{6,38},{7,39},{8,40},{9,... | collective-permute-start | bytes 294920 | tf_op jit(solution)/shard_map/ppermute | solution.py:59
  50.4 9.8 %collective-permute-start.16 = (f32[48,512]{1,0:T(8,128)S(1)}, f32[48,512]{1,0:T(8,128)S(1)}, u32[]{:S(2)}, u32[]{:S(2)}) collective-permute-start(f32[48,512]{1,0:T(8,128)S(1)} %get-tuple-element.40.own), channel_id=1, source_target_pairs={{0,96},{1,97},{2,98},{3,99},{4,100},{5,101},{6,102},{7,103},{8,104... | collective-permute-start | bytes 294920 | tf_op jit(solution)/shard_map/ppermute | solution.py:59
  54.4 13.1 %collective-permute-start.15 = (f32[64,512]{1,0:T(8,128)S(1)}, f32[64,512]{1,0:T(8,128)S(1)}, u32[]{:S(2)}, u32[]{:S(2)}) collective-permute-start(f32[64,512]{1,0:T(8,128)S(1)} %add_add_fusion.2.after.own), channel_id=1, source_target_pairs={{0,64},{1,65},{2,66},{3,67},{4,68},{5,69},{6,70},{7,71},{8,72},{9,... | collective-permute-start | bytes 393224 | tf_op jit(solution)/shard_map/ppermute | solution.py:59
  57.0 10.6 %collective-permute-start.14 = (f32[64,512]{1,0:T(8,128)S(1)}, f32[64,512]{1,0:T(8,128)S(1)}, u32[]{:S(2)}, u32[]{:S(2)}) collective-permute-start(f32[64,512]{1,0:T(8,128)S(1)} %add_add_fusion.2.after.own), channel_id=1, source_target_pairs={{0,32},{1,33},{2,34},{3,35},{4,36},{5,37},{6,38},{7,39},{8,40},{9,... | collective-permute-start | bytes 393224 | tf_op jit(solution)/shard_map/ppermute | solution.py:59
  59.2 8.3 %collective-permute-start.13 = (f32[64,512]{1,0:T(8,128)S(1)}, f32[64,512]{1,0:T(8,128)S(1)}, u32[]{:S(2)}, u32[]{:S(2)}) collective-permute-start(f32[64,512]{1,0:T(8,128)S(1)} %add_add_fusion.2.after.own), channel_id=1, source_target_pairs={{0,96},{1,97},{2,98},{3,99},{4,100},{5,101},{6,102},{7,103},{8,104... | collective-permute-start | bytes 393224 | tf_op jit(solution)/shard_map/ppermute | solution.py:59
  60.3 1.6 %collective-permute-start.19 = (f32[48,512]{1,0:T(8,128)S(1)}, f32[48,512]{1,0:T(8,128)S(1)}, u32[]{:S(2)}, u32[]{:S(2)}) collective-permute-start(f32[48,512]{1,0:T(8,128)S(1)} %settle.1.gram), channel_id=1, source_target_pairs={{0,16},{1,17},{2,18},{3,19},{4,20},{5,21},{6,22},{7,23},{8,24},{9,... | collective-permute-start | bytes 294920 | tf_op jit(solution)/shard_map/ppermute | solution.py:59
  67.6 2.0 %collective-permute-start.20 = (f32[256,512]{1,0:T(8,128)S(1)}, f32[256,512]{1,0:T(8,128)S(1)}, u32[]{:S(2)}, u32[]{:S(2)}) collective-permute-start(f32[256,512]{1,0:T(8,128)S(1)} %ordered.1.crossed), channel_id=1, source_target_pairs={{0,16},{1,17},{2,18},{3,19},{4,20},{5,21},{6,22},{7,23},{8,24},{9,... | collective-permute-start | bytes 1572872 | tf_op jit(solution)/shard_map/ppermute | solution.py:59
  70.8 12.6 %all-to-all-start = ((f32[16,1,256]{2,1,0:T(1,128)}), f32[16,1,256]{2,1,0:T(1,128)S(1)}, u32[]{:S(2)}, u32[]{:S(2)}) async-start(f32[16,1,256]{2,1,0:T(1,128)} %get-tuple-element.44), calls=%async_computation | async-start | bytes 32768 | tf_op jit(solution)/shard_map/all_to_all | solution.py:593

commit v8 on v7

--- a/solution.py
+++ b/solution.py
@@ -36,14 +36,14 @@
 
 def first_axis(k):
     def target(z, core, y, x):
-        return (z, core, y, (x + k) % 4) if core == 0 else (z, core, (y + k) % 4, x)
+        return (z, core, y, (x + k) % 4) if core == 1 else (z, core, (y + k) % 4, x)
 
     return pairs(target)
 
 
 def second_axis(k):
     def target(z, core, y, x):
-        return (z, core, (y + k) % 4, x) if core == 0 else (z, core, y, (x + k) % 4)
+        return (z, core, (y + k) % 4, x) if core == 1 else (z, core, y, (x + k) % 4)
 
     return pairs(target)
 
@@ -75,7 +75,7 @@
 def place():
     fsdp, tp = lax.axis_index("fsdp"), lax.axis_index("tp")
     core = lax.rem(fsdp, 2)
-    return lax.div(fsdp, 2), core, jnp.where(core == 0, lax.rem(tp, 4), lax.div(tp, 4))
+    return lax.div(fsdp, 2), core, jnp.where(core == 1, lax.rem(tp, 4), lax.div(tp, 4))
 
 
 def span(index, rows):

time: 86.7 us -> 86.7 us (level)
  no operation moved by 1% of the time
where the time goes in v8:
time: 86.7 us; the launch traced here: 86.4 us
  starting transfers between devices  44.5 us (51%)
  Pallas kernels  24 us (28%)
  waiting for transfers between devices  16.7 us (19%)
  between operations  0.96 us (1%)
    ppermute x21, starting transfers between devices, send(): return lax.ppermute(value, both, where)  36.5 us
    ppermute x21, waiting for transfers between devices, send(): return lax.ppermute(value, both, where)  16.4 us
    pallas_call x11, Pallas kernels, run(): pl.pallas_call(kernel, in_specs=in_specs or [vmem()] * len(operands), out...  11 us
    all_to_all x1, starting transfers between devices, local(): lax.all_to_all(squares, 'tp', 0, 0, axis_index_groups=[[8, 9, 10, 11, 12,...  7.95 us
    pallas_call x1, Pallas kernels, partial_products(): pl.pallas_call(products_kernel, grid=(2,), in_specs=[pl.BlockSpec((half,...  4.72 us
    pallas_call x1, Pallas kernels, form_momentum(): pl.pallas_call(momentum_kernel, in_specs=[hbm()] * 2 + [vmem()] * 2, out_...  4.44 us
    pallas_call x1, Pallas kernels, form_update(): pl.pallas_call(update_kernel, in_specs=[vmem()] * 4, out_specs=[hbm()] *...  2.79 us
  transfers between devices with their start and end apart: 22, of which 15 were waited for; matrix products, arithmetic and copies ran while one was open for 0% of the time, Pallas kernels for 16%

profile of v8, /device:TPU:0, one launch (start us, length us, event | category | flops | bytes accessed | tf_op | source)
XLA Modules:
  0.0 86.4 jit_solution(17503778679364424514)
XLA Ops:
  0.7 4.7 %products.1.partial = f32[1024,256]{1,0:T(8,128)S(1)} custom-call(f32[1024,1024]{1,0:T(8,128)} %momentum.9, bf16[1024,1024]{1,0:T(8,128)(2,1)} %gradient.7, f32[1024,256]{1,0:T(8,128)} %basis.2), custom_call_target="tpu_custom_call" | custom-call | flops 1610612736 | bytes 7340032 | tf_op jit(solution)/shard_map/products/pallas_call | solution.py:176
  5.5 3.4 %collective-permute-start = (f32[256,256]{1,0:T(8,128)S(1)}, f32[256,256]{1,0:T(8,128)S(1)}, u32[]{:S(2)}, u32[]{:S(2)}) collective-permute-start(f32[256,256]{1,0:T(8,128)S(1)} %get-tuple-element.27), channel_id=1, source_target_pairs={{0,8},{1,9},{2,10},{3,11},{4,12},{5,13},{6,14},{7,15},{8,0},{9,1},... | collective-permute-start | bytes 786440 | tf_op jit(solution)/shard_map/ppermute | solution.py:59
  9.5 2.6 %collective-permute-start.2 = (f32[256,256]{1,0:T(8,128)S(1)}, f32[256,256]{1,0:T(8,128)S(1)}, u32[]{:S(2)}, u32[]{:S(2)}) collective-permute-start(f32[256,256]{1,0:T(8,128)S(1)} %get-tuple-element.29), channel_id=1, source_target_pairs={{0,12},{1,13},{2,14},{3,15},{4,0},{5,1},{6,2},{7,3},{8,4},{9,5},{1... | collective-permute-start | bytes 786440 | tf_op jit(solution)/shard_map/ppermute | solution.py:59
  12.1 1.4 %collective-permute-done = f32[256,256]{1,0:T(8,128)S(1)} collective-permute-done((f32[256,256]{1,0:T(8,128)S(1)}, f32[256,256]{1,0:T(8,128)S(1)}, u32[]{:S(2)}, u32[]{:S(2)}) %collective-permute-start) | collective-permute-done | bytes 262176 | tf_op jit(solution)/shard_map/ppermute | solution.py:59
  13.4 3.0 %collective-permute-done.1 = f32[256,256]{1,0:T(8,128)S(1)} collective-permute-done((f32[256,256]{1,0:T(8,128)S(1)}, f32[256,256]{1,0:T(8,128)S(1)}, u32[]{:S(2)}, u32[]{:S(2)}) %collective-permute-start.1) | collective-permute-done | bytes 262176 | tf_op jit(solution)/shard_map/ppermute | solution.py:59
  16.7 3.1 %collective-permute-start.5 = (f32[256,256]{1,0:T(8,128)S(1)}, f32[256,256]{1,0:T(8,128)S(1)}, u32[]{:S(2)}, u32[]{:S(2)}) collective-permute-start(f32[256,256]{1,0:T(8,128)S(1)} %add_add_fusion.1), channel_id=1, source_target_pairs={{0,2},{1,3},{2,0},{3,1},{4,6},{5,7},{6,4},{7,5},{8,10},{9,11},{10,... | collective-permute-start | bytes 786440 | tf_op jit(solution)/shard_map/ppermute | solution.py:59
  20.4 2.6 %collective-permute-start.3 = (f32[256,256]{1,0:T(8,128)S(1)}, f32[256,256]{1,0:T(8,128)S(1)}, u32[]{:S(2)}, u32[]{:S(2)}) collective-permute-start(f32[256,256]{1,0:T(8,128)S(1)} %add_add_fusion.1), channel_id=1, source_target_pairs={{0,3},{1,0},{2,1},{3,2},{4,7},{5,4},{6,5},{7,6},{8,11},{9,8},{10,9... | collective-permute-start | bytes 786440 | tf_op jit(solution)/shard_map/ppermute | solution.py:59
  23.1 1.6 %collective-permute-done.5 = f32[256,256]{1,0:T(8,128)S(1)} collective-permute-done((f32[256,256]{1,0:T(8,128)S(1)}, f32[256,256]{1,0:T(8,128)S(1)}, u32[]{:S(2)}, u32[]{:S(2)}) %collective-permute-start.5) | collective-permute-done | bytes 262176 | tf_op jit(solution)/shard_map/ppermute | solution.py:59
  24.7 2.8 %collective-permute-done.4 = f32[256,256]{1,0:T(8,128)S(1)} collective-permute-done((f32[256,256]{1,0:T(8,128)S(1)}, f32[256,256]{1,0:T(8,128)S(1)}, u32[]{:S(2)}, u32[]{:S(2)}) %collective-permute-start.4) | collective-permute-done | bytes 262176 | tf_op jit(solution)/shard_map/ppermute | solution.py:59
  27.7 2.2 %collective-permute-start.8 = (f32[256,256]{1,0:T(8,128)S(1)}, f32[256,256]{1,0:T(8,128)S(1)}, u32[]{:S(2)}, u32[]{:S(2)}) collective-permute-start(f32[256,256]{1,0:T(8,128)S(1)} %add_add_fusion.refs_2_.own), channel_id=1, source_target_pairs={{0,8},{1,9},{2,10},{3,11},{4,12},{5,13},{6,14},{7,15},{8,0},{9,1},... | collective-permute-start | bytes 786440 | tf_op jit(solution)/shard_map/ppermute | solution.py:59
  29.8 1.8 %collective-permute-start.7 = (f32[256,256]{1,0:T(8,128)S(1)}, f32[256,256]{1,0:T(8,128)S(1)}, u32[]{:S(2)}, u32[]{:S(2)}) collective-permute-start(f32[256,256]{1,0:T(8,128)S(1)} %add_add_fusion.refs_2_.own), channel_id=1, source_target_pairs={{0,4},{1,5},{2,6},{3,7},{4,8},{5,9},{6,10},{7,11},{8,12},{9,13},{1... | collective-permute-start | bytes 786440 | tf_op jit(solution)/shard_map/ppermute | solution.py:59
  31.6 1.5 %collective-permute-start.6 = (f32[256,256]{1,0:T(8,128)S(1)}, f32[256,256]{1,0:T(8,128)S(1)}, u32[]{:S(2)}, u32[]{:S(2)}) collective-permute-start(f32[256,256]{1,0:T(8,128)S(1)} %add_add_fusion.refs_2_.own), channel_id=1, source_target_pairs={{0,12},{1,13},{2,14},{3,15},{4,0},{5,1},{6,2},{7,3},{8,4},{9,5},{1... | collective-permute-start | bytes 786440 | tf_op jit(solution)/shard_map/ppermute | solution.py:59
  33.9 1.8 %collective-permute-done.8.refs_2_.two = f32[256,256]{1,0:T(8,128)S(1)} collective-permute-done((f32[256,256]{1,0:T(8,128)S(1)}, f32[256,256]{1,0:T(8,128)S(1)}, u32[]{:S(2)}, u32[]{:S(2)}) %collective-permute-start.8) | collective-permute-done | bytes 262176 | tf_op jit(solution)/shard_map/ppermute | solution.py:59
  36.6 1.8 %collective-permute-done.7.one = f32[256,256]{1,0:T(8,128)S(1)} collective-permute-done((f32[256,256]{1,0:T(8,128)S(1)}, f32[256,256]{1,0:T(8,128)S(1)}, u32[]{:S(2)}, u32[]{:S(2)}) %collective-permute-start.7) | collective-permute-done | bytes 262176 | tf_op jit(solution)/shard_map/ppermute | solution.py:59
  40.6 1.4 %collective-permute-done.9.got = f32[304,512]{1,0:T(8,128)S(1)} collective-permute-done((f32[304,512]{1,0:T(8,128)S(1)}, f32[304,512]{1,0:T(8,128)S(1)}, u32[]{:S(2)}, u32[]{:S(2)}) %collective-permute-start.9) | collective-permute-done | bytes 622624 | tf_op jit(solution)/shard_map/ppermute | solution.py:59
  42.1 4.0 %collective-permute-start.10 = (f32[64,512]{1,0:T(8,128)S(1)}, f32[64,512]{1,0:T(8,128)S(1)}, u32[]{:S(2)}, u32[]{:S(2)}) collective-permute-start(f32[64,512]{1,0:T(8,128)S(1)} %get-tuple-element.37), channel_id=1, source_target_pairs={{0,64},{1,65},{2,66},{3,67},{4,68},{5,69},{6,70},{7,71},{8,72},{9,... | collective-permute-start | bytes 393224 | tf_op jit(solution)/shard_map/ppermute | solution.py:59
  47.1 2.2 %collective-permute-start.12 = (f32[64,512]{1,0:T(8,128)S(1)}, f32[64,512]{1,0:T(8,128)S(1)}, u32[]{:S(2)}, u32[]{:S(2)}) collective-permute-start(f32[64,512]{1,0:T(8,128)S(1)} %get-tuple-element.39), channel_id=1, source_target_pairs={{0,96},{1,97},{2,98},{3,99},{4,100},{5,101},{6,102},{7,103},{8,104... | collective-permute-start | bytes 393224 | tf_op jit(solution)/shard_map/ppermute | solution.py:59
  50.3 3.7 %collective-permute-start.16 = (f32[48,512]{1,0:T(8,128)S(1)}, f32[48,512]{1,0:T(8,128)S(1)}, u32[]{:S(2)}, u32[]{:S(2)}) collective-permute-start(f32[48,512]{1,0:T(8,128)S(1)} %get-tuple-element.40.own), channel_id=1, source_target_pairs={{0,96},{1,97},{2,98},{3,99},{4,100},{5,101},{6,102},{7,103},{8,104... | collective-permute-start | bytes 294920 | tf_op jit(solution)/shard_map/ppermute | solution.py:59
  54.3 2.6 %collective-permute-start.15 = (f32[64,512]{1,0:T(8,128)S(1)}, f32[64,512]{1,0:T(8,128)S(1)}, u32[]{:S(2)}, u32[]{:S(2)}) collective-permute-start(f32[64,512]{1,0:T(8,128)S(1)} %add_add_fusion.2.after.own), channel_id=1, source_target_pairs={{0,64},{1,65},{2,66},{3,67},{4,68},{5,69},{6,70},{7,71},{8,72},{9,... | collective-permute-start | bytes 393224 | tf_op jit(solution)/shard_map/ppermute | solution.py:59
  56.9 2.2 %collective-permute-start.14 = (f32[64,512]{1,0:T(8,128)S(1)}, f32[64,512]{1,0:T(8,128)S(1)}, u32[]{:S(2)}, u32[]{:S(2)}) collective-permute-start(f32[64,512]{1,0:T(8,128)S(1)} %add_add_fusion.2.after.own), channel_id=1, source_target_pairs={{0,32},{1,33},{2,34},{3,35},{4,36},{5,37},{6,38},{7,39},{8,40},{9,... | collective-permute-start | bytes 393224 | tf_op jit(solution)/shard_map/ppermute | solution.py:59
  61.7 5.7 %inverse.1.after = f32[256,256]{1,0:T(8,128)S(1)} custom-call(f32[48,512]{1,0:T(8,128)S(1)} %settle.1.gram, f32[48,512]{1,0:T(8,128)S(1)} %collective-permute-done.19.other), custom_call_target="tpu_custom_call" | custom-call | bytes 65536 | tf_op jit(solution)/shard_map/inverse/pallas_call | solution.py:145
  70.7 8.0 %all-to-all-start = ((f32[16,1,256]{2,1,0:T(1,128)}), f32[16,1,256]{2,1,0:T(1,128)S(1)}, u32[]{:S(2)}, u32[]{:S(2)}) async-start(f32[16,1,256]{2,1,0:T(1,128)} %get-tuple-element.44), calls=%async_computation | async-start | bytes 32768 | tf_op jit(solution)/shard_map/all_to_all | solution.py:593
  78.6 4.4 %momentum.8 = f32[1024,1024]{1,0:T(8,128)} custom-call(f32[1024,1024]{1,0:T(8,128)} %momentum.9, bf16[1024,1024]{1,0:T(8,128)(2,1)} %gradient.7, f32[1024,256]{1,0:T(8,128)S(1)} %basis.3, bf16[256,1024]{1,0:T(8,128)(2,1)S(1)} %get-tuple-element.45.high), custom_call_target="tpu_custom_call" | custom-call | flops 3221225472 | bytes 12582912 | tf_op jit(solution)/shard_map/momentum/pallas_call | solution.py:514
  83.4 2.8 %update.1 = (bf16[1024,1024]{1,0:T(8,128)(2,1)}, f32[1024,256]{1,0:T(8,128)}) custom-call(f32[16,256]{1,0:T(8,128)S(1)} %bitcast.3, f32[1024,256]{1,0:T(8,128)S(1)} %basis.3, bf16[256,1024]{1,0:T(8,128)(2,1)S(1)} %get-tuple-element.45.high, bf16[256,1024]{1,0:T(8,128)(2,1)S(1)} %get-tuple-element.46.low), custom_call_target="tpu_custom_call" | custom-call | flops 3221225472 | bytes 6291456 | tf_op jit(solution)/shard_map/update/pallas_call | solution.py:550
  (43 shorter events, 14.2 us)
Async XLA Ops:
  0.6 32.4 %copy-start.1 = (bf16[1024,1024]{1,0:T(8,128)(2,1)S(1)}, bf16[1024,1024]{1,0:T(8,128)(2,1)}, u32[]{:S(2)}) copy-start(bf16[1024,1024]{1,0:T(8,128)(2,1)} %gradient.7) | copy-start | bytes 6291460
  0.6 32.4 %copy-start = (f32[1024,1024]{1,0:T(8,128)S(1)}, f32[1024,1024]{1,0:T(8,128)}, u32[]{:S(2)}) copy-start(f32[1024,1024]{1,0:T(8,128)} %momentum.9) | copy-start | bytes 12582916
  5.5 8.0 %collective-permute-start = (f32[256,256]{1,0:T(8,128)S(1)}, f32[256,256]{1,0:T(8,128)S(1)}, u32[]{:S(2)}, u32[]{:S(2)}) collective-permute-start(f32[256,256]{1,0:T(8,128)S(1)} %get-tuple-element.27), channel_id=1, source_target_pairs={{0,8},{1,9},{2,10},{3,11},{4,12},{5,13},{6,14},{7,15},{8,0},{9,1},... | collective-permute-start | bytes 786440 | tf_op jit(solution)/shard_map/ppermute | solution.py:59
  8.8 7.6 %collective-permute-start.1 = (f32[256,256]{1,0:T(8,128)S(1)}, f32[256,256]{1,0:T(8,128)S(1)}, u32[]{:S(2)}, u32[]{:S(2)}) collective-permute-start(f32[256,256]{1,0:T(8,128)S(1)} %get-tuple-element.28), channel_id=1, source_target_pairs={{0,4},{1,5},{2,6},{3,7},{4,8},{5,9},{6,10},{7,11},{8,12},{9,13},{1... | collective-permute-start | bytes 786440 | tf_op jit(solution)/shard_map/ppermute | solution.py:59
  9.5 7.2 %collective-permute-start.2 = (f32[256,256]{1,0:T(8,128)S(1)}, f32[256,256]{1,0:T(8,128)S(1)}, u32[]{:S(2)}, u32[]{:S(2)}) collective-permute-start(f32[256,256]{1,0:T(8,128)S(1)} %get-tuple-element.29), channel_id=1, source_target_pairs={{0,12},{1,13},{2,14},{3,15},{4,0},{5,1},{6,2},{7,3},{8,4},{9,5},{1... | collective-permute-start | bytes 786440 | tf_op jit(solution)/shard_map/ppermute | solution.py:59
  16.7 8.0 %collective-permute-start.5 = (f32[256,256]{1,0:T(8,128)S(1)}, f32[256,256]{1,0:T(8,128)S(1)}, u32[]{:S(2)}, u32[]{:S(2)}) collective-permute-start(f32[256,256]{1,0:T(8,128)S(1)} %add_add_fusion.1), channel_id=1, source_target_pairs={{0,2},{1,3},{2,0},{3,1},{4,6},{5,7},{6,4},{7,5},{8,10},{9,11},{10,... | collective-permute-start | bytes 786440 | tf_op jit(solution)/shard_map/ppermute | solution.py:59
  19.8 7.7 %collective-permute-start.4 = (f32[256,256]{1,0:T(8,128)S(1)}, f32[256,256]{1,0:T(8,128)S(1)}, u32[]{:S(2)}, u32[]{:S(2)}) collective-permute-start(f32[256,256]{1,0:T(8,128)S(1)} %add_add_fusion.1), channel_id=1, source_target_pairs={{0,1},{1,2},{2,3},{3,0},{4,5},{5,6},{6,7},{7,4},{8,9},{9,10},{10,1... | collective-permute-start | bytes 786440 | tf_op jit(solution)/shard_map/ppermute | solution.py:59
  20.4 7.2 %collective-permute-start.3 = (f32[256,256]{1,0:T(8,128)S(1)}, f32[256,256]{1,0:T(8,128)S(1)}, u32[]{:S(2)}, u32[]{:S(2)}) collective-permute-start(f32[256,256]{1,0:T(8,128)S(1)} %add_add_fusion.1), channel_id=1, source_target_pairs={{0,3},{1,0},{2,1},{3,2},{4,7},{5,4},{6,5},{7,6},{8,11},{9,8},{10,9... | collective-permute-start | bytes 786440 | tf_op jit(solution)/shard_map/ppermute | solution.py:59
  27.7 8.1 %collective-permute-start.8 = (f32[256,256]{1,0:T(8,128)S(1)}, f32[256,256]{1,0:T(8,128)S(1)}, u32[]{:S(2)}, u32[]{:S(2)}) collective-permute-start(f32[256,256]{1,0:T(8,128)S(1)} %add_add_fusion.refs_2_.own), channel_id=1, source_target_pairs={{0,8},{1,9},{2,10},{3,11},{4,12},{5,13},{6,14},{7,15},{8,0},{9,1},... | collective-permute-start | bytes 786440 | tf_op jit(solution)/shard_map/ppermute | solution.py:59
  29.8 8.6 %collective-permute-start.7 = (f32[256,256]{1,0:T(8,128)S(1)}, f32[256,256]{1,0:T(8,128)S(1)}, u32[]{:S(2)}, u32[]{:S(2)}) collective-permute-start(f32[256,256]{1,0:T(8,128)S(1)} %add_add_fusion.refs_2_.own), channel_id=1, source_target_pairs={{0,4},{1,5},{2,6},{3,7},{4,8},{5,9},{6,10},{7,11},{8,12},{9,13},{1... | collective-permute-start | bytes 786440 | tf_op jit(solution)/shard_map/ppermute | solution.py:59
  31.6 7.2 %collective-permute-start.6 = (f32[256,256]{1,0:T(8,128)S(1)}, f32[256,256]{1,0:T(8,128)S(1)}, u32[]{:S(2)}, u32[]{:S(2)}) collective-permute-start(f32[256,256]{1,0:T(8,128)S(1)} %add_add_fusion.refs_2_.own), channel_id=1, source_target_pairs={{0,12},{1,13},{2,14},{3,15},{4,0},{5,1},{6,2},{7,3},{8,4},{9,5},{1... | collective-permute-start | bytes 786440 | tf_op jit(solution)/shard_map/ppermute | solution.py:59
  39.9 2.1 %collective-permute-start.9 = (f32[304,512]{1,0:T(8,128)S(1)}, f32[304,512]{1,0:T(8,128)S(1)}, u32[]{:S(2)}, u32[]{:S(2)}) collective-permute-start(f32[304,512]{1,0:T(8,128)S(1)} %get-tuple-element.35), channel_id=1, source_target_pairs={{0,16},{1,17},{2,18},{3,19},{4,20},{5,21},{6,22},{7,23},{8,24},{9,... | collective-permute-start | bytes 1867784 | tf_op jit(solution)/shard_map/ppermute | solution.py:59
  42.1 8.2 %collective-permute-start.10 = (f32[64,512]{1,0:T(8,128)S(1)}, f32[64,512]{1,0:T(8,128)S(1)}, u32[]{:S(2)}, u32[]{:S(2)}) collective-permute-start(f32[64,512]{1,0:T(8,128)S(1)} %get-tuple-element.37), channel_id=1, source_target_pairs={{0,64},{1,65},{2,66},{3,67},{4,68},{5,69},{6,70},{7,71},{8,72},{9,... | collective-permute-start | bytes 393224 | tf_op jit(solution)/shard_map/ppermute | solution.py:59
  46.1 8.2 %collective-permute-start.11 = (f32[64,512]{1,0:T(8,128)S(1)}, f32[64,512]{1,0:T(8,128)S(1)}, u32[]{:S(2)}, u32[]{:S(2)}) collective-permute-start(f32[64,512]{1,0:T(8,128)S(1)} %get-tuple-element.38), channel_id=1, source_target_pairs={{0,32},{1,33},{2,34},{3,35},{4,36},{5,37},{6,38},{7,39},{8,40},{9,... | collective-permute-start | bytes 393224 | tf_op jit(solution)/shard_map/ppermute | solution.py:59
  47.1 7.2 %collective-permute-start.12 = (f32[64,512]{1,0:T(8,128)S(1)}, f32[64,512]{1,0:T(8,128)S(1)}, u32[]{:S(2)}, u32[]{:S(2)}) collective-permute-start(f32[64,512]{1,0:T(8,128)S(1)} %get-tuple-element.39), channel_id=1, source_target_pairs={{0,96},{1,97},{2,98},{3,99},{4,100},{5,101},{6,102},{7,103},{8,104... | collective-permute-start | bytes 393224 | tf_op jit(solution)/shard_map/ppermute | solution.py:59
  49.3 9.9 %collective-permute-start.18 = (f32[48,512]{1,0:T(8,128)S(1)}, f32[48,512]{1,0:T(8,128)S(1)}, u32[]{:S(2)}, u32[]{:S(2)}) collective-permute-start(f32[48,512]{1,0:T(8,128)S(1)} %get-tuple-element.40.own), channel_id=1, source_target_pairs={{0,64},{1,65},{2,66},{3,67},{4,68},{5,69},{6,70},{7,71},{8,72},{9,... | collective-permute-start | bytes 294920 | tf_op jit(solution)/shard_map/ppermute | solution.py:59
  49.3 10.9 %collective-permute-start.17 = (f32[48,512]{1,0:T(8,128)S(1)}, f32[48,512]{1,0:T(8,128)S(1)}, u32[]{:S(2)}, u32[]{:S(2)}) collective-permute-start(f32[48,512]{1,0:T(8,128)S(1)} %get-tuple-element.40.own), channel_id=1, source_target_pairs={{0,32},{1,33},{2,34},{3,35},{4,36},{5,37},{6,38},{7,39},{8,40},{9,... | collective-permute-start | bytes 294920 | tf_op jit(solution)/shard_map/ppermute | solution.py:59
  50.3 9.8 %collective-permute-start.16 = (f32[48,512]{1,0:T(8,128)S(1)}, f32[48,512]{1,0:T(8,128)S(1)}, u32[]{:S(2)}, u32[]{:S(2)}) collective-permute-start(f32[48,512]{1,0:T(8,128)S(1)} %get-tuple-element.40.own), channel_id=1, source_target_pairs={{0,96},{1,97},{2,98},{3,99},{4,100},{5,101},{6,102},{7,103},{8,104... | collective-permute-start | bytes 294920 | tf_op jit(solution)/shard_map/ppermute | solution.py:59
  54.3 13.1 %collective-permute-start.15 = (f32[64,512]{1,0:T(8,128)S(1)}, f32[64,512]{1,0:T(8,128)S(1)}, u32[]{:S(2)}, u32[]{:S(2)}) collective-permute-start(f32[64,512]{1,0:T(8,128)S(1)} %add_add_fusion.2.after.own), channel_id=1, source_target_pairs={{0,64},{1,65},{2,66},{3,67},{4,68},{5,69},{6,70},{7,71},{8,72},{9,... | collective-permute-start | bytes 393224 | tf_op jit(solution)/shard_map/ppermute | solution.py:59
  56.9 10.6 %collective-permute-start.14 = (f32[64,512]{1,0:T(8,128)S(1)}, f32[64,512]{1,0:T(8,128)S(1)}, u32[]{:S(2)}, u32[]{:S(2)}) collective-permute-start(f32[64,512]{1,0:T(8,128)S(1)} %add_add_fusion.2.after.own), channel_id=1, source_target_pairs={{0,32},{1,33},{2,34},{3,35},{4,36},{5,37},{6,38},{7,39},{8,40},{9,... | collective-permute-start | bytes 393224 | tf_op jit(solution)/shard_map/ppermute | solution.py:59
  59.1 8.3 %collective-permute-start.13 = (f32[64,512]{1,0:T(8,128)S(1)}, f32[64,512]{1,0:T(8,128)S(1)}, u32[]{:S(2)}, u32[]{:S(2)}) collective-permute-start(f32[64,512]{1,0:T(8,128)S(1)} %add_add_fusion.2.after.own), channel_id=1, source_target_pairs={{0,96},{1,97},{2,98},{3,99},{4,100},{5,101},{6,102},{7,103},{8,104... | collective-permute-start | bytes 393224 | tf_op jit(solution)/shard_map/ppermute | solution.py:59
  60.2 1.6 %collective-permute-start.19 = (f32[48,512]{1,0:T(8,128)S(1)}, f32[48,512]{1,0:T(8,128)S(1)}, u32[]{:S(2)}, u32[]{:S(2)}) collective-permute-start(f32[48,512]{1,0:T(8,128)S(1)} %settle.1.gram), channel_id=1, source_target_pairs={{0,16},{1,17},{2,18},{3,19},{4,20},{5,21},{6,22},{7,23},{8,24},{9,... | collective-permute-start | bytes 294920 | tf_op jit(solution)/shard_map/ppermute | solution.py:59
  67.5 2.0 %collective-permute-start.20 = (f32[256,512]{1,0:T(8,128)S(1)}, f32[256,512]{1,0:T(8,128)S(1)}, u32[]{:S(2)}, u32[]{:S(2)}) collective-permute-start(f32[256,512]{1,0:T(8,128)S(1)} %ordered.1.crossed), channel_id=1, source_target_pairs={{0,16},{1,17},{2,18},{3,19},{4,20},{5,21},{6,22},{7,23},{8,24},{9,... | collective-permute-start | bytes 1572872 | tf_op jit(solution)/shard_map/ppermute | solution.py:59
  70.7 12.7 %all-to-all-start = ((f32[16,1,256]{2,1,0:T(1,128)}), f32[16,1,256]{2,1,0:T(1,128)S(1)}, u32[]{:S(2)}, u32[]{:S(2)}) async-start(f32[16,1,256]{2,1,0:T(1,128)} %get-tuple-element.44), calls=%async_computation | async-start | bytes 32768 | tf_op jit(solution)/shard_map/all_to_all | solution.py:593
